TPU v7x, 512 devices: a whole 4x8x8 slice. The times are simulated.
512 devices in a mesh: occ: 128 (over y_lo, x, z, core), frag: 4 (over y_hi).
Axes of the slice: x: 4, y: 8 (y_hi: 4, y_lo: 2; y = y_hi * 2 + y_lo), z: 8, core: 2. Of those that a mesh axis runs over, the one named last changes fastest.
Arguments:
- factors: bfloat16 [512, 512, 1280], P(('frag', 'occ')), parts along dimension 0, may hold values from -1 to 1
- occ_energy: float32 [512], P('frag'), parts along dimension 0, may hold values from -2 to -0.3
- vir_energy: float32 [2048], P('frag'), parts along dimension 0, may hold values from 0.2 to 4
- coeffs: bfloat16 [4096, 512], P('frag'), parts along dimension 0, may hold values from -0.25 to 0.25
Outputs:
- back: bfloat16 [1280, 512, 1024], P('occ', 'frag'), parts along dimension 1
There are 4 independent parts, one for each index of `frag`. A program takes and returns all parts, laid end to end along the dimension named above; each array names one. Nothing has to cross between parts.
All inputs are finite; a program needn't handle non-finite values.
Results may differ from a plain program's by a relative error of at most 0.008.
Values may be sent and summed in bfloat16 or wider, within the bound.
No kernel may reach another device: no remote copies, remote signals or barrier semaphores. Data moves between devices by JAX's collectives and lax.ppermute only.
A program may use at most 64 MiB of HBM per device.

v0:
```python
import jax
import jax.numpy as jnp
from jax import lax
from jax.sharding import Mesh
from jax.sharding import PartitionSpec as P

OFFSETS = 3
OCC = ("occ_0", "occ_1", "occ_2", "occ_3")
FRAG_OCC = ("frag", "occ_0", "occ_1", "occ_2", "occ_3")


def passed_along(block, axis, distance):
    devices = range(lax.axis_size(axis))
    route = [((i - distance) % len(devices), i) for i in devices]
    return lax.ppermute(block, axis, route)


def split_up(shard, dim, peers):
    before, after = (shard.shape[:dim], shard.shape[dim + 1 :])
    return jnp.moveaxis(shard.reshape(*before, peers, -1, *after), dim, 0)


def joined_along(parts, dim):
    parts = jnp.moveaxis(parts, 0, dim)
    dims = parts.shape
    return parts.reshape(*dims[:dim], dims[dim] * dims[dim + 1], *dims[dim + 2 :])


def moved_by_axis(parts, axes, turns):
    inside = parts.shape[1:]
    out = parts.reshape(*(lax.axis_size(a) for a in axes), *inside)
    for k in turns:
        out = lax.all_to_all(out, axes[k], k, k, tiled=True)
    return out.reshape(-1, *inside)


def core_and_chips(shard, groups, turns, split_dim, concat_dim):
    peers = lax.axis_size(groups[0]) * lax.axis_size(groups[1])
    parts = split_up(shard, split_dim, peers)
    return joined_along(moved_by_axis(parts, groups, turns), concat_dim)


def on_device(factors, occ_energy, vir_energy, coeffs):
    mine = factors[0]
    count = lax.axis_size(OCC)
    index = lax.axis_index(OCC)
    partners = [passed_along(mine, OCC, -offset) for offset in range(1, OFFSETS + 1)]
    own_energy = lax.dynamic_index_in_dim(occ_energy, index, 0, False)
    own = jnp.zeros((mine.shape[1], mine.shape[0]), jnp.float32)
    outgoing = []
    for offset in range(1, OFFSETS + 1):
        partner = partners[offset - 1]
        other_energy = lax.dynamic_index_in_dim(occ_energy, (index + offset) % count, 0, False)
        kmat = lax.dot_general(
            mine, partner, (((1,), (1,)), ((), ())), preferred_element_type=jnp.float32
        )
        denom = own_energy + other_energy - vir_energy[:, None] - vir_energy[None, :]
        amps = (kmat / denom).astype(jnp.bfloat16)
        own = own + lax.dot_general(
            partner, amps, (((0,), (1,)), ((), ())), preferred_element_type=jnp.float32
        )
        sent = lax.dot_general(
            mine, amps, (((0,), (0,)), ((), ())), preferred_element_type=jnp.float32
        )
        outgoing.append(sent.astype(jnp.bfloat16))
    incoming = jnp.zeros_like(own)
    for offset in range(1, OFFSETS + 1):
        arrived = passed_along(outgoing[offset - 1], OCC, offset)
        incoming = incoming + arrived.astype(jnp.float32)
    gamma = (own + incoming).astype(jnp.bfloat16)[None]
    slabs = core_and_chips(gamma, (("occ_0", "occ_1", "occ_2"), "occ_3"), (1, 0), 1, 0)
    return jnp.einsum("ipa,ma->pim", slabs, coeffs, preferred_element_type=jnp.float32).astype(
        jnp.bfloat16
    )


def solution(mesh):
    finer = Mesh(
        mesh.devices.reshape(2, 4, 8, 2, mesh.shape["frag"]),
        ("occ_0", "occ_1", "occ_2", "occ_3", "frag"),
    )
    in_specs = (P(FRAG_OCC, None, None), P("frag"), P("frag"), P("frag", None))
    out_specs = P(OCC, "frag", None)
    return jax.shard_map(
        on_device, mesh=finer, in_specs=in_specs, out_specs=out_specs, check_vma=False
    )
```

profile of v0, /device:TPU:1, one launch (start us, length us, event | category | flops | bytes accessed | tf_op | source)
XLA Modules:
  0.0 211.0 jit_solution(11770499598858110364)
XLA Ops:
  0.0 0.0 copy-start
  0.0 14.8 %collective-permute-start.1 = (bf16[512,1280]{1,0:T(8,128)(2,1)}, bf16[512,1280]{1,0:T(8,128)(2,1)}, u32[]{:S(2)}, u32[]{:S(2)}) collective-permute-start(bf16[512,1280]{1,0:T(8,128)(2,1)} %bitcast.48), channel_id=1, source_target_pairs={{8,0},{12,4},{16,8},{20,12},{24,16},{28,20},{32,24},{36,28},{40,32... | collective-permute-start | bytes 3932168 | tf_op jit(solution)/shard_map/ppermute | solution.py:15
  14.8 3.0 %collective-permute-start.2 = (bf16[512,1280]{1,0:T(8,128)(2,1)}, bf16[512,1280]{1,0:T(8,128)(2,1)}, u32[]{:S(2)}, u32[]{:S(2)}) collective-permute-start(bf16[512,1280]{1,0:T(8,128)(2,1)} %bitcast.49), channel_id=1, source_target_pairs={{12,0},{16,4},{20,8},{24,12},{28,16},{32,20},{36,24},{40,28},{44,3... | collective-permute-start | bytes 3932168 | tf_op jit(solution)/shard_map/ppermute | solution.py:15
  17.9 1.9 collective-permute-start
  19.9 1.5 fusion.17
  24.9 0.7 broadcast_subtract_fusion.2
  25.6 31.0 %collective-permute-done.1 = bf16[512,1280]{1,0:T(8,128)(2,1)} collective-permute-done((bf16[512,1280]{1,0:T(8,128)(2,1)}, bf16[512,1280]{1,0:T(8,128)(2,1)}, u32[]{:S(2)}, u32[]{:S(2)}) %collective-permute-start.1) | collective-permute-done | bytes 1310752 | tf_op jit(solution)/shard_map/ppermute | solution.py:15
  56.6 0.0 copy-start.4
  56.6 2.7 %fusion.8 = bf16[512,512]{1,0:T(8,128)(2,1)S(1)} fusion(bf16[512,1280]{1,0:T(8,128)(2,1)} %collective-permute-done.1, f32[512]{0:T(512)S(1)} %get-tuple-element.7, f32[512]{0:T(512)} %param.6, bf16[1,512,1280]{2,1,0:T(8,128)(2,1)} %param.4), kind=kOutput, calls=%fused_computation.16 | convolution fusion | flops 671875072 | bytes 3149824 | tf_op jit(solution)/shard_map/dot_general | solution.py:54
  59.3 0.0 copy-done.4
  59.3 0.0 copy-start.3
  59.3 0.9 fusion.5
  60.2 1.9 collective-permute-start.4
  62.1 22.6 %collective-permute-done.2 = bf16[512,1280]{1,0:T(8,128)(2,1)} collective-permute-done((bf16[512,1280]{1,0:T(8,128)(2,1)}, bf16[512,1280]{1,0:T(8,128)(2,1)}, u32[]{:S(2)}, u32[]{:S(2)}) %collective-permute-start.2) | collective-permute-done | bytes 1310752 | tf_op jit(solution)/shard_map/ppermute | solution.py:15
  84.7 0.0 copy-done.3
  84.7 2.2 %fusion.9 = bf16[512,512]{1,0:T(8,128)(2,1)S(1)} fusion(bf16[512,1280]{1,0:T(8,128)(2,1)} %collective-permute-done.2, f32[512]{0:T(512)S(1)} %get-tuple-element.6, f32[512]{0:T(512)S(1)} %copy-done.3, bf16[1,512,1280]{2,1,0:T(8,128)(2,1)S(1)} %copy-done.4), kind=kOutput, calls=%fused_computation.17 | convolution fusion | flops 671875072 | bytes 3149824 | tf_op jit(solution)/shard_map/dot_general | solution.py:54
  86.9 0.9 fusion.6
  87.7 1.9 collective-permute-start.5
  89.7 1.0 collective-permute-done
  90.7 0.0 copy-start.1
  90.7 0.9 fusion.7
  91.6 0.2 copy-done.1
  91.7 0.9 fusion.4
  92.6 1.9 collective-permute-start.3
  94.5 2.2 %fusion.18 = f32[512,1280]{1,0:T(8,128)S(1)} fusion(bf16[512,512]{1,0:T(8,128)(2,1)S(1)} %fusion.8, bf16[512,1280]{1,0:T(8,128)(2,1)} %collective-permute-done.1), kind=kOutput, calls=%fused_computation.29 | convolution fusion | flops 671088640 | bytes 4456448 | tf_op jit(solution)/shard_map/dot_general | solution.py:59
  96.7 0.0 copy-start.2
  96.7 2.3 %fusion.19 = f32[512,1280]{1,0:T(8,128)S(1)} fusion(bf16[512,512]{1,0:T(8,128)(2,1)S(1)} %fusion.9, bf16[512,1280]{1,0:T(8,128)(2,1)} %collective-permute-done.2), kind=kOutput, calls=%fused_computation.30 | convolution fusion | flops 671088640 | bytes 4456448 | tf_op jit(solution)/shard_map/dot_general | solution.py:59
  99.0 0.0 collective-permute-done.4
  99.0 47.8 %collective-permute-done.5 = bf16[1280,512]{0,1:T(8,128)(2,1)S(1)} collective-permute-done((bf16[1280,512]{0,1:T(8,128)(2,1)S(1)}, bf16[1280,512]{0,1:T(8,128)(2,1)S(1)}, u32[]{:S(2)}, u32[]{:S(2)}) %collective-permute-start.5) | collective-permute-done | bytes 1310752 | tf_op jit(solution)/shard_map/ppermute | solution.py:15
  146.8 0.1 collective-permute-done.3
  146.9 0.0 copy-done.2
  146.9 1.0 fusion.3
  147.9 1.5 copy.8
  149.4 2.4 %reshape_transpose_reshape_broadcast_in_dim.3 = bf16[64,2,1,10,512]{4,3,1,0,2:T(8,128)(2,1)S(1)} reshape(bf16[1280,512]{1,0:T(8,128)(2,1)} %copy.8) | data formatting | bytes 2621440 | tf_op jit(solution)/shard_map/reshape;transpose;reshape;broadcast_in_dim | solution.py:31
  151.7 0.7 copy.9
  152.5 12.0 %all_to_all.10 = bf16[64,2,1,10,512]{4,0,3,2,1:T(8,128)(2,1)S(1)} all-to-all(bf16[64,2,1,10,512]{4,0,3,2,1:T(8,128)(2,1)S(1)} %copy.9), channel_id=1, replica_groups=mesh['occ_0'=2,'occ_1'=4,'occ_2'=8,'occ_3'=2,'frag'=4] {'occ_3'}, dimensions={1} | all-to-all | bytes 2621440 | tf_op jit(solution)/shard_map/all_to_all | solution.py:33
  164.4 1.3 copy.10
  165.8 38.4 %all_to_all.11 = bf16[64,2,1,10,512]{4,1,3,2,0:T(2,128)(2,1)S(1)} all-to-all(bf16[64,2,1,10,512]{4,1,3,2,0:T(2,128)(2,1)S(1)} %copy.10), channel_id=1, replica_groups=mesh['occ_0'=2,'occ_1'=4,'occ_2'=8,'occ_3'=2,'frag'=4] {'occ_0','occ_1',..., dimensions={0} | all-to-all | bytes 2621440 | tf_op jit(solution)/shard_map/all_to_all | solution.py:33
  204.1 1.1 copy.11
  205.2 1.4 reshape_reshape.3
  206.6 0.0 copy-done
  206.6 4.4 %convert_bitcast_fusion = bf16[10,128,1024]{2,1,0:T(8,128)(2,1)} fusion(bf16[128,10,512]{2,0,1:T(8,128)(2,1)} %reshape_reshape.3, bf16[1024,512]{1,0:T(8,128)(2,1)S(1)} %copy-done), kind=kOutput, calls=%fused_computation.11 | convolution fusion | flops 1343488000 | bytes 4980736 | tf_op jit(solution)/shard_map/ipa,ma->pim/dot_general | solution.py:72
Async XLA Ops:
  0.0 206.6 %copy-start = (bf16[1024,512]{1,0:T(8,128)(2,1)S(1)}, bf16[1024,512]{1,0:T(8,128)(2,1)}, u32[]{:S(2)}) copy-start(bf16[1024,512]{1,0:T(8,128)(2,1)} %param.7) | copy-start | bytes 3145732
  0.0 56.6 %collective-permute-start.1 = (bf16[512,1280]{1,0:T(8,128)(2,1)}, bf16[512,1280]{1,0:T(8,128)(2,1)}, u32[]{:S(2)}, u32[]{:S(2)}) collective-permute-start(bf16[512,1280]{1,0:T(8,128)(2,1)} %bitcast.48), channel_id=1, source_target_pairs={{8,0},{12,4},{16,8},{20,12},{24,16},{28,20},{32,24},{36,28},{40,32... | collective-permute-start | bytes 3932168 | tf_op jit(solution)/shard_map/ppermute | solution.py:15
  14.8 69.8 %collective-permute-start.2 = (bf16[512,1280]{1,0:T(8,128)(2,1)}, bf16[512,1280]{1,0:T(8,128)(2,1)}, u32[]{:S(2)}, u32[]{:S(2)}) collective-permute-start(bf16[512,1280]{1,0:T(8,128)(2,1)} %bitcast.49), channel_id=1, source_target_pairs={{12,0},{16,4},{20,8},{24,12},{28,16},{32,20},{36,24},{40,28},{44,3... | collective-permute-start | bytes 3932168 | tf_op jit(solution)/shard_map/ppermute | solution.py:15
  17.9 72.8 %collective-permute-start = (bf16[512,1280]{1,0:T(8,128)(2,1)}, bf16[512,1280]{1,0:T(8,128)(2,1)S(1)}, u32[]{:S(2)}, u32[]{:S(2)}) collective-permute-start(bf16[512,1280]{1,0:T(8,128)(2,1)} %bitcast.50), channel_id=1, source_target_pairs={{4,0},{8,4},{12,8},{16,12},{20,16},{24,20},{28,24},{32,28},{36,32}... | collective-permute-start | bytes 3932168 | tf_op jit(solution)/shard_map/ppermute | solution.py:15
  56.6 2.7 %copy-start.4 = (bf16[1,512,1280]{2,1,0:T(8,128)(2,1)S(1)}, bf16[1,512,1280]{2,1,0:T(8,128)(2,1)}, u32[]{:S(2)}) copy-start(bf16[1,512,1280]{2,1,0:T(8,128)(2,1)} %param.4) | copy-start | bytes 3932164
  59.3 25.4 %copy-start.3 = (f32[512]{0:T(512)S(1)}, f32[512]{0:T(512)}, u32[]{:S(2)}) copy-start(f32[512]{0:T(512)} %param.6) | copy-start | bytes 6148
  60.2 38.8 %collective-permute-start.4 = (bf16[1280,512]{0,1:T(8,128)(2,1)S(1)}, bf16[1280,512]{0,1:T(8,128)(2,1)S(1)}, u32[]{:S(2)}, u32[]{:S(2)}) collective-permute-start(bf16[1280,512]{0,1:T(8,128)(2,1)S(1)} %fusion.5), channel_id=1, source_target_pairs={{504,0},{508,4},{0,8},{4,12},{8,16},{12,20},{16,24},{20,28},{24,32... | collective-permute-start | bytes 3932168 | tf_op jit(solution)/shard_map/ppermute | solution.py:15
  87.7 59.0 %collective-permute-start.5 = (bf16[1280,512]{0,1:T(8,128)(2,1)S(1)}, bf16[1280,512]{0,1:T(8,128)(2,1)S(1)}, u32[]{:S(2)}, u32[]{:S(2)}) collective-permute-start(bf16[1280,512]{0,1:T(8,128)(2,1)S(1)} %fusion.6), channel_id=1, source_target_pairs={{500,0},{504,4},{508,8},{0,12},{4,16},{8,20},{12,24},{16,28},{20,3... | collective-permute-start | bytes 3932168 | tf_op jit(solution)/shard_map/ppermute | solution.py:15
  90.7 1.1 copy-start.1
  92.6 54.2 %collective-permute-start.3 = (bf16[1280,512]{0,1:T(8,128)(2,1)S(1)}, bf16[1280,512]{0,1:T(8,128)(2,1)S(1)}, u32[]{:S(2)}, u32[]{:S(2)}) collective-permute-start(bf16[1280,512]{0,1:T(8,128)(2,1)S(1)} %fusion.4), channel_id=1, source_target_pairs={{508,0},{0,4},{4,8},{8,12},{12,16},{16,20},{20,24},{24,28},{28,32}... | collective-permute-start | bytes 3932168 | tf_op jit(solution)/shard_map/ppermute | solution.py:15
  96.7 50.2 %copy-start.2 = (bf16[512,1280]{1,0:T(8,128)(2,1)S(1)}, bf16[512,1280]{1,0:T(8,128)(2,1)}, u32[]{:S(2)}) copy-start(bf16[512,1280]{1,0:T(8,128)(2,1)} %copy-done.1) | copy-start | bytes 3932164
where the time goes:
time: 212 us; the launch traced here: 211 us
  waiting for transfers between devices  102 us (48%)
  blocking collectives  50.3 us (24%)
  starting transfers between devices  25.5 us (12%)
  matrix products  18.2 us (9%)
  local copies, waits for them, and re-layouts  10 us (5%)
  between operations  3.78 us (2%)
    ppermute x6, waiting for transfers between devices, passed_along(): return lax.ppermute(block, axis, route)  102 us
    all_to_all x2, blocking collectives, moved_by_axis(): out = lax.all_to_all(out, axes[k], k, k, tiled=True)  50.3 us
    ppermute x6, starting transfers between devices, passed_along(): return lax.ppermute(block, axis, route)  25.5 us
    dot_general x3, matrix products, on_device(): lax.dot_general(mine, partner, (((1,), (1,)), ((), ())), preferred_elemen...  5.77 us
    dot_general x3, matrix products, on_device(): lax.dot_general(partner, amps, (((0,), (1,)), ((), ())), preferred_elemen...  5.45 us
    dot_general x1, matrix products, on_device(): jnp.einsum('ipa,ma->pim', slabs, coeffs, preferred_element_type=jnp.float32)  4.37 us
  transfers between devices with their start and end apart: 6, of which 5 were waited for; matrix products, arithmetic and copies ran while one was open for 7% of the time, Pallas kernels for 0%

commit v1 on v0

v1 whole, which is shorter than its diff:
```python
import jax
import jax.numpy as jnp
from jax import lax
from jax.sharding import Mesh
from jax.sharding import PartitionSpec as P

OCC = ("occ_0", "occ_1", "occ_2", "occ_3")
FRAG_OCC = ("frag",) + OCC


def mirrored(block, count, step):
    route = [(i, (i + step if i % 2 == 0 else i - step) % count) for i in range(count)]
    return lax.ppermute(block, OCC, route)


def on_device(factors, occ_energy, vir_energy, coeffs):
    mine = factors[0]
    virtuals, aux = mine.shape
    count = lax.axis_size(OCC)
    index = lax.axis_index(OCC)
    sign = 1 - 2 * (index % 2)
    plus2 = mirrored(mine, count, -2)
    minus2 = mirrored(mine, count, 2)
    plus1 = mirrored(mine, count, 1)
    minus3 = mirrored(plus2, count, -1)
    minus1 = mirrored(plus2, count, 1)
    plus3 = mirrored(minus2, count, 1)
    own_energy = lax.dynamic_index_in_dim(occ_energy, index, 0, False)

    def contribution(other, k):
        other_energy = lax.dynamic_index_in_dim(
            occ_energy, (index + sign * k) % count, 0, False
        )
        kmat = lax.dot_general(
            mine, other, (((1,), (1,)), ((), ())), preferred_element_type=jnp.float32
        )
        denom = own_energy + other_energy - vir_energy[:, None] - vir_energy[None, :]
        amps = (kmat / denom).astype(jnp.bfloat16)
        return lax.dot_general(
            amps, other, (((1,), (0,)), ((), ())), preferred_element_type=jnp.float32
        )

    total = contribution(plus1, 1)
    total = total + contribution(plus2, 2)
    total = total + contribution(minus2, -2)
    total = total + contribution(minus1, -1)
    total = total + contribution(plus3, 3)
    total = total + contribution(minus3, -3)
    gamma = total.T.astype(jnp.bfloat16)
    slabs = lax.all_to_all(gamma.reshape(count, -1, 128), OCC, 0, 0, tiled=True)
    slabs = slabs.reshape(count, aux // count, virtuals)
    return jnp.einsum("ipa,ma->pim", slabs, coeffs, preferred_element_type=jnp.float32).astype(
        jnp.bfloat16
    )


def solution(mesh):
    finer = Mesh(
        mesh.devices.reshape(2, 4, 8, 2, mesh.shape["frag"]),
        ("occ_0", "occ_1", "occ_2", "occ_3", "frag"),
    )
    in_specs = (P(FRAG_OCC, None, None), P("frag"), P("frag"), P("frag", None))
    out_specs = P(OCC, "frag", None)
    return jax.shard_map(
        on_device, mesh=finer, in_specs=in_specs, out_specs=out_specs, check_vma=False
    )
```

time: 212 us -> 139 us (0.66)
  waiting for transfers between devices: 102 us -> 5.97 us
  matrix products: 18.2 us -> 38.1 us
  starting transfers between devices: 25.5 us -> 34.4 us
  blocking collectives: 50.3 us -> 45.1 us
  between operations: 3.78 us -> 7.62 us
  local copies, waits for them, and re-layouts: 10 us -> 6.73 us
    ppermute x6, waiting for transfers between devices: 102 us -> 5.97 us  [mirrored(): return lax.ppermute(block, OCC, route)]
    dot_general x9 -> x6, matrix products: 13.8 us -> 33.7 us  [contribution(): lax.dot_general(amps, other, (((1,), (0,)), ((), ())), preferred_element_...]
    ppermute x6, starting transfers between devices: 25.5 us -> 34.4 us  [mirrored(): return lax.ppermute(block, OCC, route)]
    all_to_all x2 -> x1, blocking collectives: 50.3 us -> 45.1 us  [on_device(): slabs = lax.all_to_all(gamma.reshape(count, -1, 128), OCC, 0, 0, tiled=True)]
    another operation x3 -> x0, local copies, waits for them, and re-layouts: 4.47 us -> none  [the longest x2 3.08 us: moved_by_axis(): out = parts.reshape(*(lax.axis_size(a) for a in axes), *inside)]
  transfers between devices with their start and end apart: 6 -> 6, of which waited for: 5 -> 1; matrix products, arithmetic and copies ran while one was open for 7% -> 21% of each run, Pallas kernels for 0% -> 0%
where the time goes in v1:
time: 139 us
  blocking collectives  45.1 us (32%)
  matrix products  38.1 us (27%)
  starting transfers between devices  34.4 us (25%)
  between operations  7.62 us (5%)
  local copies, waits for them, and re-layouts  6.73 us (5%)
  waiting for transfers between devices  5.97 us (4%)
    all_to_all x1, blocking collectives, on_device(): slabs = lax.all_to_all(gamma.reshape(count, -1, 128), OCC, 0, 0, tiled=True)  45.1 us
    ppermute x6, starting transfers between devices, mirrored(): return lax.ppermute(block, OCC, route)  34.4 us
    dot_general x6, matrix products, contribution(): lax.dot_general(amps, other, (((1,), (0,)), ((), ())), preferred_element_...  33.7 us
    ppermute x6, waiting for transfers between devices, mirrored(): return lax.ppermute(block, OCC, route)  5.97 us
    dot_general x1, matrix products, on_device(): jnp.einsum('ipa,ma->pim', slabs, coeffs, preferred_element_type=jnp.float32)  4.39 us
  transfers between devices with their start and end apart: 6, of which 1 were waited for; matrix products, arithmetic and copies ran while one was open for 21% of the time, Pallas kernels for 0%

profile of v1, /device:TPU:1, one launch (start us, length us, event | category | flops | bytes accessed | tf_op | source)
XLA Modules:
  0.0 138.6 jit_solution(5520363103575214186)
XLA Ops:
  0.0 0.0 copy-start
  0.0 5.0 %collective-permute-start.1 = (bf16[512,1280]{1,0:T(8,128)(2,1)}, bf16[512,1280]{1,0:T(8,128)(2,1)}, u32[]{:S(2)}, u32[]{:S(2)}) collective-permute-start(bf16[512,1280]{1,0:T(8,128)(2,1)} %bitcast.47), channel_id=1, source_target_pairs={{0,504},{4,12},{8,0},{12,20},{16,8},{20,28},{24,16},{28,36},{32,24... | collective-permute-start | bytes 3932168 | tf_op jit(solution)/shard_map/ppermute | solution.py:13
  5.0 11.8 %collective-permute-start.2 = (bf16[512,1280]{1,0:T(8,128)(2,1)}, bf16[512,1280]{1,0:T(8,128)(2,1)}, u32[]{:S(2)}, u32[]{:S(2)}) collective-permute-start(bf16[512,1280]{1,0:T(8,128)(2,1)} %bitcast.48), channel_id=1, source_target_pairs={{0,8},{4,508},{8,16},{12,4},{16,24},{20,12},{24,32},{28,20},{32,40... | collective-permute-start | bytes 3932168 | tf_op jit(solution)/shard_map/ppermute | solution.py:13
  16.8 2.9 %collective-permute-start = (bf16[512,1280]{1,0:T(8,128)(2,1)}, bf16[512,1280]{1,0:T(8,128)(2,1)}, u32[]{:S(2)}, u32[]{:S(2)}) collective-permute-start(bf16[512,1280]{1,0:T(8,128)(2,1)} %bitcast.49), channel_id=1, source_target_pairs={{0,4},{4,0},{8,12},{12,8},{16,20},{20,16},{24,28},{28,24},{32,36},... | collective-permute-start | bytes 3932168 | tf_op jit(solution)/shard_map/ppermute | solution.py:13
  19.8 1.6 %fusion.44 = (f32[1]{0:T(128)}, f32[1]{0:T(128)}, f32[1]{0:T(128)}, f32[1]{0:T(128)}, f32[1]{0:T(128)}, /*index=5*/f32[1]{0:T(128)}, f32[1]{0:T(128)}) fusion(f32[128]{0:T(128)} %param.5, s32[]{:T(128)S(6)} %select_n.62, s32[]{:T(128)S(6)} %select_n.60, s32[]{:T(128)S(6)} %select_n.58, s32[]{:T(128)S(6)} %select_n.56, s32[]{:T(128)S(6)} %select_n.53, ...), kind=kLoop, calls=%fused_computation.53 | loop fusion | bytes 84 | tf_op jit(solution)/shard_map/jit(dynamic_index_in_dim)/dynamic_slice | solution.py:31
  28.8 0.7 broadcast_subtract_fusion.2
  29.4 6.0 %collective-permute-done.1 = bf16[512,1280]{1,0:T(8,128)(2,1)} collective-permute-done((bf16[512,1280]{1,0:T(8,128)(2,1)}, bf16[512,1280]{1,0:T(8,128)(2,1)}, u32[]{:S(2)}, u32[]{:S(2)}) %collective-permute-start.1) | collective-permute-done | bytes 1310752 | tf_op jit(solution)/shard_map/ppermute | solution.py:13
  35.4 4.7 %collective-permute-start.5 = (bf16[512,1280]{1,0:T(8,128)(2,1)}, bf16[512,1280]{1,0:T(8,128)(2,1)}, u32[]{:S(2)}, u32[]{:S(2)}) collective-permute-start(bf16[512,1280]{1,0:T(8,128)(2,1)} %collective-permute-done.1), channel_id=1, source_target_pairs={{0,508},{4,8},{8,4},{12,16},{16,12},{20,24},{24,20},{28,32},{32,28... | collective-permute-start | bytes 3932168 | tf_op jit(solution)/shard_map/ppermute | solution.py:13
  40.1 8.3 %collective-permute-start.3 = (bf16[512,1280]{1,0:T(8,128)(2,1)}, bf16[512,1280]{1,0:T(8,128)(2,1)}, u32[]{:S(2)}, u32[]{:S(2)}) collective-permute-start(bf16[512,1280]{1,0:T(8,128)(2,1)} %collective-permute-done.1), channel_id=1, source_target_pairs={{0,4},{4,0},{8,12},{12,8},{16,20},{20,16},{24,28},{28,24},{32,36},... | collective-permute-start | bytes 3932168 | tf_op jit(solution)/shard_map/ppermute | solution.py:13
  48.3 0.0 collective-permute-done.2
  48.3 1.9 %collective-permute-start.4 = (bf16[512,1280]{1,0:T(8,128)(2,1)}, bf16[512,1280]{1,0:T(8,128)(2,1)}, u32[]{:S(2)}, u32[]{:S(2)}) collective-permute-start(bf16[512,1280]{1,0:T(8,128)(2,1)} %collective-permute-done.2), channel_id=1, source_target_pairs={{0,4},{4,0},{8,12},{12,8},{16,20},{20,16},{24,28},{28,24},{32,36},... | collective-permute-start | bytes 3932168 | tf_op jit(solution)/shard_map/ppermute | solution.py:13
  50.3 0.0 copy-start.1
  50.3 0.0 copy-start.2
  50.3 5.4 %fusion.13 = f32[512,1280]{1,0:T(8,128)} fusion(bf16[512,1280]{1,0:T(8,128)(2,1)} %collective-permute-done.2, f32[512]{0:T(512)S(1)} %get-tuple-element.6, f32[512]{0:T(512)} %param.6, bf16[1,512,1280]{2,1,0:T(8,128)(2,1)} %param.4), kind=kOutput, calls=%fused_computation.22 | convolution fusion | flops 1342963712 | bytes 5246976 | tf_op jit(solution)/shard_map/dot_general | solution.py:39
  55.7 0.0 copy-done.1
  55.7 0.0 copy-done.2
  55.7 4.9 %fusion.14 = f32[512,1280]{1,0:T(8,128)} fusion(bf16[512,1280]{1,0:T(8,128)(2,1)} %collective-permute-done.1, f32[512]{0:T(512)S(1)} %get-tuple-element.7, f32[512]{0:T(512)S(1)} %copy-done.1, bf16[1,512,1280]{2,1,0:T(8,128)(2,1)S(1)} %copy-done.2), kind=kOutput, calls=%fused_computation.23 | convolution fusion | flops 1342963712 | bytes 5246976 | tf_op jit(solution)/shard_map/dot_general | solution.py:39
  60.6 0.0 collective-permute-done
  60.6 6.5 %fusion.1 = f32[512,1280]{1,0:T(8,128)} fusion(f32[512,1280]{1,0:T(8,128)} %fusion.13, f32[512,1280]{1,0:T(8,128)} %fusion.14, bf16[512,1280]{1,0:T(8,128)(2,1)} %collective-permute-done, f32[512]{0:T(512)S(1)} %copy-done.1, f32[512]{0:T(512)S(1)} %get-tuple-element.8, bf16[1,512,1280]{2,1,0:T(8,128)(2,1)S(1)} %copy-done.2), kind=kOutput, calls=%fused_computation.3 | convolution fusion | flops 1344274432 | bytes 10489856 | tf_op jit(solution)/shard_map/dot_general | solution.py:39
  67.2 0.0 collective-permute-done.4
  67.2 4.9 %fusion.12 = f32[512,1280]{1,0:T(8,128)} fusion(bf16[512,1280]{1,0:T(8,128)(2,1)} %collective-permute-done.4, f32[512]{0:T(512)S(1)} %get-tuple-element.10, f32[512]{0:T(512)S(1)} %copy-done.1, bf16[1,512,1280]{2,1,0:T(8,128)(2,1)S(1)} %copy-done.2), kind=kOutput, calls=%fused_computation.21 | convolution fusion | flops 1342963712 | bytes 5246976 | tf_op jit(solution)/shard_map/dot_general | solution.py:39
  72.1 0.0 collective-permute-done.5
  72.1 5.0 %fusion.11 = f32[512,1280]{1,0:T(8,128)} fusion(bf16[512,1280]{1,0:T(8,128)(2,1)} %collective-permute-done.5, f32[512]{0:T(512)S(1)} %get-tuple-element.9, f32[512]{0:T(512)S(1)} %copy-done.1, bf16[1,512,1280]{2,1,0:T(8,128)(2,1)S(1)} %copy-done.2), kind=kOutput, calls=%fused_computation.20 | convolution fusion | flops 1342963712 | bytes 5246976 | tf_op jit(solution)/shard_map/dot_general | solution.py:39
  77.1 0.0 collective-permute-done.3
  77.1 6.9 %fusion.4 = bf16[1280,512]{0,1:T(8,128)(2,1)} fusion(f32[512,1280]{1,0:T(8,128)} %fusion.11, f32[512,1280]{1,0:T(8,128)} %fusion.12, f32[512,1280]{1,0:T(8,128)} %fusion.1, bf16[512,1280]{1,0:T(8,128)(2,1)} %collective-permute-done.3, f32[512]{0:T(512)S(1)} %get-tuple-element.5, f32[512]{0:T(512)S(1)} %copy-done.1, bf16[1,512,1280]{2,1,0:T(8,128)(2,1)S(1)} %copy-done.2), kind=kOutput, calls=%fused_computation.6 | convolution fusion | flops 1345585152 | bytes 11800576 | tf_op jit(solution)/shard_map/dot_general | solution.py:39
  84.0 1.6 %copy.5 = bf16[1280,512]{1,0:T(8,128)(2,1)S(1)} copy(bf16[1280,512]{0,1:T(8,128)(2,1)} %fusion.4) | data formatting | bytes 2621440 | tf_op jit(solution)/shard_map/convert_element_type | solution.py:49
  85.6 1.6 %reshape.25 = bf16[128,40,128]{2,1,0:T(8,128)(2,1)} reshape(bf16[1280,512]{1,0:T(8,128)(2,1)S(1)} %copy.5) | data formatting | bytes 2621440 | tf_op jit(solution)/shard_map/reshape | solution.py:50
  87.2 45.1 %all_to_all.5 = bf16[128,40,128]{2,1,0:T(8,128)(2,1)S(1)} all-to-all(bf16[128,40,128]{2,1,0:T(8,128)(2,1)} %reshape.25), channel_id=1, replica_groups=mesh['occ_0'=2,'occ_1'=4,'occ_2'=8,'occ_3'=2,'frag'=4] {'occ_0','occ_1',..., dimensions={0} | all-to-all | bytes 2621440 | tf_op jit(solution)/shard_map/all_to_all | solution.py:50
  132.3 1.9 %copy.6 = bf16[128,40,128]{0,2,1:T(8,128)(2,1)} copy(bf16[128,40,128]{2,1,0:T(8,128)(2,1)S(1)} %all_to_all.5) | data formatting | bytes 2621440 | tf_op jit(solution)/shard_map/all_to_all | solution.py:50
  134.2 0.0 copy-done
  134.2 4.4 %convert_bitcast_fusion = bf16[10,128,1024]{2,1,0:T(8,128)(2,1)} fusion(bf16[128,10,512]{0,2,1:T(8,128)(2,1)} %bitcast.46, bf16[1024,512]{1,0:T(8,128)(2,1)S(1)} %copy-done), kind=kOutput, calls=%fused_computation.7 | convolution fusion | flops 1343488000 | bytes 4980736 | tf_op jit(solution)/shard_map/ipa,ma->pim/dot_general | solution.py:52
Async XLA Ops:
  0.0 134.2 %copy-start = (bf16[1024,512]{1,0:T(8,128)(2,1)S(1)}, bf16[1024,512]{1,0:T(8,128)(2,1)}, u32[]{:S(2)}) copy-start(bf16[1024,512]{1,0:T(8,128)(2,1)} %param.7) | copy-start | bytes 3145732
  0.0 35.4 %collective-permute-start.1 = (bf16[512,1280]{1,0:T(8,128)(2,1)}, bf16[512,1280]{1,0:T(8,128)(2,1)}, u32[]{:S(2)}, u32[]{:S(2)}) collective-permute-start(bf16[512,1280]{1,0:T(8,128)(2,1)} %bitcast.47), channel_id=1, source_target_pairs={{0,504},{4,12},{8,0},{12,20},{16,8},{20,28},{24,16},{28,36},{32,24... | collective-permute-start | bytes 3932168 | tf_op jit(solution)/shard_map/ppermute | solution.py:13
  5.0 43.4 %collective-permute-start.2 = (bf16[512,1280]{1,0:T(8,128)(2,1)}, bf16[512,1280]{1,0:T(8,128)(2,1)}, u32[]{:S(2)}, u32[]{:S(2)}) collective-permute-start(bf16[512,1280]{1,0:T(8,128)(2,1)} %bitcast.48), channel_id=1, source_target_pairs={{0,8},{4,508},{8,16},{12,4},{16,24},{20,12},{24,32},{28,20},{32,40... | collective-permute-start | bytes 3932168 | tf_op jit(solution)/shard_map/ppermute | solution.py:13
  16.8 43.9 %collective-permute-start = (bf16[512,1280]{1,0:T(8,128)(2,1)}, bf16[512,1280]{1,0:T(8,128)(2,1)}, u32[]{:S(2)}, u32[]{:S(2)}) collective-permute-start(bf16[512,1280]{1,0:T(8,128)(2,1)} %bitcast.49), channel_id=1, source_target_pairs={{0,4},{4,0},{8,12},{12,8},{16,20},{20,16},{24,28},{28,24},{32,36},... | collective-permute-start | bytes 3932168 | tf_op jit(solution)/shard_map/ppermute | solution.py:13
  35.4 36.7 %collective-permute-start.5 = (bf16[512,1280]{1,0:T(8,128)(2,1)}, bf16[512,1280]{1,0:T(8,128)(2,1)}, u32[]{:S(2)}, u32[]{:S(2)}) collective-permute-start(bf16[512,1280]{1,0:T(8,128)(2,1)} %collective-permute-done.1), channel_id=1, source_target_pairs={{0,508},{4,8},{8,4},{12,16},{16,12},{20,24},{24,20},{28,32},{32,28... | collective-permute-start | bytes 3932168 | tf_op jit(solution)/shard_map/ppermute | solution.py:13
  40.1 37.1 %collective-permute-start.3 = (bf16[512,1280]{1,0:T(8,128)(2,1)}, bf16[512,1280]{1,0:T(8,128)(2,1)}, u32[]{:S(2)}, u32[]{:S(2)}) collective-permute-start(bf16[512,1280]{1,0:T(8,128)(2,1)} %collective-permute-done.1), channel_id=1, source_target_pairs={{0,4},{4,0},{8,12},{12,8},{16,20},{20,16},{24,28},{28,24},{32,36},... | collective-permute-start | bytes 3932168 | tf_op jit(solution)/shard_map/ppermute | solution.py:13
  48.3 18.8 %collective-permute-start.4 = (bf16[512,1280]{1,0:T(8,128)(2,1)}, bf16[512,1280]{1,0:T(8,128)(2,1)}, u32[]{:S(2)}, u32[]{:S(2)}) collective-permute-start(bf16[512,1280]{1,0:T(8,128)(2,1)} %collective-permute-done.2), channel_id=1, source_target_pairs={{0,4},{4,0},{8,12},{12,8},{16,20},{20,16},{24,28},{28,24},{32,36},... | collective-permute-start | bytes 3932168 | tf_op jit(solution)/shard_map/ppermute | solution.py:13
  50.3 5.4 %copy-start.1 = (f32[512]{0:T(512)S(1)}, f32[512]{0:T(512)}, u32[]{:S(2)}) copy-start(f32[512]{0:T(512)} %param.6) | copy-start | bytes 6148
  50.3 5.4 %copy-start.2 = (bf16[1,512,1280]{2,1,0:T(8,128)(2,1)S(1)}, bf16[1,512,1280]{2,1,0:T(8,128)(2,1)}, u32[]{:S(2)}) copy-start(bf16[1,512,1280]{2,1,0:T(8,128)(2,1)} %param.4) | copy-start | bytes 3932164

commit v2 on v1

v2 whole, which is shorter than its diff:
```python
import functools

import jax
import jax.numpy as jnp
from jax import lax
from jax.experimental import pallas as pl
from jax.experimental.pallas import tpu as pltpu
from jax.sharding import Mesh
from jax.sharding import PartitionSpec as P

OCC = ("occ_0", "occ_1", "occ_2", "occ_3")
FRAG_OCC = ("frag",) + OCC
LANES = 128
ROWS = 256
VMEM_LIMIT = 40 * 1024 * 1024

NT = (((1,), (1,)), ((), ()))
NN = (((1,), (0,)), ((), ()))


def mirrored(block, count, step):
    route = [(i, (i + step if i % 2 == 0 else i - step) % count) for i in range(count)]
    return lax.ppermute(block, OCC, route)


def pair_energy(steps, places, occ_energy):
    return occ_energy[places[steps[0] + 3]] + occ_energy[places[steps[1] + 3]]


def pair_term(steps, levels, part, left, right):
    places, occ_energy, column, row = levels
    energy = pair_energy(steps, places, occ_energy)
    kmat = lax.dot_general(left[part, :], right[...], NT, preferred_element_type=jnp.float32)
    amps = (kmat / (energy - column[part, :] - row[...])).astype(jnp.bfloat16)
    return lax.dot_general(amps, right[...], NN, preferred_element_type=jnp.float32)


def pairs_kernel(pairs, blocks, carried, again, *refs):
    levels, refs = refs[:4], refs[4:]
    held, refs = refs[:blocks], refs[blocks:]
    totals, outs = refs[:carried], refs[carried:]
    height = held[0].shape[0]
    for start in range(0, height, ROWS):
        part = pl.ds(start, ROWS)
        for k, (steps, left, right) in enumerate(pairs):
            value = pair_term(steps, levels, part, held[left], held[right])
            if k < carried:
                value = value + totals[k][part, :].astype(jnp.float32)
            outs[k][part, :] = value.astype(outs[k].dtype)
    if again:
        outs[-1][...] = held[0][...]


def pairs_sum(levels, blocks, pairs, totals=(), dtypes=(jnp.float32,), again=False):
    shape = blocks[0].shape
    vmem = pl.BlockSpec(memory_space=pltpu.VMEM)
    smem = pl.BlockSpec(memory_space=pltpu.SMEM)
    outs = [jax.ShapeDtypeStruct(shape, dtype) for dtype in dtypes]
    if again:
        outs.append(jax.ShapeDtypeStruct(shape, blocks[0].dtype))
    return pl.pallas_call(
        functools.partial(pairs_kernel, pairs, len(blocks), len(totals), again),
        out_shape=outs,
        in_specs=[smem] * 2 + [vmem] * (2 + len(blocks) + len(totals)),
        out_specs=[vmem] * len(outs),
        compiler_params=pltpu.CompilerParams(vmem_limit_bytes=VMEM_LIMIT),
        cost_estimate=pl.CostEstimate(flops=1000, bytes_accessed=1000, transcendentals=0),
        name="pairs",
    )(*levels, *blocks, *totals)


def last_kernel(steps, *refs):
    levels = refs[:4]
    mine, other, total, arrived, out, wide = refs[4:]
    virtuals, aux = mine.shape
    cols = virtuals // LANES
    for piece in range(cols):
        part = pl.ds(piece * LANES, LANES)
        value = pair_term(steps, levels, part, mine, other)
        value = value + total[part, :] + arrived[part, :].astype(jnp.float32)
        wide[pl.ds(piece, aux, stride=cols), :] = value.T
    out[...] = wide[...].astype(out.dtype)


def last_pair(levels, steps, mine, other, total, arrived):
    virtuals, aux = mine.shape
    cols = virtuals // LANES
    vmem = pl.BlockSpec(memory_space=pltpu.VMEM)
    smem = pl.BlockSpec(memory_space=pltpu.SMEM)
    return pl.pallas_call(
        functools.partial(last_kernel, steps),
        out_shape=jax.ShapeDtypeStruct((aux * cols, LANES), jnp.bfloat16),
        in_specs=[smem] * 2 + [vmem] * 6,
        out_specs=vmem,
        scratch_shapes=[pltpu.VMEM((aux * cols, LANES), jnp.float32)],
        compiler_params=pltpu.CompilerParams(vmem_limit_bytes=VMEM_LIMIT),
        cost_estimate=pl.CostEstimate(flops=1000, bytes_accessed=1000, transcendentals=0),
        name="last",
    )(*levels, mine, other, total, arrived)


def back_kernel(cols, chunk, slabs, coeffs, out, wide, flat):
    count = out.shape[1]
    height = slabs.shape[0] // count

    @pl.when(pl.program_id(0) == 0)
    def _():
        wide[...] = slabs[...].astype(jnp.float32)

    base = pl.program_id(0) * (chunk * cols)
    for p in range(chunk):
        for c in range(cols):
            piece = wide[pl.ds(base + p * cols + c, count, stride=height), :]
            flat[p * count : (p + 1) * count, c * LANES : (c + 1) * LANES] = piece.astype(
                jnp.bfloat16
            )
    back = lax.dot_general(flat[...], coeffs[...], NT, preferred_element_type=jnp.float32)
    out[...] = back.astype(out.dtype).reshape(out.shape)


def back_transform(slabs, coeffs, count):
    atoms, virtuals = coeffs.shape
    cols = virtuals // LANES
    rows = slabs.shape[0] // (count * cols)
    chunk = 2
    return pl.pallas_call(
        functools.partial(back_kernel, cols, chunk),
        grid=(rows // chunk,),
        out_shape=jax.ShapeDtypeStruct((rows, count, atoms), jnp.bfloat16),
        in_specs=[
            pl.BlockSpec(slabs.shape, lambda s: (0, 0)),
            pl.BlockSpec(coeffs.shape, lambda s: (0, 0)),
        ],
        out_specs=pl.BlockSpec((chunk, count, atoms), lambda s: (s, 0, 0)),
        scratch_shapes=[
            pltpu.VMEM(slabs.shape, jnp.float32),
            pltpu.VMEM((chunk * count, virtuals), jnp.bfloat16),
        ],
        compiler_params=pltpu.CompilerParams(vmem_limit_bytes=VMEM_LIMIT),
        cost_estimate=pl.CostEstimate(
            flops=2 * rows * count * virtuals * atoms,
            bytes_accessed=2 * rows * count * (virtuals + atoms),
            transcendentals=0,
        ),
        name="back",
    )(slabs, coeffs)


def on_device(factors, occ_energy, vir_energy, coeffs):
    mine = factors[0]
    count = lax.axis_size(OCC)
    index = lax.axis_index(OCC)
    sign = 1 - 2 * (index % 2)
    places = jnp.stack([(index + sign * k) % count for k in range(-3, 4)])
    levels = (places, occ_energy, vir_energy[:, None], vir_energy[None, :])
    f32, bf16 = jnp.float32, jnp.bfloat16

    plus2 = mirrored(mine, count, -2)
    plus1 = mirrored(mine, count, 1)
    total, again = pairs_sum(levels, [mine, plus1], [((0, 1), 0, 1)], again=True)
    minus2 = mirrored(again, count, 2)
    minus3 = mirrored(plus2, count, -1)
    total, beside = pairs_sum(
        levels, [mine, plus1, plus2], [((0, 2), 0, 2), ((1, 2), 1, 2)], [total], [f32, f32]
    )
    (beside,) = pairs_sum(levels, [plus1, minus2], [((1, -2), 0, 1)], [beside], [bf16])
    (total,) = pairs_sum(levels, [mine, minus2], [((0, -2), 0, 1)], [total])
    arrived = mirrored(beside, count, 1)
    gamma = last_pair(levels, (0, -3), mine, minus3, total, arrived)
    slabs = lax.all_to_all(gamma.reshape(count, -1, LANES), OCC, 0, 0, tiled=True)
    return back_transform(slabs.reshape(-1, LANES), coeffs, count)


def solution(mesh):
    finer = Mesh(
        mesh.devices.reshape(2, 4, 8, 2, mesh.shape["frag"]),
        ("occ_0", "occ_1", "occ_2", "occ_3", "frag"),
    )
    in_specs = (P(FRAG_OCC, None, None), P("frag"), P("frag"), P("frag", None))
    out_specs = P(OCC, "frag", None)
    return jax.shard_map(
        on_device, mesh=finer, in_specs=in_specs, out_specs=out_specs, check_vma=False
    )
```

time: 139 us -> 112 us (0.81)
  matrix products: 38.1 us -> 0 us
  Pallas kernels: 0 us -> 18.5 us
  waiting for transfers between devices: 5.97 us -> 18.3 us
  starting transfers between devices: 34.4 us -> 25 us
  between operations: 7.62 us -> 0.28 us
  local copies, waits for them, and re-layouts: 6.73 us -> 3.57 us
    dot_general x7 -> x0, matrix products: 38.1 us -> none  [the longest x6 33.7 us: contribution(): lax.dot_general(amps, other, (((1,), (0,)), ((), ())), preferred_element_...]
    pallas_call x0 -> x6, Pallas kernels: none -> 18.5 us  [the longest x4 10.8 us: pairs_sum(): pl.pallas_call(functools.partial(pairs_kernel, pairs, len(blocks), len(to...]
    ppermute x6 -> x5, waiting for transfers between devices: 5.97 us -> 18.3 us  [mirrored(): return lax.ppermute(block, OCC, route)]
    ppermute x6 -> x5, starting transfers between devices: 34.4 us -> 25 us  [mirrored(): return lax.ppermute(block, OCC, route)]
    unnamed x6 -> x10, local copies, waits for them, and re-layouts: 0.02 us -> 2.66 us
    all_to_all x1 -> x0, local copies, waits for them, and re-layouts: 1.88 us -> none  [on_device(): slabs = lax.all_to_all(gamma.reshape(count, -1, 128), OCC, 0, 0, tiled=True)]
    reshape x1 -> x0, local copies, waits for them, and re-layouts: 1.64 us -> none  [on_device(): slabs = lax.all_to_all(gamma.reshape(count, -1, 128), OCC, 0, 0, tiled=True)]
    convert_element_type x1 -> x0, local copies, waits for them, and re-layouts: 1.6 us -> none  [on_device(): gamma = total.T.astype(jnp.bfloat16)]
  transfers between devices with their start and end apart: 6 -> 5, of which waited for: 1 -> 3; matrix products, arithmetic and copies ran while one was open for 21% -> 1% of each run, Pallas kernels for 0% -> 10%
where the time goes in v2:
time: 112 us; the launch traced here: 111 us
  blocking collectives  45.8 us (41%)
  starting transfers between devices  25 us (22%)
  Pallas kernels  18.5 us (17%)
  waiting for transfers between devices  18.3 us (16%)
  local copies, waits for them, and re-layouts  3.57 us (3%)
    all_to_all x1, blocking collectives, on_device(): lax.all_to_all(gamma.reshape(count, -1, LANES), OCC, 0, 0, tiled=True)  45.8 us
    ppermute x5, starting transfers between devices, mirrored(): return lax.ppermute(block, OCC, route)  25 us
    ppermute x5, waiting for transfers between devices, mirrored(): return lax.ppermute(block, OCC, route)  18.3 us
    pallas_call x4, Pallas kernels, pairs_sum(): pl.pallas_call(functools.partial(pairs_kernel, pairs, len(blocks), len(to...  10.8 us
    pallas_call x1, Pallas kernels, back_transform(): pl.pallas_call(functools.partial(back_kernel, cols, chunk), grid=(rows //...  3.99 us
    pallas_call x1, Pallas kernels, last_pair(): pl.pallas_call(functools.partial(last_kernel, steps), out_shape=jax.Shape...  3.69 us
    unnamed x10, local copies, waits for them, and re-layouts  2.66 us
  transfers between devices with their start and end apart: 5, of which 3 were waited for; matrix products, arithmetic and copies ran while one was open for 1% of the time, Pallas kernels for 10%

profile of v2, /device:TPU:1, one launch (start us, length us, event | category | flops | bytes accessed | tf_op | source)
XLA Modules:
  0.0 111.5 jit_solution(8347443914013556434)
XLA Ops:
  0.0 8.8 %collective-permute-start.2 = (bf16[512,1280]{1,0:T(8,128)(2,1)}, bf16[512,1280]{1,0:T(8,128)(2,1)S(1)}, u32[]{:S(2)}, u32[]{:S(2)}) collective-permute-start(bf16[512,1280]{1,0:T(8,128)(2,1)} %bitcast.12), channel_id=1, source_target_pairs={{0,4},{4,0},{8,12},{12,8},{16,20},{20,16},{24,28},{28,24},{32,36},... | collective-permute-start | bytes 3932168 | tf_op jit(solution)/shard_map/ppermute | solution.py:23
  8.8 1.9 %collective-permute-start = (bf16[512,1280]{1,0:T(8,128)(2,1)}, bf16[512,1280]{1,0:T(8,128)(2,1)S(1)}, u32[]{:S(2)}, u32[]{:S(2)}) collective-permute-start(bf16[512,1280]{1,0:T(8,128)(2,1)} %bitcast.13), channel_id=1, source_target_pairs={{0,504},{4,12},{8,0},{12,20},{16,8},{20,28},{24,16},{28,36},{32,24... | collective-permute-start | bytes 3932168 | tf_op jit(solution)/shard_map/ppermute | solution.py:23
  10.8 0.8 copy.9.refs_2_
  11.7 0.1 stack.31.refs_0_
  11.8 0.0 collective-permute-done.2.refs_5_.refs_4_
  11.8 0.0 copy-start
  11.8 1.3 %copy-done = bf16[1,512,1280]{2,1,0:T(8,128)(2,1)S(1)} copy-done((bf16[1,512,1280]{2,1,0:T(8,128)(2,1)S(1)}, bf16[1,512,1280]{2,1,0:T(8,128)(2,1)}, u32[]{:S(2)}) %copy-start) | copy-done | bytes 1310744
  13.1 0.0 copy-start.3
  13.1 0.7 copy-done.3
  13.8 0.0 copy-start.4
  13.8 0.7 copy-done.4
  14.5 2.3 %pairs.4 = (f32[512,1280]{1,0:T(8,128)S(1)}, bf16[512,1280]{1,0:T(8,128)(2,1)S(1)}) custom-call(s32[7]{0:T(128)S(1)} %stack.31.refs_0_, f32[128]{0:T(128)S(1)} %copy-done.4, f32[512,1]{1,0:T(8,128)S(1)} %copy.9.refs_2_, f32[1,512]{1,0:T(1,128)S(1)} %bitcast.21, bf16[512,1280]{1,0:T(8,128)(2,1)S(1)} %bitcast.14, ...), custom_call_target="tpu_custom_call" | custom-call | flops 1000 | bytes 1000 | tf_op jit(solution)/shard_map/pairs/pallas_call | solution.py:61
  16.8 8.5 %collective-permute-start.3 = (bf16[512,1280]{1,0:T(8,128)(2,1)S(1)}, bf16[512,1280]{1,0:T(8,128)(2,1)S(1)}, u32[]{:S(2)}, u32[]{:S(2)}) collective-permute-start(bf16[512,1280]{1,0:T(8,128)(2,1)S(1)} %get-tuple-element.9), channel_id=1, source_target_pairs={{0,8},{4,508},{8,16},{12,4},{16,24},{20,12},{24,32},{28,20},{32,40... | collective-permute-start | bytes 3932168 | tf_op jit(solution)/shard_map/ppermute | solution.py:23
  25.3 7.2 %collective-permute-done.refs_6_ = bf16[512,1280]{1,0:T(8,128)(2,1)S(1)} collective-permute-done((bf16[512,1280]{1,0:T(8,128)(2,1)}, bf16[512,1280]{1,0:T(8,128)(2,1)S(1)}, u32[]{:S(2)}, u32[]{:S(2)}) %collective-permute-start) | collective-permute-done | bytes 1310752 | tf_op jit(solution)/shard_map/ppermute | solution.py:23
  32.5 3.8 %collective-permute-start.1 = (bf16[512,1280]{1,0:T(8,128)(2,1)S(1)}, bf16[512,1280]{1,0:T(8,128)(2,1)S(1)}, u32[]{:S(2)}, u32[]{:S(2)}) collective-permute-start(bf16[512,1280]{1,0:T(8,128)(2,1)S(1)} %collective-permute-done.refs_6_), channel_id=1, source_target_pairs={{0,508},{4,8},{8,4},{12,16},{16,12},{20,24},{24,20},{28,32},{32,28... | collective-permute-start | bytes 3932168 | tf_op jit(solution)/shard_map/ppermute | solution.py:23
  36.3 3.8 %pairs.5 = (f32[512,1280]{1,0:T(8,128)S(1)}, f32[512,1280]{1,0:T(8,128)S(1)}) custom-call(s32[7]{0:T(128)S(1)} %stack.31.refs_0_, f32[128]{0:T(128)S(1)} %copy-done.4, f32[512,1]{1,0:T(8,128)S(1)} %copy.9.refs_2_, f32[1,512]{1,0:T(1,128)S(1)} %bitcast.22, bf16[512,1280]{1,0:T(8,128)(2,1)S(1)} %bitcast.15, ...), custom_call_target="tpu_custom_call" | custom-call | flops 1000 | bytes 1000 | tf_op jit(solution)/shard_map/pairs/pallas_call | solution.py:61
  40.2 10.5 %collective-permute-done.3.refs_5_ = bf16[512,1280]{1,0:T(8,128)(2,1)S(1)} collective-permute-done((bf16[512,1280]{1,0:T(8,128)(2,1)S(1)}, bf16[512,1280]{1,0:T(8,128)(2,1)S(1)}, u32[]{:S(2)}, u32[]{:S(2)}) %collective-permute-start.3) | collective-permute-done | bytes 1310752 | tf_op jit(solution)/shard_map/ppermute | solution.py:23
  50.7 0.0 copy-start.1
  50.7 2.3 %pairs.7 = bf16[512,1280]{1,0:T(8,128)(2,1)S(1)} custom-call(s32[7]{0:T(128)S(1)} %stack.31.refs_0_, f32[128]{0:T(128)S(1)} %copy-done.4, f32[512,1]{1,0:T(8,128)S(1)} %copy.9.refs_2_, f32[1,512]{1,0:T(1,128)S(1)} %bitcast.23, bf16[512,1280]{1,0:T(8,128)(2,1)S(1)} %collective-permute-done.2.refs_5_.refs_4_, ...), custom_call_target="tpu_custom_call" | custom-call | flops 1000 | bytes 1000 | tf_op jit(solution)/shard_map/pairs/pallas_call | solution.py:61
  53.0 1.9 %collective-permute-start.4 = (bf16[512,1280]{1,0:T(8,128)(2,1)S(1)}, bf16[512,1280]{1,0:T(8,128)(2,1)S(1)}, u32[]{:S(2)}, u32[]{:S(2)}) collective-permute-start(bf16[512,1280]{1,0:T(8,128)(2,1)S(1)} %pairs.7), channel_id=1, source_target_pairs={{0,4},{4,0},{8,12},{12,8},{16,20},{20,16},{24,28},{28,24},{32,36},... | collective-permute-start | bytes 3932168 | tf_op jit(solution)/shard_map/ppermute | solution.py:23
  54.9 0.0 copy-done.1
  54.9 2.3 %pairs.6.refs_6_ = f32[512,1280]{1,0:T(8,128)S(1)} custom-call(s32[7]{0:T(128)S(1)} %stack.31.refs_0_, f32[128]{0:T(128)S(1)} %copy-done.4, f32[512,1]{1,0:T(8,128)S(1)} %copy.9.refs_2_, f32[1,512]{1,0:T(1,128)S(1)} %bitcast.24, bf16[512,1280]{1,0:T(8,128)(2,1)S(1)} %bitcast.16, bf16[512,1280]{1,0:T(8,128)(2,1)S(1)} %collective-permute-done.3.refs_5_, ...), custom_call_target="tpu_custom_call" | custom-call | flops 1000 | bytes 1000 | tf_op jit(solution)/shard_map/pairs/pallas_call | solution.py:61
  57.2 0.0 collective-permute-done.1.refs_5_
  57.2 0.7 collective-permute-done.4.refs_7_
  57.9 3.7 %last.1 = bf16[5120,128]{1,0:T(8,128)(2,1)S(1)} custom-call(s32[7]{0:T(128)S(1)} %stack.31.refs_0_, f32[128]{0:T(128)S(1)} %copy-done.4, f32[512,1]{1,0:T(8,128)S(1)} %copy.9.refs_2_, f32[1,512]{1,0:T(1,128)S(1)} %bitcast.25, bf16[512,1280]{1,0:T(8,128)(2,1)S(1)} %bitcast.17, bf16[512,1280]{1,0:T(8,128)(2,1)S(1)} %collective-permute-done.1.refs_5_, ...), custom_call_target="tpu_custom_call" | custom-call | flops 1000 | bytes 1000 | tf_op jit(solution)/shard_map/last/pallas_call | solution.py:90
  61.6 0.0 copy-start.2
  61.6 45.8 %all_to_all.5 = bf16[128,40,128]{2,1,0:T(8,128)(2,1)S(1)} all-to-all(bf16[128,40,128]{2,1,0:T(8,128)(2,1)S(1)} %bitcast.18), channel_id=1, replica_groups=mesh['occ_0'=2,'occ_1'=4,'occ_2'=8,'occ_3'=2,'frag'=4] {'occ_0','occ_1',..., dimensions={0} | all-to-all | bytes 2621440 | tf_op jit(solution)/shard_map/all_to_all | solution.py:170
  107.5 0.0 copy-done.2
  107.5 4.0 %back.1 = bf16[10,128,1024]{2,1,0:T(8,128)(2,1)} custom-call(bf16[5120,128]{1,0:T(8,128)(2,1)S(1)} %bitcast.19, bf16[1024,512]{1,0:T(8,128)(2,1)S(1)} %copy-done.2), custom_call_target="tpu_custom_call" | custom-call | flops 1342177280 | bytes 3932160 | tf_op jit(solution)/shard_map/back/pallas_call | solution.py:126
Async XLA Ops:
  0.0 11.8 %collective-permute-start.2 = (bf16[512,1280]{1,0:T(8,128)(2,1)}, bf16[512,1280]{1,0:T(8,128)(2,1)S(1)}, u32[]{:S(2)}, u32[]{:S(2)}) collective-permute-start(bf16[512,1280]{1,0:T(8,128)(2,1)} %bitcast.12), channel_id=1, source_target_pairs={{0,4},{4,0},{8,12},{12,8},{16,20},{20,16},{24,28},{28,24},{32,36},... | collective-permute-start | bytes 3932168 | tf_op jit(solution)/shard_map/ppermute | solution.py:23
  8.8 23.7 %collective-permute-start = (bf16[512,1280]{1,0:T(8,128)(2,1)}, bf16[512,1280]{1,0:T(8,128)(2,1)S(1)}, u32[]{:S(2)}, u32[]{:S(2)}) collective-permute-start(bf16[512,1280]{1,0:T(8,128)(2,1)} %bitcast.13), channel_id=1, source_target_pairs={{0,504},{4,12},{8,0},{12,20},{16,8},{20,28},{24,16},{28,36},{32,24... | collective-permute-start | bytes 3932168 | tf_op jit(solution)/shard_map/ppermute | solution.py:23
  11.8 1.3 %copy-start = (bf16[1,512,1280]{2,1,0:T(8,128)(2,1)S(1)}, bf16[1,512,1280]{2,1,0:T(8,128)(2,1)}, u32[]{:S(2)}) copy-start(bf16[1,512,1280]{2,1,0:T(8,128)(2,1)} %param.4) | copy-start | bytes 3932164
  13.1 0.7 copy-start.3
  13.8 0.7 copy-start.4
  16.8 33.9 %collective-permute-start.3 = (bf16[512,1280]{1,0:T(8,128)(2,1)S(1)}, bf16[512,1280]{1,0:T(8,128)(2,1)S(1)}, u32[]{:S(2)}, u32[]{:S(2)}) collective-permute-start(bf16[512,1280]{1,0:T(8,128)(2,1)S(1)} %get-tuple-element.9), channel_id=1, source_target_pairs={{0,8},{4,508},{8,16},{12,4},{16,24},{20,12},{24,32},{28,20},{32,40... | collective-permute-start | bytes 3932168 | tf_op jit(solution)/shard_map/ppermute | solution.py:23
  32.5 24.7 %collective-permute-start.1 = (bf16[512,1280]{1,0:T(8,128)(2,1)S(1)}, bf16[512,1280]{1,0:T(8,128)(2,1)S(1)}, u32[]{:S(2)}, u32[]{:S(2)}) collective-permute-start(bf16[512,1280]{1,0:T(8,128)(2,1)S(1)} %collective-permute-done.refs_6_), channel_id=1, source_target_pairs={{0,508},{4,8},{8,4},{12,16},{16,12},{20,24},{24,20},{28,32},{32,28... | collective-permute-start | bytes 3932168 | tf_op jit(solution)/shard_map/ppermute | solution.py:23
  50.7 4.3 %copy-start.1 = (bf16[1,512,1280]{2,1,0:T(8,128)(2,1)S(1)}, bf16[1,512,1280]{2,1,0:T(8,128)(2,1)}, u32[]{:S(2)}) copy-start(bf16[1,512,1280]{2,1,0:T(8,128)(2,1)} %param.4) | copy-start | bytes 3932164
  53.0 4.9 %collective-permute-start.4 = (bf16[512,1280]{1,0:T(8,128)(2,1)S(1)}, bf16[512,1280]{1,0:T(8,128)(2,1)S(1)}, u32[]{:S(2)}, u32[]{:S(2)}) collective-permute-start(bf16[512,1280]{1,0:T(8,128)(2,1)S(1)} %pairs.7), channel_id=1, source_target_pairs={{0,4},{4,0},{8,12},{12,8},{16,20},{20,16},{24,28},{28,24},{32,36},... | collective-permute-start | bytes 3932168 | tf_op jit(solution)/shard_map/ppermute | solution.py:23
  61.6 45.9 %copy-start.2 = (bf16[1024,512]{1,0:T(8,128)(2,1)S(1)}, bf16[1024,512]{1,0:T(8,128)(2,1)}, u32[]{:S(2)}) copy-start(bf16[1024,512]{1,0:T(8,128)(2,1)} %coeffs.1) | copy-start | bytes 3145732

commit v3 on v1

v3 whole, which is shorter than its diff:
```python
import functools

import jax
import jax.numpy as jnp
from jax import lax
from jax.experimental import pallas as pl
from jax.experimental.pallas import tpu as pltpu
from jax.sharding import Mesh
from jax.sharding import PartitionSpec as P

OCC = ("occ_0", "occ_1", "occ_2", "occ_3")
FRAG_OCC = ("frag",) + OCC
LANES = 128
PARTS = 2
VMEM_LIMIT = 40 * 1024 * 1024

NT = (((1,), (1,)), ((), ()))
TN = (((0,), (0,)), ((), ()))


def mirrored(block, count, step):
    route = [(i, (i + step if i % 2 == 0 else i - step) % count) for i in range(count)]
    return lax.ppermute(block, OCC, route)


def amplitudes(steps, levels, left, right):
    places, occ_energy, column, row = levels
    energy = occ_energy[places[steps[0] + 3]] + occ_energy[places[steps[1] + 3]]
    kmat = lax.dot_general(right[...], left[...], NT, preferred_element_type=jnp.float32)
    return (kmat / (energy - column[...] - row[...])).astype(jnp.bfloat16)


def pair_terms(amps, right):
    aux = right.shape[1]
    for start in range(0, aux, aux // PARTS):
        block = right[:, start : start + aux // PARTS]
        yield (
            pl.ds(start, aux // PARTS),
            lax.dot_general(block, amps, TN, preferred_element_type=jnp.float32),
        )


def pairs_kernel(pairs, blocks, carried, *refs):
    levels, refs = refs[:4], refs[4:]
    held, refs = refs[:blocks], refs[blocks:]
    totals, outs = refs[:carried], refs[carried:]
    for k, (steps, left, right) in enumerate(pairs):
        amps = amplitudes(steps, levels, held[left], held[right])
        for part, value in pair_terms(amps, held[right]):
            if k < carried:
                value = value + totals[k][part, :]
            outs[k][part, :] = value.astype(outs[k].dtype)


def first_kernel(steps, *refs):
    levels = refs[:4]
    mine, upper, lower, total, again, other = refs[4:]
    half = upper.shape[0]
    other[:half, :] = upper[...]
    other[half:, :] = lower[...]
    again[...] = mine[...]
    amps = amplitudes(steps, levels, mine, other)
    for part, value in pair_terms(amps, other):
        total[part, :] = value


def last_kernel(steps, *refs):
    levels = refs[:4]
    mine, other, total, arrived, out, wide = refs[4:]
    cols = mine.shape[0] // LANES
    amps = amplitudes(steps, levels, mine, other)
    for part, value in pair_terms(amps, other):
        value = value + total[part, :] + arrived[part, :].astype(jnp.float32)
        for c in range(cols):
            rows = pl.ds(part.start * cols + c, part.size, stride=cols)
            wide[rows, :] = value[:, c * LANES : (c + 1) * LANES]
    out[...] = wide[...].astype(out.dtype)


def local_call(kernel, levels, arrays, outs, scratch=(), name=None, flops=1000):
    vmem = pl.BlockSpec(memory_space=pltpu.VMEM)
    smem = pl.BlockSpec(memory_space=pltpu.SMEM)
    return pl.pallas_call(
        kernel,
        out_shape=[jax.ShapeDtypeStruct(shape, dtype) for shape, dtype in outs],
        in_specs=[smem] * 2 + [vmem] * (2 + len(arrays)),
        out_specs=[vmem] * len(outs),
        scratch_shapes=list(scratch),
        compiler_params=pltpu.CompilerParams(vmem_limit_bytes=VMEM_LIMIT),
        cost_estimate=pl.CostEstimate(flops=flops, bytes_accessed=1000, transcendentals=0),
        name=name,
    )(*levels, *arrays)


def pairs_sum(levels, blocks, pairs, totals, dtypes):
    shape = blocks[0].shape[::-1]
    kernel = functools.partial(pairs_kernel, pairs, len(blocks), len(totals))
    outs = [(shape, dtype) for dtype in dtypes]
    flops = 10**10 if len(pairs) > 1 else 1000
    return local_call(kernel, levels, [*blocks, *totals], outs, name="pairs", flops=flops)


def first_pair(levels, steps, mine, upper, lower):
    block = (mine.shape, mine.dtype)
    outs = [(mine.shape[::-1], jnp.float32), block, block]
    kernel = functools.partial(first_kernel, steps)
    return local_call(kernel, levels, [mine, upper, lower], outs, name="first")


def last_pair(levels, steps, mine, other, total, arrived):
    shape = (mine.size // LANES, LANES)
    kernel = functools.partial(last_kernel, steps)
    (gamma,) = local_call(
        kernel,
        levels,
        [mine, other, total, arrived],
        [(shape, jnp.bfloat16)],
        [pltpu.VMEM(shape, jnp.float32)],
        name="last",
    )
    return gamma


def back_kernel(chunk, slabs, coeffs, out, wide, flat, done, sems):
    rows, count, _ = done.shape
    cols = coeffs.shape[1] // LANES
    wide[...] = slabs[...].astype(jnp.float32)
    copies = []
    for k in range(rows // chunk):
        for p in range(chunk):
            for c in range(cols):
                source = pl.ds(((k * chunk + p) * cols) + c, count, stride=rows * cols)
                flat[p * count : (p + 1) * count, c * LANES : (c + 1) * LANES] = wide[
                    source, :
                ].astype(flat.dtype)
        back = lax.dot_general(flat[...], coeffs[...], NT, preferred_element_type=jnp.float32)
        part = pl.ds(k * chunk, chunk)
        done[part] = back.astype(done.dtype).reshape(chunk, count, -1)
        copies.append(pltpu.make_async_copy(done.at[part], out.at[part], sems.at[k]))
        copies[-1].start()
    for copy in copies:
        copy.wait()


def back_transform(slabs, coeffs, count):
    atoms, virtuals = coeffs.shape
    rows = slabs.size // (count * virtuals)
    chunk = 2
    shape = (rows, count, atoms)
    vmem = pl.BlockSpec(memory_space=pltpu.VMEM)
    return pl.pallas_call(
        functools.partial(back_kernel, chunk),
        out_shape=jax.ShapeDtypeStruct(shape, jnp.bfloat16),
        in_specs=[vmem, vmem],
        out_specs=pl.BlockSpec(memory_space=pl.ANY),
        scratch_shapes=[
            pltpu.VMEM(slabs.shape, jnp.float32),
            pltpu.VMEM((chunk * count, virtuals), jnp.bfloat16),
            pltpu.VMEM(shape, jnp.bfloat16),
            pltpu.SemaphoreType.DMA((rows // chunk,)),
        ],
        compiler_params=pltpu.CompilerParams(vmem_limit_bytes=VMEM_LIMIT),
        cost_estimate=pl.CostEstimate(
            flops=2 * rows * count * virtuals * atoms,
            bytes_accessed=2 * rows * count * (virtuals + atoms),
            transcendentals=0,
        ),
        name="back",
    )(slabs, coeffs)


def on_device(factors, occ_energy, vir_energy, coeffs):
    mine = factors[0]
    count = lax.axis_size(OCC)
    index = lax.axis_index(OCC)
    sign = 1 - 2 * (index % 2)
    places = jnp.stack([(index + sign * k) % count for k in range(-3, 4)])
    levels = (places, occ_energy, vir_energy[:, None], vir_energy[None, :])
    f32, bf16 = jnp.float32, jnp.bfloat16

    half = mine.shape[0] // 2
    plus2 = mirrored(mine, count, -2)
    upper = mirrored(mine[:half], count, 1)
    lower = mirrored(mine[half:], count, 1)
    total, again, plus1 = first_pair(levels, (0, 1), mine, upper, lower)
    minus2 = mirrored(again, count, 2)
    minus3 = mirrored(plus2, count, -1)
    total, beside = pairs_sum(
        levels, [mine, plus1, plus2], [((0, 2), 0, 2), ((1, 2), 1, 2)], [total], [f32, f32]
    )
    (beside,) = pairs_sum(levels, [plus1, minus2], [((1, -2), 0, 1)], [beside], [bf16])
    (total,) = pairs_sum(levels, [mine, minus2], [((0, -2), 0, 1)], [total], [f32])
    arrived = mirrored(beside, count, 1)
    gamma = last_pair(levels, (0, -3), mine, minus3, total, arrived)
    slabs = lax.all_to_all(gamma.reshape(count, -1, LANES), OCC, 0, 0, tiled=True)
    return back_transform(slabs.reshape(-1, LANES), coeffs, count)


def solution(mesh):
    finer = Mesh(
        mesh.devices.reshape(2, 4, 8, 2, mesh.shape["frag"]),
        ("occ_0", "occ_1", "occ_2", "occ_3", "frag"),
    )
    in_specs = (P(FRAG_OCC, None, None), P("frag"), P("frag"), P("frag", None))
    out_specs = P(OCC, "frag", None)
    return jax.shard_map(
        on_device, mesh=finer, in_specs=in_specs, out_specs=out_specs, check_vma=False
    )
```

time: 139 us -> 109 us (0.78)
  matrix products: 38.1 us -> 0 us
  Pallas kernels: 0 us -> 16 us
  waiting for transfers between devices: 5.97 us -> 21.4 us
  between operations: 7.62 us -> 0.29 us
  blocking collectives: 45.1 us -> 39.6 us
  starting transfers between devices: 34.4 us -> 29.2 us
  local copies, waits for them, and re-layouts: 6.73 us -> 2.46 us
    dot_general x7 -> x0, matrix products: 38.1 us -> none  [the longest x6 33.7 us: contribution(): lax.dot_general(amps, other, (((1,), (0,)), ((), ())), preferred_element_...]
    pallas_call x0 -> x6, Pallas kernels: none -> 16 us  [the longest x5 13.4 us: local_call(): pl.pallas_call(kernel, out_shape=[jax.ShapeDtypeStruct(shape, dtype) for...]
    ppermute x6, waiting for transfers between devices: 5.97 us -> 21.4 us  [mirrored(): return lax.ppermute(block, OCC, route)]
    all_to_all x1, blocking collectives: 45.1 us -> 39.6 us  [on_device(): lax.all_to_all(gamma.reshape(count, -1, LANES), OCC, 0, 0, tiled=True)]
    ppermute x6, starting transfers between devices: 34.4 us -> 29.2 us  [mirrored(): return lax.ppermute(block, OCC, route)]
    slice x0 -> x1, local copies, waits for them, and re-layouts: none -> 2.21 us  [on_device(): lower = mirrored(mine[half:], count, 1)]
    all_to_all x1 -> x0, local copies, waits for them, and re-layouts: 1.88 us -> none  [on_device(): slabs = lax.all_to_all(gamma.reshape(count, -1, 128), OCC, 0, 0, tiled=True)]
    reshape x1 -> x0, local copies, waits for them, and re-layouts: 1.64 us -> none  [on_device(): slabs = lax.all_to_all(gamma.reshape(count, -1, 128), OCC, 0, 0, tiled=True)]
  transfers between devices with their start and end apart: 6 -> 6, of which waited for: 1 -> 4; matrix products, arithmetic and copies ran while one was open for 21% -> 2% of each run, Pallas kernels for 0% -> 10%
where the time goes in v3:
time: 109 us
  blocking collectives  39.6 us (36%)
  starting transfers between devices  29.2 us (27%)
  waiting for transfers between devices  21.4 us (20%)
  Pallas kernels  16 us (15%)
  local copies, waits for them, and re-layouts  2.46 us (2%)
    all_to_all x1, blocking collectives, on_device(): lax.all_to_all(gamma.reshape(count, -1, LANES), OCC, 0, 0, tiled=True)  39.6 us
    ppermute x6, starting transfers between devices, mirrored(): return lax.ppermute(block, OCC, route)  29.2 us
    ppermute x6, waiting for transfers between devices, mirrored(): return lax.ppermute(block, OCC, route)  21.4 us
    pallas_call x5, Pallas kernels, local_call(): pl.pallas_call(kernel, out_shape=[jax.ShapeDtypeStruct(shape, dtype) for...  13.4 us
    pallas_call x1, Pallas kernels, back_transform(): pl.pallas_call(functools.partial(back_kernel, chunk), out_shape=jax.Shape...  2.66 us
    slice x1, local copies, waits for them, and re-layouts, on_device(): lower = mirrored(mine[half:], count, 1)  2.21 us
  transfers between devices with their start and end apart: 6, of which 4 were waited for; matrix products, arithmetic and copies ran while one was open for 2% of the time, Pallas kernels for 10%

profile of v3, /device:TPU:1, one launch (start us, length us, event | category | flops | bytes accessed | tf_op | source)
XLA Modules:
  0.0 109.0 jit_solution(16717083048797524939)
XLA Ops:
  0.0 0.0 copy-start.2
  0.0 0.0 copy-start
  0.0 0.0 copy-start.3
  0.0 5.0 %collective-permute-start = (bf16[512,1280]{1,0:T(8,128)(2,1)}, bf16[512,1280]{1,0:T(8,128)(2,1)}, u32[]{:S(2)}, u32[]{:S(2)}) collective-permute-start(bf16[512,1280]{1,0:T(8,128)(2,1)} %bitcast.16), channel_id=1, source_target_pairs={{0,504},{4,12},{8,0},{12,20},{16,8},{20,28},{24,16},{28,36},{32,24... | collective-permute-start | bytes 3932168 | tf_op jit(solution)/shard_map/ppermute | solution.py:23
  5.0 2.2 %slice_bitcast_fusion = (bf16[256,1280]{1,0:T(8,128)(2,1)S(1)}, bf16[256,1280]{1,0:T(8,128)(2,1)}) fusion(bf16[1,512,1280]{2,1,0:T(8,128)(2,1)} %param.4), kind=kLoop, calls=%fused_computation | loop fusion | bytes 2621440 | tf_op jit(solution)/shard_map/slice | solution.py:184
  7.2 12.7 %collective-permute-start.2 = (bf16[256,1280]{1,0:T(8,128)(2,1)}, bf16[256,1280]{1,0:T(8,128)(2,1)S(1)}, u32[]{:S(2)}, u32[]{:S(2)}) collective-permute-start(bf16[256,1280]{1,0:T(8,128)(2,1)} %get-tuple-element.16), channel_id=1, source_target_pairs={{0,4},{4,0},{8,12},{12,8},{16,20},{20,16},{24,28},{28,24},{32,36},... | collective-permute-start | bytes 1966088 | tf_op jit(solution)/shard_map/ppermute | solution.py:23
  19.9 1.9 %collective-permute-start.3 = (bf16[256,1280]{1,0:T(8,128)(2,1)S(1)}, bf16[256,1280]{1,0:T(8,128)(2,1)S(1)}, u32[]{:S(2)}, u32[]{:S(2)}) collective-permute-start(bf16[256,1280]{1,0:T(8,128)(2,1)S(1)} %get-tuple-element.15), channel_id=1, source_target_pairs={{0,4},{4,0},{8,12},{12,8},{16,20},{20,16},{24,28},{28,24},{32,36},... | collective-permute-start | bytes 1966088 | tf_op jit(solution)/shard_map/ppermute | solution.py:23
  22.0 0.0 copy-done.2
  22.0 0.1 copy.9.refs_2_
  22.2 0.1 stack.31.refs_0_
  22.3 0.0 collective-permute-done.2.refs_5_
  22.3 1.6 %collective-permute-done.3.refs_6_ = bf16[256,1280]{1,0:T(8,128)(2,1)S(1)} collective-permute-done((bf16[256,1280]{1,0:T(8,128)(2,1)S(1)}, bf16[256,1280]{1,0:T(8,128)(2,1)S(1)}, u32[]{:S(2)}, u32[]{:S(2)}) %collective-permute-start.3) | collective-permute-done | bytes 655392 | tf_op jit(solution)/shard_map/ppermute | solution.py:23
  23.9 0.0 copy-done
  23.9 0.0 copy-done.3
  23.9 2.2 %first.1 = (f32[1280,512]{1,0:T(8,128)S(1)}, bf16[512,1280]{1,0:T(8,128)(2,1)S(1)}, bf16[512,1280]{1,0:T(8,128)(2,1)S(1)}) custom-call(s32[7]{0:T(128)S(1)} %stack.31.refs_0_, f32[128]{0:T(128)S(1)} %copy-done.3, f32[512,1]{1,0:T(8,128)S(1)} %copy.9.refs_2_, f32[1,512]{1,0:T(1,128)S(1)} %bitcast.24, bf16[512,1280]{1,0:T(8,128)(2,1)S(1)} %bitcast.17, ...), custom_call_target="tpu_custom_call" | custom-call | flops 1000 | bytes 1000 | tf_op jit(solution)/shard_map/first/pallas_call | solution.py:83
  26.2 2.2 %collective-permute-start.4 = (bf16[512,1280]{1,0:T(8,128)(2,1)S(1)}, bf16[512,1280]{1,0:T(8,128)(2,1)S(1)}, u32[]{:S(2)}, u32[]{:S(2)}) collective-permute-start(bf16[512,1280]{1,0:T(8,128)(2,1)S(1)} %get-tuple-element.10), channel_id=1, source_target_pairs={{0,8},{4,508},{8,16},{12,4},{16,24},{20,12},{24,32},{28,20},{32,40... | collective-permute-start | bytes 3932168 | tf_op jit(solution)/shard_map/ppermute | solution.py:23
  28.3 1.8 %collective-permute-done.refs_6_ = bf16[512,1280]{1,0:T(8,128)(2,1)} collective-permute-done((bf16[512,1280]{1,0:T(8,128)(2,1)}, bf16[512,1280]{1,0:T(8,128)(2,1)}, u32[]{:S(2)}, u32[]{:S(2)}) %collective-permute-start) | collective-permute-done | bytes 1310752 | tf_op jit(solution)/shard_map/ppermute | solution.py:23
  30.2 1.9 %collective-permute-start.1 = (bf16[512,1280]{1,0:T(8,128)(2,1)}, bf16[512,1280]{1,0:T(8,128)(2,1)S(1)}, u32[]{:S(2)}, u32[]{:S(2)}) collective-permute-start(bf16[512,1280]{1,0:T(8,128)(2,1)} %collective-permute-done.refs_6_), channel_id=1, source_target_pairs={{0,508},{4,8},{8,4},{12,16},{16,12},{20,24},{24,20},{28,32},{32,28... | collective-permute-start | bytes 3932168 | tf_op jit(solution)/shard_map/ppermute | solution.py:23
  32.1 4.4 %pairs.3 = (f32[1280,512]{1,0:T(8,128)S(1)}, f32[1280,512]{1,0:T(8,128)S(1)}) custom-call(s32[7]{0:T(128)S(1)} %stack.31.refs_0_, f32[128]{0:T(128)S(1)} %copy-done.3, f32[512,1]{1,0:T(8,128)S(1)} %copy.9.refs_2_, f32[1,512]{1,0:T(1,128)S(1)} %bitcast.25, bf16[512,1280]{1,0:T(8,128)(2,1)S(1)} %bitcast.18, ...), custom_call_target="tpu_custom_call" | custom-call | flops 10000000000 | bytes 1000 | tf_op jit(solution)/shard_map/pairs/pallas_call | solution.py:83
  36.5 17.5 %collective-permute-done.4.refs_5_ = bf16[512,1280]{1,0:T(8,128)(2,1)S(1)} collective-permute-done((bf16[512,1280]{1,0:T(8,128)(2,1)S(1)}, bf16[512,1280]{1,0:T(8,128)(2,1)S(1)}, u32[]{:S(2)}, u32[]{:S(2)}) %collective-permute-start.4) | collective-permute-done | bytes 1310752 | tf_op jit(solution)/shard_map/ppermute | solution.py:23
  54.0 2.2 %pairs.5 = bf16[1280,512]{1,0:T(8,128)(2,1)S(1)} custom-call(s32[7]{0:T(128)S(1)} %stack.31.refs_0_, f32[128]{0:T(128)S(1)} %copy-done.3, f32[512,1]{1,0:T(8,128)S(1)} %copy.9.refs_2_, f32[1,512]{1,0:T(1,128)S(1)} %bitcast.26, bf16[512,1280]{1,0:T(8,128)(2,1)S(1)} %get-tuple-element.11.refs_5_.refs_4_, bf16[512,1280]{1,0:T(8,128)(2,1)S(1)} %collective-permute-done.4.refs_5_, ...), custom_call_target="tpu_custom_call" | custom-call | flops 1000 | bytes 1000 | tf_op jit(solution)/shard_map/pairs/pallas_call | solution.py:83
  56.2 5.5 %collective-permute-start.5 = (bf16[1280,512]{1,0:T(8,128)(2,1)S(1)}, bf16[1280,512]{1,0:T(8,128)(2,1)S(1)}, u32[]{:S(2)}, u32[]{:S(2)}) collective-permute-start(bf16[1280,512]{1,0:T(8,128)(2,1)S(1)} %pairs.5), channel_id=1, source_target_pairs={{0,4},{4,0},{8,12},{12,8},{16,20},{20,16},{24,28},{28,24},{32,36},... | collective-permute-start | bytes 3932168 | tf_op jit(solution)/shard_map/ppermute | solution.py:23
  61.7 2.2 %pairs.4.refs_6_ = f32[1280,512]{1,0:T(8,128)S(1)} custom-call(s32[7]{0:T(128)S(1)} %stack.31.refs_0_, f32[128]{0:T(128)S(1)} %copy-done.3, f32[512,1]{1,0:T(8,128)S(1)} %copy.9.refs_2_, f32[1,512]{1,0:T(1,128)S(1)} %bitcast.27, bf16[512,1280]{1,0:T(8,128)(2,1)S(1)} %bitcast.19, bf16[512,1280]{1,0:T(8,128)(2,1)S(1)} %collective-permute-done.4.refs_5_, ...), custom_call_target="tpu_custom_call" | custom-call | flops 1000 | bytes 1000 | tf_op jit(solution)/shard_map/pairs/pallas_call | solution.py:83
  63.9 0.0 collective-permute-done.1.refs_5_
  63.9 0.4 collective-permute-done.5.refs_7_
  64.3 2.4 %last.1 = bf16[5120,128]{1,0:T(8,128)(2,1)S(1)} custom-call(s32[7]{0:T(128)S(1)} %stack.31.refs_0_, f32[128]{0:T(128)S(1)} %copy-done.3, f32[512,1]{1,0:T(8,128)S(1)} %copy.9.refs_2_, f32[1,512]{1,0:T(1,128)S(1)} %bitcast.28, bf16[512,1280]{1,0:T(8,128)(2,1)S(1)} %bitcast.20, bf16[512,1280]{1,0:T(8,128)(2,1)S(1)} %collective-permute-done.1.refs_5_, ...), custom_call_target="tpu_custom_call" | custom-call | flops 1000 | bytes 1000 | tf_op jit(solution)/shard_map/last/pallas_call | solution.py:83
  66.7 0.0 copy-start.1
  66.7 39.6 %all_to_all.5 = bf16[128,40,128]{2,1,0:T(8,128)(2,1)S(1)} all-to-all(bf16[128,40,128]{2,1,0:T(8,128)(2,1)S(1)} %bitcast.21), channel_id=1, replica_groups=mesh['occ_0'=2,'occ_1'=4,'occ_2'=8,'occ_3'=2,'frag'=4] {'occ_0','occ_1',..., dimensions={0} | all-to-all | bytes 2621440 | tf_op jit(solution)/shard_map/all_to_all | solution.py:195
  106.3 0.0 copy-done.1
  106.3 2.7 %back.1 = bf16[10,128,1024]{2,1,0:T(8,128)(2,1)} custom-call(bf16[5120,128]{1,0:T(8,128)(2,1)S(1)} %bitcast.22, bf16[1024,512]{1,0:T(8,128)(2,1)S(1)} %copy-done.1), custom_call_target="tpu_custom_call" | custom-call | flops 1342177280 | bytes 3932160 | tf_op jit(solution)/shard_map/back/pallas_call | solution.py:151
Async XLA Ops:
  0.0 22.0 %copy-start.2 = (f32[512]{0:T(512)S(1)}, f32[512]{0:T(512)}, u32[]{:S(2)}) copy-start(f32[512]{0:T(512)} %param.6) | copy-start | bytes 6148
  0.0 23.9 %copy-start = (bf16[1,512,1280]{2,1,0:T(8,128)(2,1)S(1)}, bf16[1,512,1280]{2,1,0:T(8,128)(2,1)}, u32[]{:S(2)}) copy-start(bf16[1,512,1280]{2,1,0:T(8,128)(2,1)} %param.4) | copy-start | bytes 3932164
  0.0 23.9 %copy-start.3 = (f32[128]{0:T(128)S(1)}, f32[128]{0:T(128)}, u32[]{:S(2)}) copy-start(f32[128]{0:T(128)} %refs_1_.9) | copy-start | bytes 1540
  0.0 30.1 %collective-permute-start = (bf16[512,1280]{1,0:T(8,128)(2,1)}, bf16[512,1280]{1,0:T(8,128)(2,1)}, u32[]{:S(2)}, u32[]{:S(2)}) collective-permute-start(bf16[512,1280]{1,0:T(8,128)(2,1)} %bitcast.16), channel_id=1, source_target_pairs={{0,504},{4,12},{8,0},{12,20},{16,8},{20,28},{24,16},{28,36},{32,24... | collective-permute-start | bytes 3932168 | tf_op jit(solution)/shard_map/ppermute | solution.py:23
  7.2 15.1 %collective-permute-start.2 = (bf16[256,1280]{1,0:T(8,128)(2,1)}, bf16[256,1280]{1,0:T(8,128)(2,1)S(1)}, u32[]{:S(2)}, u32[]{:S(2)}) collective-permute-start(bf16[256,1280]{1,0:T(8,128)(2,1)} %get-tuple-element.16), channel_id=1, source_target_pairs={{0,4},{4,0},{8,12},{12,8},{16,20},{20,16},{24,28},{28,24},{32,36},... | collective-permute-start | bytes 1966088 | tf_op jit(solution)/shard_map/ppermute | solution.py:23
  19.9 4.0 %collective-permute-start.3 = (bf16[256,1280]{1,0:T(8,128)(2,1)S(1)}, bf16[256,1280]{1,0:T(8,128)(2,1)S(1)}, u32[]{:S(2)}, u32[]{:S(2)}) collective-permute-start(bf16[256,1280]{1,0:T(8,128)(2,1)S(1)} %get-tuple-element.15), channel_id=1, source_target_pairs={{0,4},{4,0},{8,12},{12,8},{16,20},{20,16},{24,28},{28,24},{32,36},... | collective-permute-start | bytes 1966088 | tf_op jit(solution)/shard_map/ppermute | solution.py:23
  26.2 27.8 %collective-permute-start.4 = (bf16[512,1280]{1,0:T(8,128)(2,1)S(1)}, bf16[512,1280]{1,0:T(8,128)(2,1)S(1)}, u32[]{:S(2)}, u32[]{:S(2)}) collective-permute-start(bf16[512,1280]{1,0:T(8,128)(2,1)S(1)} %get-tuple-element.10), channel_id=1, source_target_pairs={{0,8},{4,508},{8,16},{12,4},{16,24},{20,12},{24,32},{28,20},{32,40... | collective-permute-start | bytes 3932168 | tf_op jit(solution)/shard_map/ppermute | solution.py:23
  30.2 33.7 %collective-permute-start.1 = (bf16[512,1280]{1,0:T(8,128)(2,1)}, bf16[512,1280]{1,0:T(8,128)(2,1)S(1)}, u32[]{:S(2)}, u32[]{:S(2)}) collective-permute-start(bf16[512,1280]{1,0:T(8,128)(2,1)} %collective-permute-done.refs_6_), channel_id=1, source_target_pairs={{0,508},{4,8},{8,4},{12,16},{16,12},{20,24},{24,20},{28,32},{32,28... | collective-permute-start | bytes 3932168 | tf_op jit(solution)/shard_map/ppermute | solution.py:23
  56.2 8.2 %collective-permute-start.5 = (bf16[1280,512]{1,0:T(8,128)(2,1)S(1)}, bf16[1280,512]{1,0:T(8,128)(2,1)S(1)}, u32[]{:S(2)}, u32[]{:S(2)}) collective-permute-start(bf16[1280,512]{1,0:T(8,128)(2,1)S(1)} %pairs.5), channel_id=1, source_target_pairs={{0,4},{4,0},{8,12},{12,8},{16,20},{20,16},{24,28},{28,24},{32,36},... | collective-permute-start | bytes 3932168 | tf_op jit(solution)/shard_map/ppermute | solution.py:23
  66.7 39.6 %copy-start.1 = (bf16[1024,512]{1,0:T(8,128)(2,1)S(1)}, bf16[1024,512]{1,0:T(8,128)(2,1)}, u32[]{:S(2)}) copy-start(bf16[1024,512]{1,0:T(8,128)(2,1)} %coeffs.1) | copy-start | bytes 3145732

commit v4 on v3

--- a/solution.py
+++ b/solution.py
@@ -40,37 +40,63 @@
         )
 
 
-def pairs_kernel(pairs, blocks, carried, *refs):
+def pairs_kernel(pairs, blocks, carried, pieces, *refs):
     levels, refs = refs[:4], refs[4:]
     held, refs = refs[:blocks], refs[blocks:]
     totals, outs = refs[:carried], refs[carried:]
     for k, (steps, left, right) in enumerate(pairs):
         amps = amplitudes(steps, levels, held[left], held[right])
-        for part, value in pair_terms(amps, held[right]):
+        for n, (part, value) in enumerate(pair_terms(amps, held[right])):
             if k < carried:
                 value = value + totals[k][part, :]
-            outs[k][part, :] = value.astype(outs[k].dtype)
+            if pieces:
+                outs[n][...] = value.astype(outs[n].dtype)
+            else:
+                outs[k][part, :] = value
 
 
 def first_kernel(steps, *refs):
     levels = refs[:4]
-    mine, upper, lower, total, again, other = refs[4:]
+    mine, upper, lower, total, other = refs[4:]
     half = upper.shape[0]
     other[:half, :] = upper[...]
     other[half:, :] = lower[...]
-    again[...] = mine[...]
     amps = amplitudes(steps, levels, mine, other)
     for part, value in pair_terms(amps, other):
         total[part, :] = value
 
 
+def split_kernel(mine, upper, lower, again):
+    half = upper.shape[0]
+    upper[...] = mine[:half, :]
+    lower[...] = mine[half:, :]
+    again[...] = mine[...]
+
+
+def split(mine):
+    rows, aux = mine.shape
+    vmem = pl.BlockSpec(memory_space=pltpu.VMEM)
+    return pl.pallas_call(
+        split_kernel,
+        out_shape=[
+            jax.ShapeDtypeStruct((height, aux), mine.dtype)
+            for height in (rows // 2, rows // 2, rows)
+        ],
+        in_specs=[vmem],
+        out_specs=[vmem] * 3,
+        compiler_params=pltpu.CompilerParams(vmem_limit_bytes=VMEM_LIMIT),
+        cost_estimate=pl.CostEstimate(flops=1000, bytes_accessed=1000, transcendentals=0),
+        name="split",
+    )(mine)
+
+
 def last_kernel(steps, *refs):
     levels = refs[:4]
-    mine, other, total, arrived, out, wide = refs[4:]
+    mine, other, total, *arrived, out, wide = refs[4:]
     cols = mine.shape[0] // LANES
     amps = amplitudes(steps, levels, mine, other)
-    for part, value in pair_terms(amps, other):
-        value = value + total[part, :] + arrived[part, :].astype(jnp.float32)
+    for piece, (part, value) in zip(arrived, pair_terms(amps, other)):
+        value = value + total[part, :] + piece[...].astype(jnp.float32)
         for c in range(cols):
             rows = pl.ds(part.start * cols + c, part.size, stride=cols)
             wide[rows, :] = value[:, c * LANES : (c + 1) * LANES]
@@ -92,17 +118,18 @@
     )(*levels, *arrays)
 
 
-def pairs_sum(levels, blocks, pairs, totals, dtypes):
-    shape = blocks[0].shape[::-1]
-    kernel = functools.partial(pairs_kernel, pairs, len(blocks), len(totals))
-    outs = [(shape, dtype) for dtype in dtypes]
+def pairs_sum(levels, blocks, pairs, totals, pieces=0):
+    virtuals, aux = blocks[0].shape
+    kernel = functools.partial(pairs_kernel, pairs, len(blocks), len(totals), pieces)
+    outs = [((aux, virtuals), jnp.float32)] * len(pairs)
+    if pieces:
+        outs = [((aux // pieces, virtuals), jnp.bfloat16)] * pieces
     flops = 10**10 if len(pairs) > 1 else 1000
     return local_call(kernel, levels, [*blocks, *totals], outs, name="pairs", flops=flops)
 
 
 def first_pair(levels, steps, mine, upper, lower):
-    block = (mine.shape, mine.dtype)
-    outs = [(mine.shape[::-1], jnp.float32), block, block]
+    outs = [(mine.shape[::-1], jnp.float32), (mine.shape, mine.dtype)]
     kernel = functools.partial(first_kernel, steps)
     return local_call(kernel, levels, [mine, upper, lower], outs, name="first")
 
@@ -113,7 +140,7 @@
     (gamma,) = local_call(
         kernel,
         levels,
-        [mine, other, total, arrived],
+        [mine, other, total, *arrived],
         [(shape, jnp.bfloat16)],
         [pltpu.VMEM(shape, jnp.float32)],
         name="last",
@@ -176,21 +203,19 @@
     sign = 1 - 2 * (index % 2)
     places = jnp.stack([(index + sign * k) % count for k in range(-3, 4)])
     levels = (places, occ_energy, vir_energy[:, None], vir_energy[None, :])
-    f32, bf16 = jnp.float32, jnp.bfloat16
-
-    half = mine.shape[0] // 2
+
     plus2 = mirrored(mine, count, -2)
-    upper = mirrored(mine[:half], count, 1)
-    lower = mirrored(mine[half:], count, 1)
-    total, again, plus1 = first_pair(levels, (0, 1), mine, upper, lower)
+    upper, lower, again = split(mine)
     minus2 = mirrored(again, count, 2)
+    upper, lower = mirrored(upper, count, 1), mirrored(lower, count, 1)
+    total, plus1 = first_pair(levels, (0, 1), mine, upper, lower)
     minus3 = mirrored(plus2, count, -1)
     total, beside = pairs_sum(
-        levels, [mine, plus1, plus2], [((0, 2), 0, 2), ((1, 2), 1, 2)], [total], [f32, f32]
-    )
-    (beside,) = pairs_sum(levels, [plus1, minus2], [((1, -2), 0, 1)], [beside], [bf16])
-    (total,) = pairs_sum(levels, [mine, minus2], [((0, -2), 0, 1)], [total], [f32])
-    arrived = mirrored(beside, count, 1)
+        levels, [mine, plus1, plus2], [((0, 2), 0, 2), ((1, 2), 1, 2)], [total]
+    )
+    beside = pairs_sum(levels, [plus1, minus2], [((1, -2), 0, 1)], [beside], PARTS)
+    (total,) = pairs_sum(levels, [mine, minus2], [((0, -2), 0, 1)], [total])
+    arrived = [mirrored(piece, count, 1) for piece in beside]
     gamma = last_pair(levels, (0, -3), mine, minus3, total, arrived)
     slabs = lax.all_to_all(gamma.reshape(count, -1, LANES), OCC, 0, 0, tiled=True)
     return back_transform(slabs.reshape(-1, LANES), coeffs, count)

time: 109 us -> 108 us (level)
  waiting for transfers between devices: 21.4 us -> 16.1 us
  blocking collectives: 39.6 us -> 43 us
  Pallas kernels: 16 us -> 18.2 us
  starting transfers between devices: 29.2 us -> 28 us
    ppermute x6 -> x7, waiting for transfers between devices: 21.4 us -> 16.1 us  [mirrored(): return lax.ppermute(block, OCC, route)]
    all_to_all x1, blocking collectives: 39.6 us -> 43 us  [on_device(): lax.all_to_all(gamma.reshape(count, -1, LANES), OCC, 0, 0, tiled=True)]
    slice x1 -> x0, local copies, waits for them, and re-layouts: 2.21 us -> none  [on_device(): lower = mirrored(mine[half:], count, 1)]
    pallas_call x0 -> x1, Pallas kernels: none -> 1.66 us  [split(): pl.pallas_call(split_kernel, out_shape=[jax.ShapeDtypeStruct((height, aux...]
    unnamed x8 -> x10, local copies, waits for them, and re-layouts: 0.02 us -> 1.34 us
    ppermute x6 -> x7, starting transfers between devices: 29.2 us -> 28 us  [mirrored(): return lax.ppermute(block, OCC, route)]
  transfers between devices with their start and end apart: 6 -> 7, of which waited for: 4 -> 2; matrix products, arithmetic and copies ran while one was open for 2% -> 0% of each run, Pallas kernels for 10% -> 12%
where the time goes in v4:
time: 108 us; the launch traced here: 107 us
  blocking collectives  43 us (40%)
  starting transfers between devices  28 us (26%)
  Pallas kernels  18.2 us (17%)
  waiting for transfers between devices  16.1 us (15%)
  local copies, waits for them, and re-layouts  1.57 us (1%)
    all_to_all x1, blocking collectives, on_device(): lax.all_to_all(gamma.reshape(count, -1, LANES), OCC, 0, 0, tiled=True)  43 us
    ppermute x7, starting transfers between devices, mirrored(): return lax.ppermute(block, OCC, route)  28 us
    ppermute x7, waiting for transfers between devices, mirrored(): return lax.ppermute(block, OCC, route)  16.1 us
    pallas_call x5, Pallas kernels, local_call(): pl.pallas_call(kernel, out_shape=[jax.ShapeDtypeStruct(shape, dtype) for...  13.9 us
    pallas_call x1, Pallas kernels, back_transform(): pl.pallas_call(functools.partial(back_kernel, chunk), out_shape=jax.Shape...  2.65 us
  transfers between devices with their start and end apart: 7, of which 2 were waited for; matrix products, arithmetic and copies ran while one was open for 0% of the time, Pallas kernels for 12%

profile of v4, /device:TPU:1, one launch (start us, length us, event | category | flops | bytes accessed | tf_op | source)
XLA Modules:
  0.0 107.2 jit_solution(17466955760852166884)
XLA Ops:
  0.0 0.0 copy-start.4
  0.0 5.0 %collective-permute-start = (bf16[512,1280]{1,0:T(8,128)(2,1)}, bf16[512,1280]{1,0:T(8,128)(2,1)}, u32[]{:S(2)}, u32[]{:S(2)}) collective-permute-start(bf16[512,1280]{1,0:T(8,128)(2,1)} %bitcast.12), channel_id=1, source_target_pairs={{0,504},{4,12},{8,0},{12,20},{16,8},{20,28},{24,16},{28,36},{32,24... | collective-permute-start | bytes 3932168 | tf_op jit(solution)/shard_map/ppermute | solution.py:23
  5.0 0.0 copy-start
  5.0 1.3 %copy-done = bf16[1,512,1280]{2,1,0:T(8,128)(2,1)S(1)} copy-done((bf16[1,512,1280]{2,1,0:T(8,128)(2,1)S(1)}, bf16[1,512,1280]{2,1,0:T(8,128)(2,1)}, u32[]{:S(2)}) %copy-start) | copy-done | bytes 1310744
  6.3 0.0 copy-start.3
  6.3 0.0 copy-start.1
  6.3 1.7 %split.1 = (bf16[256,1280]{1,0:T(8,128)(2,1)}, bf16[256,1280]{1,0:T(8,128)(2,1)}, bf16[512,1280]{1,0:T(8,128)(2,1)}) custom-call(bf16[512,1280]{1,0:T(8,128)(2,1)S(1)} %bitcast.13), custom_call_target="tpu_custom_call" | custom-call | flops 1000 | bytes 1000 | tf_op jit(solution)/shard_map/split/pallas_call | solution.py:79
  8.0 12.7 %collective-permute-start.3 = (bf16[256,1280]{1,0:T(8,128)(2,1)}, bf16[256,1280]{1,0:T(8,128)(2,1)S(1)}, u32[]{:S(2)}, u32[]{:S(2)}) collective-permute-start(bf16[256,1280]{1,0:T(8,128)(2,1)} %get-tuple-element.15), channel_id=1, source_target_pairs={{0,4},{4,0},{8,12},{12,8},{16,20},{20,16},{24,28},{28,24},{32,36},... | collective-permute-start | bytes 1966088 | tf_op jit(solution)/shard_map/ppermute | solution.py:23
  20.7 1.9 %collective-permute-start.4 = (bf16[256,1280]{1,0:T(8,128)(2,1)}, bf16[256,1280]{1,0:T(8,128)(2,1)}, u32[]{:S(2)}, u32[]{:S(2)}) collective-permute-start(bf16[256,1280]{1,0:T(8,128)(2,1)} %get-tuple-element.16), channel_id=1, source_target_pairs={{0,4},{4,0},{8,12},{12,8},{16,20},{20,16},{24,28},{28,24},{32,36},... | collective-permute-start | bytes 1966088 | tf_op jit(solution)/shard_map/ppermute | solution.py:23
  22.6 2.2 %collective-permute-start.2 = (bf16[512,1280]{1,0:T(8,128)(2,1)}, bf16[512,1280]{1,0:T(8,128)(2,1)S(1)}, u32[]{:S(2)}, u32[]{:S(2)}) collective-permute-start(bf16[512,1280]{1,0:T(8,128)(2,1)} %get-tuple-element.14), channel_id=1, source_target_pairs={{0,8},{4,508},{8,16},{12,4},{16,24},{20,12},{24,32},{28,20},{32,40... | collective-permute-start | bytes 3932168 | tf_op jit(solution)/shard_map/ppermute | solution.py:23
  24.9 0.0 copy-done.3
  24.9 0.1 copy.9.refs_2_
  25.1 0.1 stack.31.refs_0_
  25.2 0.0 collective-permute-done.3.refs_5_
  25.2 0.0 collective-permute-done.4.refs_6_
  25.2 0.0 copy-done.4
  25.2 0.0 copy-done.1
  25.3 2.7 %first.1 = (f32[1280,512]{1,0:T(8,128)S(1)}, bf16[512,1280]{1,0:T(8,128)(2,1)S(1)}) custom-call(s32[7]{0:T(128)S(1)} %stack.31.refs_0_, f32[128]{0:T(128)S(1)} %copy-done.4, f32[512,1]{1,0:T(8,128)S(1)} %copy.9.refs_2_, f32[1,512]{1,0:T(1,128)S(1)} %bitcast.21, bf16[512,1280]{1,0:T(8,128)(2,1)S(1)} %bitcast.14, ...), custom_call_target="tpu_custom_call" | custom-call | flops 1000 | bytes 1000 | tf_op jit(solution)/shard_map/first/pallas_call | solution.py:109
  28.0 2.1 %collective-permute-done.refs_6_ = bf16[512,1280]{1,0:T(8,128)(2,1)} collective-permute-done((bf16[512,1280]{1,0:T(8,128)(2,1)}, bf16[512,1280]{1,0:T(8,128)(2,1)}, u32[]{:S(2)}, u32[]{:S(2)}) %collective-permute-start) | collective-permute-done | bytes 1310752 | tf_op jit(solution)/shard_map/ppermute | solution.py:23
  30.1 1.9 %collective-permute-start.1 = (bf16[512,1280]{1,0:T(8,128)(2,1)}, bf16[512,1280]{1,0:T(8,128)(2,1)S(1)}, u32[]{:S(2)}, u32[]{:S(2)}) collective-permute-start(bf16[512,1280]{1,0:T(8,128)(2,1)} %collective-permute-done.refs_6_), channel_id=1, source_target_pairs={{0,508},{4,8},{8,4},{12,16},{16,12},{20,24},{24,20},{28,32},{32,28... | collective-permute-start | bytes 3932168 | tf_op jit(solution)/shard_map/ppermute | solution.py:23
  32.1 4.4 %pairs.3 = (f32[1280,512]{1,0:T(8,128)S(1)}, f32[1280,512]{1,0:T(8,128)S(1)}) custom-call(s32[7]{0:T(128)S(1)} %stack.31.refs_0_, f32[128]{0:T(128)S(1)} %copy-done.4, f32[512,1]{1,0:T(8,128)S(1)} %copy.9.refs_2_, f32[1,512]{1,0:T(1,128)S(1)} %bitcast.22, bf16[512,1280]{1,0:T(8,128)(2,1)S(1)} %bitcast.15, ...), custom_call_target="tpu_custom_call" | custom-call | flops 10000000000 | bytes 1000 | tf_op jit(solution)/shard_map/pairs/pallas_call | solution.py:109
  36.5 13.9 %collective-permute-done.2.refs_5_ = bf16[512,1280]{1,0:T(8,128)(2,1)S(1)} collective-permute-done((bf16[512,1280]{1,0:T(8,128)(2,1)}, bf16[512,1280]{1,0:T(8,128)(2,1)S(1)}, u32[]{:S(2)}, u32[]{:S(2)}) %collective-permute-start.2) | collective-permute-done | bytes 1310752 | tf_op jit(solution)/shard_map/ppermute | solution.py:23
  50.4 2.2 %pairs.5 = (bf16[640,512]{1,0:T(8,128)(2,1)S(1)}, bf16[640,512]{1,0:T(8,128)(2,1)S(1)}) custom-call(s32[7]{0:T(128)S(1)} %stack.31.refs_0_, f32[128]{0:T(128)S(1)} %copy-done.4, f32[512,1]{1,0:T(8,128)S(1)} %copy.9.refs_2_, f32[1,512]{1,0:T(1,128)S(1)} %bitcast.23, bf16[512,1280]{1,0:T(8,128)(2,1)S(1)} %get-tuple-element.17.refs_5_.refs_4_, ...), custom_call_target="tpu_custom_call" | custom-call | flops 1000 | bytes 1000 | tf_op jit(solution)/shard_map/pairs/pallas_call | solution.py:109
  52.6 1.9 %collective-permute-start.5 = (bf16[640,512]{1,0:T(8,128)(2,1)S(1)}, bf16[640,512]{1,0:T(8,128)(2,1)S(1)}, u32[]{:S(2)}, u32[]{:S(2)}) collective-permute-start(bf16[640,512]{1,0:T(8,128)(2,1)S(1)} %get-tuple-element.21), channel_id=1, source_target_pairs={{0,4},{4,0},{8,12},{12,8},{16,20},{20,16},{24,28},{28,24},{32,36},... | collective-permute-start | bytes 1966088 | tf_op jit(solution)/shard_map/ppermute | solution.py:23
  54.5 2.4 %collective-permute-start.6 = (bf16[640,512]{1,0:T(8,128)(2,1)S(1)}, bf16[640,512]{1,0:T(8,128)(2,1)S(1)}, u32[]{:S(2)}, u32[]{:S(2)}) collective-permute-start(bf16[640,512]{1,0:T(8,128)(2,1)S(1)} %get-tuple-element.22), channel_id=1, source_target_pairs={{0,4},{4,0},{8,12},{12,8},{16,20},{20,16},{24,28},{28,24},{32,36},... | collective-permute-start | bytes 1966088 | tf_op jit(solution)/shard_map/ppermute | solution.py:23
  56.9 2.2 %pairs.4.refs_6_ = f32[1280,512]{1,0:T(8,128)S(1)} custom-call(s32[7]{0:T(128)S(1)} %stack.31.refs_0_, f32[128]{0:T(128)S(1)} %copy-done.4, f32[512,1]{1,0:T(8,128)S(1)} %copy.9.refs_2_, f32[1,512]{1,0:T(1,128)S(1)} %bitcast.24, bf16[512,1280]{1,0:T(8,128)(2,1)S(1)} %bitcast.16, bf16[512,1280]{1,0:T(8,128)(2,1)S(1)} %collective-permute-done.2.refs_5_, ...), custom_call_target="tpu_custom_call" | custom-call | flops 1000 | bytes 1000 | tf_op jit(solution)/shard_map/pairs/pallas_call | solution.py:109
  59.1 0.0 collective-permute-done.5.refs_7_
  59.1 0.0 collective-permute-done.6.refs_8_
  59.2 0.0 collective-permute-done.1.refs_5_
  59.2 2.4 %last.1 = bf16[5120,128]{1,0:T(8,128)(2,1)S(1)} custom-call(s32[7]{0:T(128)S(1)} %stack.31.refs_0_, f32[128]{0:T(128)S(1)} %copy-done.4, f32[512,1]{1,0:T(8,128)S(1)} %copy.9.refs_2_, f32[1,512]{1,0:T(1,128)S(1)} %bitcast.25, bf16[512,1280]{1,0:T(8,128)(2,1)S(1)} %bitcast.17, bf16[512,1280]{1,0:T(8,128)(2,1)S(1)} %collective-permute-done.1.refs_5_, ...), custom_call_target="tpu_custom_call" | custom-call | flops 1000 | bytes 1000 | tf_op jit(solution)/shard_map/last/pallas_call | solution.py:109
  61.5 0.0 copy-start.2
  61.5 43.0 %all_to_all.5 = bf16[128,40,128]{2,1,0:T(8,128)(2,1)S(1)} all-to-all(bf16[128,40,128]{2,1,0:T(8,128)(2,1)S(1)} %bitcast.18), channel_id=1, replica_groups=mesh['occ_0'=2,'occ_1'=4,'occ_2'=8,'occ_3'=2,'frag'=4] {'occ_0','occ_1',..., dimensions={0} | all-to-all | bytes 2621440 | tf_op jit(solution)/shard_map/all_to_all | solution.py:220
  104.6 0.0 copy-done.2
  104.6 2.7 %back.1 = bf16[10,128,1024]{2,1,0:T(8,128)(2,1)} custom-call(bf16[5120,128]{1,0:T(8,128)(2,1)S(1)} %bitcast.19, bf16[1024,512]{1,0:T(8,128)(2,1)S(1)} %copy-done.2), custom_call_target="tpu_custom_call" | custom-call | flops 1342177280 | bytes 3932160 | tf_op jit(solution)/shard_map/back/pallas_call | solution.py:178
Async XLA Ops:
  0.0 25.2 %copy-start.4 = (f32[128]{0:T(128)S(1)}, f32[128]{0:T(128)}, u32[]{:S(2)}) copy-start(f32[128]{0:T(128)} %refs_1_.9) | copy-start | bytes 1540
  0.0 30.1 %collective-permute-start = (bf16[512,1280]{1,0:T(8,128)(2,1)}, bf16[512,1280]{1,0:T(8,128)(2,1)}, u32[]{:S(2)}, u32[]{:S(2)}) collective-permute-start(bf16[512,1280]{1,0:T(8,128)(2,1)} %bitcast.12), channel_id=1, source_target_pairs={{0,504},{4,12},{8,0},{12,20},{16,8},{20,28},{24,16},{28,36},{32,24... | collective-permute-start | bytes 3932168 | tf_op jit(solution)/shard_map/ppermute | solution.py:23
  5.0 1.3 %copy-start = (bf16[1,512,1280]{2,1,0:T(8,128)(2,1)S(1)}, bf16[1,512,1280]{2,1,0:T(8,128)(2,1)}, u32[]{:S(2)}) copy-start(bf16[1,512,1280]{2,1,0:T(8,128)(2,1)} %param.4) | copy-start | bytes 3932164
  6.3 18.6 %copy-start.3 = (f32[512]{0:T(512)S(1)}, f32[512]{0:T(512)}, u32[]{:S(2)}) copy-start(f32[512]{0:T(512)} %param.6) | copy-start | bytes 6148
  6.3 19.0 %copy-start.1 = (bf16[1,512,1280]{2,1,0:T(8,128)(2,1)S(1)}, bf16[1,512,1280]{2,1,0:T(8,128)(2,1)}, u32[]{:S(2)}) copy-start(bf16[1,512,1280]{2,1,0:T(8,128)(2,1)} %param.4) | copy-start | bytes 3932164
  8.0 17.3 %collective-permute-start.3 = (bf16[256,1280]{1,0:T(8,128)(2,1)}, bf16[256,1280]{1,0:T(8,128)(2,1)S(1)}, u32[]{:S(2)}, u32[]{:S(2)}) collective-permute-start(bf16[256,1280]{1,0:T(8,128)(2,1)} %get-tuple-element.15), channel_id=1, source_target_pairs={{0,4},{4,0},{8,12},{12,8},{16,20},{20,16},{24,28},{28,24},{32,36},... | collective-permute-start | bytes 1966088 | tf_op jit(solution)/shard_map/ppermute | solution.py:23
  20.7 4.5 %collective-permute-start.4 = (bf16[256,1280]{1,0:T(8,128)(2,1)}, bf16[256,1280]{1,0:T(8,128)(2,1)}, u32[]{:S(2)}, u32[]{:S(2)}) collective-permute-start(bf16[256,1280]{1,0:T(8,128)(2,1)} %get-tuple-element.16), channel_id=1, source_target_pairs={{0,4},{4,0},{8,12},{12,8},{16,20},{20,16},{24,28},{28,24},{32,36},... | collective-permute-start | bytes 1966088 | tf_op jit(solution)/shard_map/ppermute | solution.py:23
  22.6 27.8 %collective-permute-start.2 = (bf16[512,1280]{1,0:T(8,128)(2,1)}, bf16[512,1280]{1,0:T(8,128)(2,1)S(1)}, u32[]{:S(2)}, u32[]{:S(2)}) collective-permute-start(bf16[512,1280]{1,0:T(8,128)(2,1)} %get-tuple-element.14), channel_id=1, source_target_pairs={{0,8},{4,508},{8,16},{12,4},{16,24},{20,12},{24,32},{28,20},{32,40... | collective-permute-start | bytes 3932168 | tf_op jit(solution)/shard_map/ppermute | solution.py:23
  30.1 29.0 %collective-permute-start.1 = (bf16[512,1280]{1,0:T(8,128)(2,1)}, bf16[512,1280]{1,0:T(8,128)(2,1)S(1)}, u32[]{:S(2)}, u32[]{:S(2)}) collective-permute-start(bf16[512,1280]{1,0:T(8,128)(2,1)} %collective-permute-done.refs_6_), channel_id=1, source_target_pairs={{0,508},{4,8},{8,4},{12,16},{16,12},{20,24},{24,20},{28,32},{32,28... | collective-permute-start | bytes 3932168 | tf_op jit(solution)/shard_map/ppermute | solution.py:23
  52.6 6.5 %collective-permute-start.5 = (bf16[640,512]{1,0:T(8,128)(2,1)S(1)}, bf16[640,512]{1,0:T(8,128)(2,1)S(1)}, u32[]{:S(2)}, u32[]{:S(2)}) collective-permute-start(bf16[640,512]{1,0:T(8,128)(2,1)S(1)} %get-tuple-element.21), channel_id=1, source_target_pairs={{0,4},{4,0},{8,12},{12,8},{16,20},{20,16},{24,28},{28,24},{32,36},... | collective-permute-start | bytes 1966088 | tf_op jit(solution)/shard_map/ppermute | solution.py:23
  54.5 4.6 %collective-permute-start.6 = (bf16[640,512]{1,0:T(8,128)(2,1)S(1)}, bf16[640,512]{1,0:T(8,128)(2,1)S(1)}, u32[]{:S(2)}, u32[]{:S(2)}) collective-permute-start(bf16[640,512]{1,0:T(8,128)(2,1)S(1)} %get-tuple-element.22), channel_id=1, source_target_pairs={{0,4},{4,0},{8,12},{12,8},{16,20},{20,16},{24,28},{28,24},{32,36},... | collective-permute-start | bytes 1966088 | tf_op jit(solution)/shard_map/ppermute | solution.py:23
  61.5 43.1 %copy-start.2 = (bf16[1024,512]{1,0:T(8,128)(2,1)S(1)}, bf16[1024,512]{1,0:T(8,128)(2,1)}, u32[]{:S(2)}) copy-start(bf16[1024,512]{1,0:T(8,128)(2,1)} %coeffs.1) | copy-start | bytes 3145732

commit v5 on v4

--- a/solution.py
+++ b/solution.py
@@ -40,19 +40,16 @@
         )
 
 
-def pairs_kernel(pairs, blocks, carried, pieces, *refs):
+def pairs_kernel(pairs, blocks, carried, *refs):
     levels, refs = refs[:4], refs[4:]
     held, refs = refs[:blocks], refs[blocks:]
     totals, outs = refs[:carried], refs[carried:]
     for k, (steps, left, right) in enumerate(pairs):
         amps = amplitudes(steps, levels, held[left], held[right])
-        for n, (part, value) in enumerate(pair_terms(amps, held[right])):
+        for part, value in pair_terms(amps, held[right]):
             if k < carried:
                 value = value + totals[k][part, :]
-            if pieces:
-                outs[n][...] = value.astype(outs[n].dtype)
-            else:
-                outs[k][part, :] = value
+            outs[k][part, :] = value.astype(outs[k].dtype)
 
 
 def first_kernel(steps, *refs):
@@ -90,13 +87,16 @@
     )(mine)
 
 
-def last_kernel(steps, *refs):
+def amps_kernel(steps, *refs):
     levels = refs[:4]
-    mine, other, total, *arrived, out, wide = refs[4:]
-    cols = mine.shape[0] // LANES
-    amps = amplitudes(steps, levels, mine, other)
-    for piece, (part, value) in zip(arrived, pair_terms(amps, other)):
-        value = value + total[part, :] + piece[...].astype(jnp.float32)
+    mine, other, out = refs[4:]
+    out[...] = amplitudes(steps, levels, mine, other)
+
+
+def last_kernel(amps, other, total, arrived, out, wide):
+    cols = other.shape[0] // LANES
+    for part, value in pair_terms(amps[...], other):
+        value = value + total[part, :] + arrived[part, :].astype(jnp.float32)
         for c in range(cols):
             rows = pl.ds(part.start * cols + c, part.size, stride=cols)
             wide[rows, :] = value[:, c * LANES : (c + 1) * LANES]
@@ -118,12 +118,10 @@
     )(*levels, *arrays)
 
 
-def pairs_sum(levels, blocks, pairs, totals, pieces=0):
-    virtuals, aux = blocks[0].shape
-    kernel = functools.partial(pairs_kernel, pairs, len(blocks), len(totals), pieces)
-    outs = [((aux, virtuals), jnp.float32)] * len(pairs)
-    if pieces:
-        outs = [((aux // pieces, virtuals), jnp.bfloat16)] * pieces
+def pairs_sum(levels, blocks, pairs, totals, dtypes):
+    shape = blocks[0].shape[::-1]
+    kernel = functools.partial(pairs_kernel, pairs, len(blocks), len(totals))
+    outs = [(shape, dtype) for dtype in dtypes]
     flops = 10**10 if len(pairs) > 1 else 1000
     return local_call(kernel, levels, [*blocks, *totals], outs, name="pairs", flops=flops)
 
@@ -135,17 +133,22 @@
 
 
 def last_pair(levels, steps, mine, other, total, arrived):
+    virtuals, aux = mine.shape
+    kernel = functools.partial(amps_kernel, steps)
+    outs = [((virtuals, virtuals), jnp.bfloat16)]
+    (amps,) = local_call(kernel, levels, [mine, other], outs, name="amps")
     shape = (mine.size // LANES, LANES)
-    kernel = functools.partial(last_kernel, steps)
-    (gamma,) = local_call(
-        kernel,
-        levels,
-        [mine, other, total, *arrived],
-        [(shape, jnp.bfloat16)],
-        [pltpu.VMEM(shape, jnp.float32)],
+    vmem = pl.BlockSpec(memory_space=pltpu.VMEM)
+    return pl.pallas_call(
+        last_kernel,
+        out_shape=jax.ShapeDtypeStruct(shape, jnp.bfloat16),
+        in_specs=[vmem] * 4,
+        out_specs=vmem,
+        scratch_shapes=[pltpu.VMEM(shape, jnp.float32)],
+        compiler_params=pltpu.CompilerParams(vmem_limit_bytes=VMEM_LIMIT),
+        cost_estimate=pl.CostEstimate(flops=1000, bytes_accessed=1000, transcendentals=0),
         name="last",
-    )
-    return gamma
+    )(amps, other, total, arrived)
 
 
 def back_kernel(chunk, slabs, coeffs, out, wide, flat, done, sems):
@@ -203,6 +206,7 @@
     sign = 1 - 2 * (index % 2)
     places = jnp.stack([(index + sign * k) % count for k in range(-3, 4)])
     levels = (places, occ_energy, vir_energy[:, None], vir_energy[None, :])
+    f32, bf16 = jnp.float32, jnp.bfloat16
 
     plus2 = mirrored(mine, count, -2)
     upper, lower, again = split(mine)
@@ -211,11 +215,11 @@
     total, plus1 = first_pair(levels, (0, 1), mine, upper, lower)
     minus3 = mirrored(plus2, count, -1)
     total, beside = pairs_sum(
-        levels, [mine, plus1, plus2], [((0, 2), 0, 2), ((1, 2), 1, 2)], [total]
+        levels, [mine, plus1, plus2], [((0, 2), 0, 2), ((1, 2), 1, 2)], [total], [f32, f32]
     )
-    beside = pairs_sum(levels, [plus1, minus2], [((1, -2), 0, 1)], [beside], PARTS)
-    (total,) = pairs_sum(levels, [mine, minus2], [((0, -2), 0, 1)], [total])
-    arrived = [mirrored(piece, count, 1) for piece in beside]
+    (beside,) = pairs_sum(levels, [plus1, minus2], [((1, -2), 0, 1)], [beside], [bf16])
+    (total,) = pairs_sum(levels, [mine, minus2], [((0, -2), 0, 1)], [total], [f32])
+    arrived = mirrored(beside, count, 1)
     gamma = last_pair(levels, (0, -3), mine, minus3, total, arrived)
     slabs = lax.all_to_all(gamma.reshape(count, -1, LANES), OCC, 0, 0, tiled=True)
     return back_transform(slabs.reshape(-1, LANES), coeffs, count)

time: 108 us -> 108 us (level)
  starting transfers between devices: 28 us -> 25.6 us
  blocking collectives: 43 us -> 45.2 us
    ppermute x7 -> x6, starting transfers between devices: 28 us -> 25.6 us  [mirrored(): return lax.ppermute(block, OCC, route)]
    all_to_all x1, blocking collectives: 43 us -> 45.2 us  [on_device(): lax.all_to_all(gamma.reshape(count, -1, LANES), OCC, 0, 0, tiled=True)]
    ppermute x7 -> x6, waiting for transfers between devices: 16.1 us -> 16.1 us  [mirrored(): return lax.ppermute(block, OCC, route)]
  transfers between devices with their start and end apart: 7 -> 6, of which waited for: 2 -> 2; matrix products, arithmetic and copies ran while one was open for 0% -> 0% of each run, Pallas kernels for 12% -> 14%
where the time goes in v5:
time: 108 us; the launch traced here: 107 us
  blocking collectives  45.2 us (42%)
  starting transfers between devices  25.6 us (24%)
  Pallas kernels  18.3 us (17%)
  waiting for transfers between devices  16.1 us (15%)
  local copies, waits for them, and re-layouts  1.57 us (1%)
    all_to_all x1, blocking collectives, on_device(): lax.all_to_all(gamma.reshape(count, -1, LANES), OCC, 0, 0, tiled=True)  45.2 us
    ppermute x6, starting transfers between devices, mirrored(): return lax.ppermute(block, OCC, route)  25.6 us
    ppermute x6, waiting for transfers between devices, mirrored(): return lax.ppermute(block, OCC, route)  16.1 us
    pallas_call x5, Pallas kernels, local_call(): pl.pallas_call(kernel, out_shape=[jax.ShapeDtypeStruct(shape, dtype) for...  13 us
    pallas_call x1, Pallas kernels, back_transform(): pl.pallas_call(functools.partial(back_kernel, chunk), out_shape=jax.Shape...  2.66 us
  transfers between devices with their start and end apart: 6, of which 2 were waited for; matrix products, arithmetic and copies ran while one was open for 0% of the time, Pallas kernels for 14%

profile of v5, /device:TPU:1, one launch (start us, length us, event | category | flops | bytes accessed | tf_op | source)
XLA Modules:
  0.0 107.1 jit_solution(15097590269137478157)
XLA Ops:
  0.0 0.0 copy-start.4
  0.0 5.0 %collective-permute-start = (bf16[512,1280]{1,0:T(8,128)(2,1)}, bf16[512,1280]{1,0:T(8,128)(2,1)}, u32[]{:S(2)}, u32[]{:S(2)}) collective-permute-start(bf16[512,1280]{1,0:T(8,128)(2,1)} %bitcast.12), channel_id=1, source_target_pairs={{0,504},{4,12},{8,0},{12,20},{16,8},{20,28},{24,16},{28,36},{32,24... | collective-permute-start | bytes 3932168 | tf_op jit(solution)/shard_map/ppermute | solution.py:23
  5.0 0.0 copy-start
  5.0 1.3 %copy-done = bf16[1,512,1280]{2,1,0:T(8,128)(2,1)S(1)} copy-done((bf16[1,512,1280]{2,1,0:T(8,128)(2,1)S(1)}, bf16[1,512,1280]{2,1,0:T(8,128)(2,1)}, u32[]{:S(2)}) %copy-start) | copy-done | bytes 1310744
  6.3 0.0 copy-start.3
  6.3 0.0 copy-start.1
  6.3 1.7 %split.1 = (bf16[256,1280]{1,0:T(8,128)(2,1)}, bf16[256,1280]{1,0:T(8,128)(2,1)}, bf16[512,1280]{1,0:T(8,128)(2,1)}) custom-call(bf16[512,1280]{1,0:T(8,128)(2,1)S(1)} %bitcast.13), custom_call_target="tpu_custom_call" | custom-call | flops 1000 | bytes 1000 | tf_op jit(solution)/shard_map/split/pallas_call | solution.py:76
  8.0 12.7 %collective-permute-start.3 = (bf16[256,1280]{1,0:T(8,128)(2,1)}, bf16[256,1280]{1,0:T(8,128)(2,1)S(1)}, u32[]{:S(2)}, u32[]{:S(2)}) collective-permute-start(bf16[256,1280]{1,0:T(8,128)(2,1)} %get-tuple-element.13), channel_id=1, source_target_pairs={{0,4},{4,0},{8,12},{12,8},{16,20},{20,16},{24,28},{28,24},{32,36},... | collective-permute-start | bytes 1966088 | tf_op jit(solution)/shard_map/ppermute | solution.py:23
  20.7 1.9 %collective-permute-start.4 = (bf16[256,1280]{1,0:T(8,128)(2,1)}, bf16[256,1280]{1,0:T(8,128)(2,1)}, u32[]{:S(2)}, u32[]{:S(2)}) collective-permute-start(bf16[256,1280]{1,0:T(8,128)(2,1)} %get-tuple-element.14), channel_id=1, source_target_pairs={{0,4},{4,0},{8,12},{12,8},{16,20},{20,16},{24,28},{28,24},{32,36},... | collective-permute-start | bytes 1966088 | tf_op jit(solution)/shard_map/ppermute | solution.py:23
  22.6 2.2 %collective-permute-start.2 = (bf16[512,1280]{1,0:T(8,128)(2,1)}, bf16[512,1280]{1,0:T(8,128)(2,1)S(1)}, u32[]{:S(2)}, u32[]{:S(2)}) collective-permute-start(bf16[512,1280]{1,0:T(8,128)(2,1)} %get-tuple-element.12), channel_id=1, source_target_pairs={{0,8},{4,508},{8,16},{12,4},{16,24},{20,12},{24,32},{28,20},{32,40... | collective-permute-start | bytes 3932168 | tf_op jit(solution)/shard_map/ppermute | solution.py:23
  24.9 0.0 copy-done.3
  24.9 0.1 copy.5.refs_2_
  25.1 0.1 stack.31.refs_0_
  25.2 0.0 collective-permute-done.3.refs_5_
  25.2 0.0 collective-permute-done.4.refs_6_
  25.2 0.0 copy-done.4
  25.2 0.0 copy-done.1
  25.3 2.7 %first.1 = (f32[1280,512]{1,0:T(8,128)S(1)}, bf16[512,1280]{1,0:T(8,128)(2,1)S(1)}) custom-call(s32[7]{0:T(128)S(1)} %stack.31.refs_0_, f32[128]{0:T(128)S(1)} %copy-done.4, f32[512,1]{1,0:T(8,128)S(1)} %copy.5.refs_2_, f32[1,512]{1,0:T(1,128)S(1)} %bitcast.21, bf16[512,1280]{1,0:T(8,128)(2,1)S(1)} %bitcast.14, ...), custom_call_target="tpu_custom_call" | custom-call | flops 1000 | bytes 1000 | tf_op jit(solution)/shard_map/first/pallas_call | solution.py:109
  28.0 2.1 %collective-permute-done.refs_6_ = bf16[512,1280]{1,0:T(8,128)(2,1)} collective-permute-done((bf16[512,1280]{1,0:T(8,128)(2,1)}, bf16[512,1280]{1,0:T(8,128)(2,1)}, u32[]{:S(2)}, u32[]{:S(2)}) %collective-permute-start) | collective-permute-done | bytes 1310752 | tf_op jit(solution)/shard_map/ppermute | solution.py:23
  30.1 1.9 %collective-permute-start.1 = (bf16[512,1280]{1,0:T(8,128)(2,1)}, bf16[512,1280]{1,0:T(8,128)(2,1)S(1)}, u32[]{:S(2)}, u32[]{:S(2)}) collective-permute-start(bf16[512,1280]{1,0:T(8,128)(2,1)} %collective-permute-done.refs_6_), channel_id=1, source_target_pairs={{0,508},{4,8},{8,4},{12,16},{16,12},{20,24},{24,20},{28,32},{32,28... | collective-permute-start | bytes 3932168 | tf_op jit(solution)/shard_map/ppermute | solution.py:23
  32.1 4.4 %pairs.3 = (f32[1280,512]{1,0:T(8,128)S(1)}, f32[1280,512]{1,0:T(8,128)S(1)}) custom-call(s32[7]{0:T(128)S(1)} %stack.31.refs_0_, f32[128]{0:T(128)S(1)} %copy-done.4, f32[512,1]{1,0:T(8,128)S(1)} %copy.5.refs_2_, f32[1,512]{1,0:T(1,128)S(1)} %bitcast.22, bf16[512,1280]{1,0:T(8,128)(2,1)S(1)} %bitcast.15, ...), custom_call_target="tpu_custom_call" | custom-call | flops 10000000000 | bytes 1000 | tf_op jit(solution)/shard_map/pairs/pallas_call | solution.py:109
  36.5 13.9 %collective-permute-done.2.refs_5_ = bf16[512,1280]{1,0:T(8,128)(2,1)S(1)} collective-permute-done((bf16[512,1280]{1,0:T(8,128)(2,1)}, bf16[512,1280]{1,0:T(8,128)(2,1)S(1)}, u32[]{:S(2)}, u32[]{:S(2)}) %collective-permute-start.2) | collective-permute-done | bytes 1310752 | tf_op jit(solution)/shard_map/ppermute | solution.py:23
  50.4 2.2 %pairs.5 = bf16[1280,512]{1,0:T(8,128)(2,1)S(1)} custom-call(s32[7]{0:T(128)S(1)} %stack.31.refs_0_, f32[128]{0:T(128)S(1)} %copy-done.4, f32[512,1]{1,0:T(8,128)S(1)} %copy.5.refs_2_, f32[1,512]{1,0:T(1,128)S(1)} %bitcast.23, bf16[512,1280]{1,0:T(8,128)(2,1)S(1)} %get-tuple-element.15.refs_5_.refs_4_, bf16[512,1280]{1,0:T(8,128)(2,1)S(1)} %collective-permute-done.2.refs_5_, ...), custom_call_target="tpu_custom_call" | custom-call | flops 1000 | bytes 1000 | tf_op jit(solution)/shard_map/pairs/pallas_call | solution.py:109
  52.6 1.9 %collective-permute-start.5 = (bf16[1280,512]{1,0:T(8,128)(2,1)S(1)}, bf16[1280,512]{1,0:T(8,128)(2,1)S(1)}, u32[]{:S(2)}, u32[]{:S(2)}) collective-permute-start(bf16[1280,512]{1,0:T(8,128)(2,1)S(1)} %pairs.5), channel_id=1, source_target_pairs={{0,4},{4,0},{8,12},{12,8},{16,20},{20,16},{24,28},{28,24},{32,36},... | collective-permute-start | bytes 3932168 | tf_op jit(solution)/shard_map/ppermute | solution.py:23
  54.5 2.2 %pairs.4.total = f32[1280,512]{1,0:T(8,128)S(1)} custom-call(s32[7]{0:T(128)S(1)} %stack.31.refs_0_, f32[128]{0:T(128)S(1)} %copy-done.4, f32[512,1]{1,0:T(8,128)S(1)} %copy.5.refs_2_, f32[1,512]{1,0:T(1,128)S(1)} %bitcast.24, bf16[512,1280]{1,0:T(8,128)(2,1)S(1)} %bitcast.16, bf16[512,1280]{1,0:T(8,128)(2,1)S(1)} %collective-permute-done.2.refs_5_, ...), custom_call_target="tpu_custom_call" | custom-call | flops 1000 | bytes 1000 | tf_op jit(solution)/shard_map/pairs/pallas_call | solution.py:109
  56.7 0.0 collective-permute-done.1.refs_5_.other
  56.7 1.4 %amps.1 = bf16[512,512]{1,0:T(8,128)(2,1)S(1)} custom-call(s32[7]{0:T(128)S(1)} %stack.31.refs_0_, f32[128]{0:T(128)S(1)} %copy-done.4, f32[512,1]{1,0:T(8,128)S(1)} %copy.5.refs_2_, f32[1,512]{1,0:T(1,128)S(1)} %bitcast.25, bf16[512,1280]{1,0:T(8,128)(2,1)S(1)} %bitcast.17, bf16[512,1280]{1,0:T(8,128)(2,1)S(1)} %collective-permute-done.1.refs_5_.other), custom_call_target="tpu_custom_call" | custom-call | flops 1000 | bytes 1000 | tf_op jit(solution)/shard_map/amps/pallas_call | solution.py:109
  58.2 0.0 collective-permute-done.5.arrived
  58.2 1.0 last.1
  59.2 0.0 copy-start.2
  59.2 45.2 %all_to_all.5 = bf16[128,40,128]{2,1,0:T(8,128)(2,1)S(1)} all-to-all(bf16[128,40,128]{2,1,0:T(8,128)(2,1)S(1)} %bitcast.18), channel_id=1, replica_groups=mesh['occ_0'=2,'occ_1'=4,'occ_2'=8,'occ_3'=2,'frag'=4] {'occ_0','occ_1',..., dimensions={0} | all-to-all | bytes 2621440 | tf_op jit(solution)/shard_map/all_to_all | solution.py:224
  104.5 0.0 copy-done.2
  104.5 2.7 %back.1 = bf16[10,128,1024]{2,1,0:T(8,128)(2,1)} custom-call(bf16[5120,128]{1,0:T(8,128)(2,1)S(1)} %bitcast.19, bf16[1024,512]{1,0:T(8,128)(2,1)S(1)} %copy-done.2), custom_call_target="tpu_custom_call" | custom-call | flops 1342177280 | bytes 3932160 | tf_op jit(solution)/shard_map/back/pallas_call | solution.py:181
Async XLA Ops:
  0.0 25.2 %copy-start.4 = (f32[128]{0:T(128)S(1)}, f32[128]{0:T(128)}, u32[]{:S(2)}) copy-start(f32[128]{0:T(128)} %refs_1_.9) | copy-start | bytes 1540
  0.0 30.1 %collective-permute-start = (bf16[512,1280]{1,0:T(8,128)(2,1)}, bf16[512,1280]{1,0:T(8,128)(2,1)}, u32[]{:S(2)}, u32[]{:S(2)}) collective-permute-start(bf16[512,1280]{1,0:T(8,128)(2,1)} %bitcast.12), channel_id=1, source_target_pairs={{0,504},{4,12},{8,0},{12,20},{16,8},{20,28},{24,16},{28,36},{32,24... | collective-permute-start | bytes 3932168 | tf_op jit(solution)/shard_map/ppermute | solution.py:23
  5.0 1.3 %copy-start = (bf16[1,512,1280]{2,1,0:T(8,128)(2,1)S(1)}, bf16[1,512,1280]{2,1,0:T(8,128)(2,1)}, u32[]{:S(2)}) copy-start(bf16[1,512,1280]{2,1,0:T(8,128)(2,1)} %param.4) | copy-start | bytes 3932164
  6.3 18.6 %copy-start.3 = (f32[512]{0:T(512)S(1)}, f32[512]{0:T(512)}, u32[]{:S(2)}) copy-start(f32[512]{0:T(512)} %param.6) | copy-start | bytes 6148
  6.3 19.0 %copy-start.1 = (bf16[1,512,1280]{2,1,0:T(8,128)(2,1)S(1)}, bf16[1,512,1280]{2,1,0:T(8,128)(2,1)}, u32[]{:S(2)}) copy-start(bf16[1,512,1280]{2,1,0:T(8,128)(2,1)} %param.4) | copy-start | bytes 3932164
  8.0 17.3 %collective-permute-start.3 = (bf16[256,1280]{1,0:T(8,128)(2,1)}, bf16[256,1280]{1,0:T(8,128)(2,1)S(1)}, u32[]{:S(2)}, u32[]{:S(2)}) collective-permute-start(bf16[256,1280]{1,0:T(8,128)(2,1)} %get-tuple-element.13), channel_id=1, source_target_pairs={{0,4},{4,0},{8,12},{12,8},{16,20},{20,16},{24,28},{28,24},{32,36},... | collective-permute-start | bytes 1966088 | tf_op jit(solution)/shard_map/ppermute | solution.py:23
  20.7 4.5 %collective-permute-start.4 = (bf16[256,1280]{1,0:T(8,128)(2,1)}, bf16[256,1280]{1,0:T(8,128)(2,1)}, u32[]{:S(2)}, u32[]{:S(2)}) collective-permute-start(bf16[256,1280]{1,0:T(8,128)(2,1)} %get-tuple-element.14), channel_id=1, source_target_pairs={{0,4},{4,0},{8,12},{12,8},{16,20},{20,16},{24,28},{28,24},{32,36},... | collective-permute-start | bytes 1966088 | tf_op jit(solution)/shard_map/ppermute | solution.py:23
  22.6 27.8 %collective-permute-start.2 = (bf16[512,1280]{1,0:T(8,128)(2,1)}, bf16[512,1280]{1,0:T(8,128)(2,1)S(1)}, u32[]{:S(2)}, u32[]{:S(2)}) collective-permute-start(bf16[512,1280]{1,0:T(8,128)(2,1)} %get-tuple-element.12), channel_id=1, source_target_pairs={{0,8},{4,508},{8,16},{12,4},{16,24},{20,12},{24,32},{28,20},{32,40... | collective-permute-start | bytes 3932168 | tf_op jit(solution)/shard_map/ppermute | solution.py:23
  30.1 26.6 %collective-permute-start.1 = (bf16[512,1280]{1,0:T(8,128)(2,1)}, bf16[512,1280]{1,0:T(8,128)(2,1)S(1)}, u32[]{:S(2)}, u32[]{:S(2)}) collective-permute-start(bf16[512,1280]{1,0:T(8,128)(2,1)} %collective-permute-done.refs_6_), channel_id=1, source_target_pairs={{0,508},{4,8},{8,4},{12,16},{16,12},{20,24},{24,20},{28,32},{32,28... | collective-permute-start | bytes 3932168 | tf_op jit(solution)/shard_map/ppermute | solution.py:23
  52.6 5.6 %collective-permute-start.5 = (bf16[1280,512]{1,0:T(8,128)(2,1)S(1)}, bf16[1280,512]{1,0:T(8,128)(2,1)S(1)}, u32[]{:S(2)}, u32[]{:S(2)}) collective-permute-start(bf16[1280,512]{1,0:T(8,128)(2,1)S(1)} %pairs.5), channel_id=1, source_target_pairs={{0,4},{4,0},{8,12},{12,8},{16,20},{20,16},{24,28},{28,24},{32,36},... | collective-permute-start | bytes 3932168 | tf_op jit(solution)/shard_map/ppermute | solution.py:23
  59.2 45.2 %copy-start.2 = (bf16[1024,512]{1,0:T(8,128)(2,1)S(1)}, bf16[1024,512]{1,0:T(8,128)(2,1)}, u32[]{:S(2)}) copy-start(bf16[1024,512]{1,0:T(8,128)(2,1)} %coeffs.1) | copy-start | bytes 3145732

commit v6 on v5

--- a/solution.py
+++ b/solution.py
@@ -103,7 +103,7 @@
     out[...] = wide[...].astype(out.dtype)
 
 
-def local_call(kernel, levels, arrays, outs, scratch=(), name=None, flops=1000):
+def local_call(kernel, levels, arrays, outs, scratch=(), name=None):
     vmem = pl.BlockSpec(memory_space=pltpu.VMEM)
     smem = pl.BlockSpec(memory_space=pltpu.SMEM)
     return pl.pallas_call(
@@ -113,7 +113,7 @@
         out_specs=[vmem] * len(outs),
         scratch_shapes=list(scratch),
         compiler_params=pltpu.CompilerParams(vmem_limit_bytes=VMEM_LIMIT),
-        cost_estimate=pl.CostEstimate(flops=flops, bytes_accessed=1000, transcendentals=0),
+        cost_estimate=pl.CostEstimate(flops=1000, bytes_accessed=1000, transcendentals=0),
         name=name,
     )(*levels, *arrays)
 
@@ -122,8 +122,7 @@
     shape = blocks[0].shape[::-1]
     kernel = functools.partial(pairs_kernel, pairs, len(blocks), len(totals))
     outs = [(shape, dtype) for dtype in dtypes]
-    flops = 10**10 if len(pairs) > 1 else 1000
-    return local_call(kernel, levels, [*blocks, *totals], outs, name="pairs", flops=flops)
+    return local_call(kernel, levels, [*blocks, *totals], outs, name="pairs")
 
 
 def first_pair(levels, steps, mine, upper, lower):

time: 108 us -> 109 us (level)
  waiting for transfers between devices: 16.1 us -> 7.21 us
  starting transfers between devices: 25.6 us -> 34.3 us
  blocking collectives: 45.2 us -> 47.3 us
    ppermute x6, waiting for transfers between devices: 16.1 us -> 7.21 us  [mirrored(): return lax.ppermute(block, OCC, route)]
    ppermute x6, starting transfers between devices: 25.6 us -> 34.3 us  [mirrored(): return lax.ppermute(block, OCC, route)]
    all_to_all x1, blocking collectives: 45.2 us -> 47.3 us  [on_device(): lax.all_to_all(gamma.reshape(count, -1, LANES), OCC, 0, 0, tiled=True)]
  transfers between devices with their start and end apart: 6 -> 6, of which waited for: 2 -> 4; matrix products, arithmetic and copies ran while one was open for 0% -> 0% of each run, Pallas kernels for 14% -> 13%
where the time goes in v6:
time: 109 us
  blocking collectives  47.3 us (43%)
  starting transfers between devices  34.3 us (31%)
  Pallas kernels  18.3 us (17%)
  waiting for transfers between devices  7.21 us (7%)
  local copies, waits for them, and re-layouts  1.57 us (1%)
    all_to_all x1, blocking collectives, on_device(): lax.all_to_all(gamma.reshape(count, -1, LANES), OCC, 0, 0, tiled=True)  47.3 us
    ppermute x6, starting transfers between devices, mirrored(): return lax.ppermute(block, OCC, route)  34.3 us
    pallas_call x5, Pallas kernels, local_call(): pl.pallas_call(kernel, out_shape=[jax.ShapeDtypeStruct(shape, dtype) for...  13 us
    ppermute x6, waiting for transfers between devices, mirrored(): return lax.ppermute(block, OCC, route)  7.21 us
    pallas_call x1, Pallas kernels, back_transform(): pl.pallas_call(functools.partial(back_kernel, chunk), out_shape=jax.Shape...  2.66 us
  transfers between devices with their start and end apart: 6, of which 4 were waited for; matrix products, arithmetic and copies ran while one was open for 0% of the time, Pallas kernels for 13%

profile of v6, /device:TPU:1, one launch (start us, length us, event | category | flops | bytes accessed | tf_op | source)
XLA Modules:
  0.0 109.1 jit_solution(12765465545871575285)
XLA Ops:
  0.0 0.0 copy-start.4
  0.0 5.0 %collective-permute-start = (bf16[512,1280]{1,0:T(8,128)(2,1)}, bf16[512,1280]{1,0:T(8,128)(2,1)}, u32[]{:S(2)}, u32[]{:S(2)}) collective-permute-start(bf16[512,1280]{1,0:T(8,128)(2,1)} %bitcast.12), channel_id=1, source_target_pairs={{0,504},{4,12},{8,0},{12,20},{16,8},{20,28},{24,16},{28,36},{32,24... | collective-permute-start | bytes 3932168 | tf_op jit(solution)/shard_map/ppermute | solution.py:23
  5.0 0.0 copy-start
  5.0 1.3 %copy-done = bf16[1,512,1280]{2,1,0:T(8,128)(2,1)S(1)} copy-done((bf16[1,512,1280]{2,1,0:T(8,128)(2,1)S(1)}, bf16[1,512,1280]{2,1,0:T(8,128)(2,1)}, u32[]{:S(2)}) %copy-start) | copy-done | bytes 1310744
  6.3 0.0 copy-start.3
  6.3 0.0 copy-start.1
  6.3 1.7 %split.1 = (bf16[256,1280]{1,0:T(8,128)(2,1)}, bf16[256,1280]{1,0:T(8,128)(2,1)}, bf16[512,1280]{1,0:T(8,128)(2,1)}) custom-call(bf16[512,1280]{1,0:T(8,128)(2,1)S(1)} %bitcast.13), custom_call_target="tpu_custom_call" | custom-call | flops 1000 | bytes 1000 | tf_op jit(solution)/shard_map/split/pallas_call | solution.py:76
  8.0 11.8 %collective-permute-start.2 = (bf16[512,1280]{1,0:T(8,128)(2,1)}, bf16[512,1280]{1,0:T(8,128)(2,1)S(1)}, u32[]{:S(2)}, u32[]{:S(2)}) collective-permute-start(bf16[512,1280]{1,0:T(8,128)(2,1)} %get-tuple-element.12), channel_id=1, source_target_pairs={{0,8},{4,508},{8,16},{12,4},{16,24},{20,12},{24,32},{28,20},{32,40... | collective-permute-start | bytes 3932168 | tf_op jit(solution)/shard_map/ppermute | solution.py:23
  19.7 2.9 %collective-permute-start.3 = (bf16[256,1280]{1,0:T(8,128)(2,1)}, bf16[256,1280]{1,0:T(8,128)(2,1)S(1)}, u32[]{:S(2)}, u32[]{:S(2)}) collective-permute-start(bf16[256,1280]{1,0:T(8,128)(2,1)} %get-tuple-element.13), channel_id=1, source_target_pairs={{0,4},{4,0},{8,12},{12,8},{16,20},{20,16},{24,28},{28,24},{32,36},... | collective-permute-start | bytes 1966088 | tf_op jit(solution)/shard_map/ppermute | solution.py:23
  22.6 1.9 %collective-permute-start.4 = (bf16[256,1280]{1,0:T(8,128)(2,1)}, bf16[256,1280]{1,0:T(8,128)(2,1)}, u32[]{:S(2)}, u32[]{:S(2)}) collective-permute-start(bf16[256,1280]{1,0:T(8,128)(2,1)} %get-tuple-element.14), channel_id=1, source_target_pairs={{0,4},{4,0},{8,12},{12,8},{16,20},{20,16},{24,28},{28,24},{32,36},... | collective-permute-start | bytes 1966088 | tf_op jit(solution)/shard_map/ppermute | solution.py:23
  24.7 0.0 copy-done.3
  24.7 0.1 copy.5.refs_2_
  24.9 0.1 stack.31.refs_0_
  25.0 0.0 collective-permute-done.3.refs_5_
  25.0 2.0 %collective-permute-done.4.refs_6_ = bf16[256,1280]{1,0:T(8,128)(2,1)} collective-permute-done((bf16[256,1280]{1,0:T(8,128)(2,1)}, bf16[256,1280]{1,0:T(8,128)(2,1)}, u32[]{:S(2)}, u32[]{:S(2)}) %collective-permute-start.4) | collective-permute-done | bytes 655392 | tf_op jit(solution)/shard_map/ppermute | solution.py:23
  26.9 0.0 copy-done.4
  26.9 0.0 copy-done.1
  27.0 2.7 %first.1 = (f32[1280,512]{1,0:T(8,128)S(1)}, bf16[512,1280]{1,0:T(8,128)(2,1)S(1)}) custom-call(s32[7]{0:T(128)S(1)} %stack.31.refs_0_, f32[128]{0:T(128)S(1)} %copy-done.4, f32[512,1]{1,0:T(8,128)S(1)} %copy.5.refs_2_, f32[1,512]{1,0:T(1,128)S(1)} %bitcast.21, bf16[512,1280]{1,0:T(8,128)(2,1)S(1)} %bitcast.14, ...), custom_call_target="tpu_custom_call" | custom-call | flops 1000 | bytes 1000 | tf_op jit(solution)/shard_map/first/pallas_call | solution.py:109
  29.7 2.6 %collective-permute-done.refs_6_ = bf16[512,1280]{1,0:T(8,128)(2,1)} collective-permute-done((bf16[512,1280]{1,0:T(8,128)(2,1)}, bf16[512,1280]{1,0:T(8,128)(2,1)}, u32[]{:S(2)}, u32[]{:S(2)}) %collective-permute-start) | collective-permute-done | bytes 1310752 | tf_op jit(solution)/shard_map/ppermute | solution.py:23
  32.3 8.5 %collective-permute-start.1 = (bf16[512,1280]{1,0:T(8,128)(2,1)}, bf16[512,1280]{1,0:T(8,128)(2,1)S(1)}, u32[]{:S(2)}, u32[]{:S(2)}) collective-permute-start(bf16[512,1280]{1,0:T(8,128)(2,1)} %collective-permute-done.refs_6_), channel_id=1, source_target_pairs={{0,508},{4,8},{8,4},{12,16},{16,12},{20,24},{24,20},{28,32},{32,28... | collective-permute-start | bytes 3932168 | tf_op jit(solution)/shard_map/ppermute | solution.py:23
  40.8 4.4 %pairs.3 = (f32[1280,512]{1,0:T(8,128)S(1)}, f32[1280,512]{1,0:T(8,128)S(1)}) custom-call(s32[7]{0:T(128)S(1)} %stack.31.refs_0_, f32[128]{0:T(128)S(1)} %copy-done.4, f32[512,1]{1,0:T(8,128)S(1)} %copy.5.refs_2_, f32[1,512]{1,0:T(1,128)S(1)} %bitcast.22, bf16[512,1280]{1,0:T(8,128)(2,1)S(1)} %bitcast.15, ...), custom_call_target="tpu_custom_call" | custom-call | flops 1000 | bytes 1000 | tf_op jit(solution)/shard_map/pairs/pallas_call | solution.py:109
  45.2 0.1 collective-permute-done.2.refs_5_
  45.3 2.2 %pairs.5 = bf16[1280,512]{1,0:T(8,128)(2,1)S(1)} custom-call(s32[7]{0:T(128)S(1)} %stack.31.refs_0_, f32[128]{0:T(128)S(1)} %copy-done.4, f32[512,1]{1,0:T(8,128)S(1)} %copy.5.refs_2_, f32[1,512]{1,0:T(1,128)S(1)} %bitcast.23, bf16[512,1280]{1,0:T(8,128)(2,1)S(1)} %get-tuple-element.15.refs_5_.refs_4_, bf16[512,1280]{1,0:T(8,128)(2,1)S(1)} %collective-permute-done.2.refs_5_, ...), custom_call_target="tpu_custom_call" | custom-call | flops 1000 | bytes 1000 | tf_op jit(solution)/shard_map/pairs/pallas_call | solution.py:109
  47.5 4.4 %collective-permute-start.5 = (bf16[1280,512]{1,0:T(8,128)(2,1)S(1)}, bf16[1280,512]{1,0:T(8,128)(2,1)S(1)}, u32[]{:S(2)}, u32[]{:S(2)}) collective-permute-start(bf16[1280,512]{1,0:T(8,128)(2,1)S(1)} %pairs.5), channel_id=1, source_target_pairs={{0,4},{4,0},{8,12},{12,8},{16,20},{20,16},{24,28},{28,24},{32,36},... | collective-permute-start | bytes 3932168 | tf_op jit(solution)/shard_map/ppermute | solution.py:23
  51.9 2.2 %pairs.4.total = f32[1280,512]{1,0:T(8,128)S(1)} custom-call(s32[7]{0:T(128)S(1)} %stack.31.refs_0_, f32[128]{0:T(128)S(1)} %copy-done.4, f32[512,1]{1,0:T(8,128)S(1)} %copy.5.refs_2_, f32[1,512]{1,0:T(1,128)S(1)} %bitcast.24, bf16[512,1280]{1,0:T(8,128)(2,1)S(1)} %bitcast.16, bf16[512,1280]{1,0:T(8,128)(2,1)S(1)} %collective-permute-done.2.refs_5_, ...), custom_call_target="tpu_custom_call" | custom-call | flops 1000 | bytes 1000 | tf_op jit(solution)/shard_map/pairs/pallas_call | solution.py:109
  54.1 2.5 %collective-permute-done.1.refs_5_.other = bf16[512,1280]{1,0:T(8,128)(2,1)S(1)} collective-permute-done((bf16[512,1280]{1,0:T(8,128)(2,1)}, bf16[512,1280]{1,0:T(8,128)(2,1)S(1)}, u32[]{:S(2)}, u32[]{:S(2)}) %collective-permute-start.1) | collective-permute-done | bytes 1310752 | tf_op jit(solution)/shard_map/ppermute | solution.py:23
  56.6 1.4 %amps.1 = bf16[512,512]{1,0:T(8,128)(2,1)S(1)} custom-call(s32[7]{0:T(128)S(1)} %stack.31.refs_0_, f32[128]{0:T(128)S(1)} %copy-done.4, f32[512,1]{1,0:T(8,128)S(1)} %copy.5.refs_2_, f32[1,512]{1,0:T(1,128)S(1)} %bitcast.25, bf16[512,1280]{1,0:T(8,128)(2,1)S(1)} %bitcast.17, bf16[512,1280]{1,0:T(8,128)(2,1)S(1)} %collective-permute-done.1.refs_5_.other), custom_call_target="tpu_custom_call" | custom-call | flops 1000 | bytes 1000 | tf_op jit(solution)/shard_map/amps/pallas_call | solution.py:109
  58.0 0.0 collective-permute-done.5.arrived
  58.0 1.1 last.1
  59.1 0.0 copy-start.2
  59.1 47.3 %all_to_all.5 = bf16[128,40,128]{2,1,0:T(8,128)(2,1)S(1)} all-to-all(bf16[128,40,128]{2,1,0:T(8,128)(2,1)S(1)} %bitcast.18), channel_id=1, replica_groups=mesh['occ_0'=2,'occ_1'=4,'occ_2'=8,'occ_3'=2,'frag'=4] {'occ_0','occ_1',..., dimensions={0} | all-to-all | bytes 2621440 | tf_op jit(solution)/shard_map/all_to_all | solution.py:223
  106.4 0.0 copy-done.2
  106.4 2.7 %back.1 = bf16[10,128,1024]{2,1,0:T(8,128)(2,1)} custom-call(bf16[5120,128]{1,0:T(8,128)(2,1)S(1)} %bitcast.19, bf16[1024,512]{1,0:T(8,128)(2,1)S(1)} %copy-done.2), custom_call_target="tpu_custom_call" | custom-call | flops 1342177280 | bytes 3932160 | tf_op jit(solution)/shard_map/back/pallas_call | solution.py:180
Async XLA Ops:
  0.0 26.9 %copy-start.4 = (f32[128]{0:T(128)S(1)}, f32[128]{0:T(128)}, u32[]{:S(2)}) copy-start(f32[128]{0:T(128)} %refs_1_.9) | copy-start | bytes 1540
  0.0 32.3 %collective-permute-start = (bf16[512,1280]{1,0:T(8,128)(2,1)}, bf16[512,1280]{1,0:T(8,128)(2,1)}, u32[]{:S(2)}, u32[]{:S(2)}) collective-permute-start(bf16[512,1280]{1,0:T(8,128)(2,1)} %bitcast.12), channel_id=1, source_target_pairs={{0,504},{4,12},{8,0},{12,20},{16,8},{20,28},{24,16},{28,36},{32,24... | collective-permute-start | bytes 3932168 | tf_op jit(solution)/shard_map/ppermute | solution.py:23
  5.0 1.3 %copy-start = (bf16[1,512,1280]{2,1,0:T(8,128)(2,1)S(1)}, bf16[1,512,1280]{2,1,0:T(8,128)(2,1)}, u32[]{:S(2)}) copy-start(bf16[1,512,1280]{2,1,0:T(8,128)(2,1)} %param.4) | copy-start | bytes 3932164
  6.3 18.4 %copy-start.3 = (f32[512]{0:T(512)S(1)}, f32[512]{0:T(512)}, u32[]{:S(2)}) copy-start(f32[512]{0:T(512)} %param.6) | copy-start | bytes 6148
  6.3 20.7 %copy-start.1 = (bf16[1,512,1280]{2,1,0:T(8,128)(2,1)S(1)}, bf16[1,512,1280]{2,1,0:T(8,128)(2,1)}, u32[]{:S(2)}) copy-start(bf16[1,512,1280]{2,1,0:T(8,128)(2,1)} %param.4) | copy-start | bytes 3932164
  8.0 37.4 %collective-permute-start.2 = (bf16[512,1280]{1,0:T(8,128)(2,1)}, bf16[512,1280]{1,0:T(8,128)(2,1)S(1)}, u32[]{:S(2)}, u32[]{:S(2)}) collective-permute-start(bf16[512,1280]{1,0:T(8,128)(2,1)} %get-tuple-element.12), channel_id=1, source_target_pairs={{0,8},{4,508},{8,16},{12,4},{16,24},{20,12},{24,32},{28,20},{32,40... | collective-permute-start | bytes 3932168 | tf_op jit(solution)/shard_map/ppermute | solution.py:23
  19.7 5.2 %collective-permute-start.3 = (bf16[256,1280]{1,0:T(8,128)(2,1)}, bf16[256,1280]{1,0:T(8,128)(2,1)S(1)}, u32[]{:S(2)}, u32[]{:S(2)}) collective-permute-start(bf16[256,1280]{1,0:T(8,128)(2,1)} %get-tuple-element.13), channel_id=1, source_target_pairs={{0,4},{4,0},{8,12},{12,8},{16,20},{20,16},{24,28},{28,24},{32,36},... | collective-permute-start | bytes 1966088 | tf_op jit(solution)/shard_map/ppermute | solution.py:23
  22.6 4.3 %collective-permute-start.4 = (bf16[256,1280]{1,0:T(8,128)(2,1)}, bf16[256,1280]{1,0:T(8,128)(2,1)}, u32[]{:S(2)}, u32[]{:S(2)}) collective-permute-start(bf16[256,1280]{1,0:T(8,128)(2,1)} %get-tuple-element.14), channel_id=1, source_target_pairs={{0,4},{4,0},{8,12},{12,8},{16,20},{20,16},{24,28},{28,24},{32,36},... | collective-permute-start | bytes 1966088 | tf_op jit(solution)/shard_map/ppermute | solution.py:23
  32.3 24.2 %collective-permute-start.1 = (bf16[512,1280]{1,0:T(8,128)(2,1)}, bf16[512,1280]{1,0:T(8,128)(2,1)S(1)}, u32[]{:S(2)}, u32[]{:S(2)}) collective-permute-start(bf16[512,1280]{1,0:T(8,128)(2,1)} %collective-permute-done.refs_6_), channel_id=1, source_target_pairs={{0,508},{4,8},{8,4},{12,16},{16,12},{20,24},{24,20},{28,32},{32,28... | collective-permute-start | bytes 3932168 | tf_op jit(solution)/shard_map/ppermute | solution.py:23
  47.5 10.5 %collective-permute-start.5 = (bf16[1280,512]{1,0:T(8,128)(2,1)S(1)}, bf16[1280,512]{1,0:T(8,128)(2,1)S(1)}, u32[]{:S(2)}, u32[]{:S(2)}) collective-permute-start(bf16[1280,512]{1,0:T(8,128)(2,1)S(1)} %pairs.5), channel_id=1, source_target_pairs={{0,4},{4,0},{8,12},{12,8},{16,20},{20,16},{24,28},{28,24},{32,36},... | collective-permute-start | bytes 3932168 | tf_op jit(solution)/shard_map/ppermute | solution.py:23
  59.1 47.3 %copy-start.2 = (bf16[1024,512]{1,0:T(8,128)(2,1)S(1)}, bf16[1024,512]{1,0:T(8,128)(2,1)}, u32[]{:S(2)}) copy-start(bf16[1024,512]{1,0:T(8,128)(2,1)} %coeffs.1) | copy-start | bytes 3145732

commit v7 on v5

--- a/solution.py
+++ b/solution.py
@@ -63,11 +63,10 @@
         total[part, :] = value
 
 
-def split_kernel(mine, upper, lower, again):
+def split_kernel(mine, upper, lower):
     half = upper.shape[0]
     upper[...] = mine[:half, :]
     lower[...] = mine[half:, :]
-    again[...] = mine[...]
 
 
 def split(mine):
@@ -75,12 +74,9 @@
     vmem = pl.BlockSpec(memory_space=pltpu.VMEM)
     return pl.pallas_call(
         split_kernel,
-        out_shape=[
-            jax.ShapeDtypeStruct((height, aux), mine.dtype)
-            for height in (rows // 2, rows // 2, rows)
-        ],
+        out_shape=[jax.ShapeDtypeStruct((rows // 2, aux), mine.dtype)] * 2,
         in_specs=[vmem],
-        out_specs=[vmem] * 3,
+        out_specs=[vmem] * 2,
         compiler_params=pltpu.CompilerParams(vmem_limit_bytes=VMEM_LIMIT),
         cost_estimate=pl.CostEstimate(flops=1000, bytes_accessed=1000, transcendentals=0),
         name="split",
@@ -209,10 +205,10 @@
     f32, bf16 = jnp.float32, jnp.bfloat16
 
     plus2 = mirrored(mine, count, -2)
-    upper, lower, again = split(mine)
-    minus2 = mirrored(again, count, 2)
+    upper, lower = split(mine)
     upper, lower = mirrored(upper, count, 1), mirrored(lower, count, 1)
     total, plus1 = first_pair(levels, (0, 1), mine, upper, lower)
+    minus2 = mirrored(plus1, count, -1)
     minus3 = mirrored(plus2, count, -1)
     total, beside = pairs_sum(
         levels, [mine, plus1, plus2], [((0, 2), 0, 2), ((1, 2), 1, 2)], [total], [f32, f32]

time: 108 us -> 108 us (level)
  starting transfers between devices: 25.6 us -> 29.4 us
  blocking collectives: 45.2 us -> 42.9 us
  Pallas kernels: 18.3 us -> 17 us
    ppermute x6, starting transfers between devices: 25.6 us -> 29.4 us  [mirrored(): return lax.ppermute(block, OCC, route)]
    all_to_all x1, blocking collectives: 45.2 us -> 42.9 us  [on_device(): lax.all_to_all(gamma.reshape(count, -1, LANES), OCC, 0, 0, tiled=True)]
  transfers between devices with their start and end apart: 6 -> 6, of which waited for: 2 -> 4; matrix products, arithmetic and copies ran while one was open for 0% -> 0% of each run, Pallas kernels for 14% -> 12%
where the time goes in v7:
time: 108 us; the launch traced here: 107 us
  blocking collectives  42.9 us (40%)
  starting transfers between devices  29.4 us (27%)
  Pallas kernels  17 us (16%)
  waiting for transfers between devices  16.3 us (15%)
  local copies, waits for them, and re-layouts  1.57 us (1%)
    all_to_all x1, blocking collectives, on_device(): lax.all_to_all(gamma.reshape(count, -1, LANES), OCC, 0, 0, tiled=True)  42.9 us
    ppermute x6, starting transfers between devices, mirrored(): return lax.ppermute(block, OCC, route)  29.4 us
    ppermute x6, waiting for transfers between devices, mirrored(): return lax.ppermute(block, OCC, route)  16.3 us
    pallas_call x5, Pallas kernels, local_call(): pl.pallas_call(kernel, out_shape=[jax.ShapeDtypeStruct(shape, dtype) for...  12.4 us
    pallas_call x1, Pallas kernels, back_transform(): pl.pallas_call(functools.partial(back_kernel, chunk), out_shape=jax.Shape...  2.66 us
  transfers between devices with their start and end apart: 6, of which 4 were waited for; matrix products, arithmetic and copies ran while one was open for 0% of the time, Pallas kernels for 12%

profile of v7, /device:TPU:1, one launch (start us, length us, event | category | flops | bytes accessed | tf_op | source)
XLA Modules:
  0.0 107.5 jit_solution(14298424154708454697)
XLA Ops:
  0.0 0.0 copy-start.4
  0.0 5.0 %collective-permute-start = (bf16[512,1280]{1,0:T(8,128)(2,1)}, bf16[512,1280]{1,0:T(8,128)(2,1)}, u32[]{:S(2)}, u32[]{:S(2)}) collective-permute-start(bf16[512,1280]{1,0:T(8,128)(2,1)} %bitcast.12), channel_id=1, source_target_pairs={{0,504},{4,12},{8,0},{12,20},{16,8},{20,28},{24,16},{28,36},{32,24... | collective-permute-start | bytes 3932168 | tf_op jit(solution)/shard_map/ppermute | solution.py:23
  5.0 0.0 copy-start
  5.0 1.3 %copy-done = bf16[1,512,1280]{2,1,0:T(8,128)(2,1)S(1)} copy-done((bf16[1,512,1280]{2,1,0:T(8,128)(2,1)S(1)}, bf16[1,512,1280]{2,1,0:T(8,128)(2,1)}, u32[]{:S(2)}) %copy-start) | copy-done | bytes 1310744
  6.3 0.0 copy-start.3
  6.3 0.0 copy-start.1
  6.3 0.9 split.1
  7.2 12.7 %collective-permute-start.2 = (bf16[256,1280]{1,0:T(8,128)(2,1)}, bf16[256,1280]{1,0:T(8,128)(2,1)S(1)}, u32[]{:S(2)}, u32[]{:S(2)}) collective-permute-start(bf16[256,1280]{1,0:T(8,128)(2,1)} %get-tuple-element.11), channel_id=1, source_target_pairs={{0,4},{4,0},{8,12},{12,8},{16,20},{20,16},{24,28},{28,24},{32,36},... | collective-permute-start | bytes 1966088 | tf_op jit(solution)/shard_map/ppermute | solution.py:23
  19.9 1.9 %collective-permute-start.3 = (bf16[256,1280]{1,0:T(8,128)(2,1)S(1)}, bf16[256,1280]{1,0:T(8,128)(2,1)S(1)}, u32[]{:S(2)}, u32[]{:S(2)}) collective-permute-start(bf16[256,1280]{1,0:T(8,128)(2,1)S(1)} %get-tuple-element.12), channel_id=1, source_target_pairs={{0,4},{4,0},{8,12},{12,8},{16,20},{20,16},{24,28},{28,24},{32,36},... | collective-permute-start | bytes 1966088 | tf_op jit(solution)/shard_map/ppermute | solution.py:23
  22.0 0.0 copy-done.3
  22.0 0.1 copy.5.refs_2_
  22.2 0.1 stack.31.refs_0_
  22.3 0.0 collective-permute-done.2.refs_5_
  22.3 1.6 %collective-permute-done.3.refs_6_ = bf16[256,1280]{1,0:T(8,128)(2,1)S(1)} collective-permute-done((bf16[256,1280]{1,0:T(8,128)(2,1)S(1)}, bf16[256,1280]{1,0:T(8,128)(2,1)S(1)}, u32[]{:S(2)}, u32[]{:S(2)}) %collective-permute-start.3) | collective-permute-done | bytes 655392 | tf_op jit(solution)/shard_map/ppermute | solution.py:23
  23.9 0.0 copy-done.4
  23.9 0.0 copy-done.1
  23.9 2.2 %first.1 = (f32[1280,512]{1,0:T(8,128)S(1)}, bf16[512,1280]{1,0:T(8,128)(2,1)S(1)}) custom-call(s32[7]{0:T(128)S(1)} %stack.31.refs_0_, f32[128]{0:T(128)S(1)} %copy-done.4, f32[512,1]{1,0:T(8,128)S(1)} %copy.5.refs_2_, f32[1,512]{1,0:T(1,128)S(1)} %bitcast.21, bf16[512,1280]{1,0:T(8,128)(2,1)S(1)} %bitcast.14, ...), custom_call_target="tpu_custom_call" | custom-call | flops 1000 | bytes 1000 | tf_op jit(solution)/shard_map/first/pallas_call | solution.py:105
  26.1 1.9 %collective-permute-start.4 = (bf16[512,1280]{1,0:T(8,128)(2,1)S(1)}, bf16[512,1280]{1,0:T(8,128)(2,1)S(1)}, u32[]{:S(2)}, u32[]{:S(2)}) collective-permute-start(bf16[512,1280]{1,0:T(8,128)(2,1)S(1)} %get-tuple-element.13.refs_5_.refs_4_), channel_id=1, source_target_pairs={{0,508},{4,8},{8,4},{12,16},{16,12},{20,24},{24,20},{28,32},{32,28... | collective-permute-start | bytes 3932168 | tf_op jit(solution)/shard_map/ppermute | solution.py:23
  28.1 2.1 %collective-permute-done.refs_6_ = bf16[512,1280]{1,0:T(8,128)(2,1)} collective-permute-done((bf16[512,1280]{1,0:T(8,128)(2,1)}, bf16[512,1280]{1,0:T(8,128)(2,1)}, u32[]{:S(2)}, u32[]{:S(2)}) %collective-permute-start) | collective-permute-done | bytes 1310752 | tf_op jit(solution)/shard_map/ppermute | solution.py:23
  30.1 1.9 %collective-permute-start.1 = (bf16[512,1280]{1,0:T(8,128)(2,1)}, bf16[512,1280]{1,0:T(8,128)(2,1)S(1)}, u32[]{:S(2)}, u32[]{:S(2)}) collective-permute-start(bf16[512,1280]{1,0:T(8,128)(2,1)} %collective-permute-done.refs_6_), channel_id=1, source_target_pairs={{0,508},{4,8},{8,4},{12,16},{16,12},{20,24},{24,20},{28,32},{32,28... | collective-permute-start | bytes 3932168 | tf_op jit(solution)/shard_map/ppermute | solution.py:23
  32.1 4.4 %pairs.3 = (f32[1280,512]{1,0:T(8,128)S(1)}, f32[1280,512]{1,0:T(8,128)S(1)}) custom-call(s32[7]{0:T(128)S(1)} %stack.31.refs_0_, f32[128]{0:T(128)S(1)} %copy-done.4, f32[512,1]{1,0:T(8,128)S(1)} %copy.5.refs_2_, f32[1,512]{1,0:T(1,128)S(1)} %bitcast.22, bf16[512,1280]{1,0:T(8,128)(2,1)S(1)} %bitcast.15, ...), custom_call_target="tpu_custom_call" | custom-call | flops 10000000000 | bytes 1000 | tf_op jit(solution)/shard_map/pairs/pallas_call | solution.py:105
  36.5 8.9 %collective-permute-done.4.refs_5_ = bf16[512,1280]{1,0:T(8,128)(2,1)S(1)} collective-permute-done((bf16[512,1280]{1,0:T(8,128)(2,1)S(1)}, bf16[512,1280]{1,0:T(8,128)(2,1)S(1)}, u32[]{:S(2)}, u32[]{:S(2)}) %collective-permute-start.4) | collective-permute-done | bytes 1310752 | tf_op jit(solution)/shard_map/ppermute | solution.py:23
  45.4 2.2 %pairs.5 = bf16[1280,512]{1,0:T(8,128)(2,1)S(1)} custom-call(s32[7]{0:T(128)S(1)} %stack.31.refs_0_, f32[128]{0:T(128)S(1)} %copy-done.4, f32[512,1]{1,0:T(8,128)S(1)} %copy.5.refs_2_, f32[1,512]{1,0:T(1,128)S(1)} %bitcast.23, bf16[512,1280]{1,0:T(8,128)(2,1)S(1)} %get-tuple-element.13.refs_5_.refs_4_, bf16[512,1280]{1,0:T(8,128)(2,1)S(1)} %collective-permute-done.4.refs_5_, ...), custom_call_target="tpu_custom_call" | custom-call | flops 1000 | bytes 1000 | tf_op jit(solution)/shard_map/pairs/pallas_call | solution.py:105
  47.5 6.0 %collective-permute-start.5 = (bf16[1280,512]{1,0:T(8,128)(2,1)S(1)}, bf16[1280,512]{1,0:T(8,128)(2,1)S(1)}, u32[]{:S(2)}, u32[]{:S(2)}) collective-permute-start(bf16[1280,512]{1,0:T(8,128)(2,1)S(1)} %pairs.5), channel_id=1, source_target_pairs={{0,4},{4,0},{8,12},{12,8},{16,20},{20,16},{24,28},{28,24},{32,36},... | collective-permute-start | bytes 3932168 | tf_op jit(solution)/shard_map/ppermute | solution.py:23
  53.5 2.2 %pairs.4.total = f32[1280,512]{1,0:T(8,128)S(1)} custom-call(s32[7]{0:T(128)S(1)} %stack.31.refs_0_, f32[128]{0:T(128)S(1)} %copy-done.4, f32[512,1]{1,0:T(8,128)S(1)} %copy.5.refs_2_, f32[1,512]{1,0:T(1,128)S(1)} %bitcast.24, bf16[512,1280]{1,0:T(8,128)(2,1)S(1)} %bitcast.16, bf16[512,1280]{1,0:T(8,128)(2,1)S(1)} %collective-permute-done.4.refs_5_, ...), custom_call_target="tpu_custom_call" | custom-call | flops 1000 | bytes 1000 | tf_op jit(solution)/shard_map/pairs/pallas_call | solution.py:105
  55.7 3.7 %collective-permute-done.1.refs_5_.other = bf16[512,1280]{1,0:T(8,128)(2,1)S(1)} collective-permute-done((bf16[512,1280]{1,0:T(8,128)(2,1)}, bf16[512,1280]{1,0:T(8,128)(2,1)S(1)}, u32[]{:S(2)}, u32[]{:S(2)}) %collective-permute-start.1) | collective-permute-done | bytes 1310752 | tf_op jit(solution)/shard_map/ppermute | solution.py:23
  59.4 1.4 %amps.1 = bf16[512,512]{1,0:T(8,128)(2,1)S(1)} custom-call(s32[7]{0:T(128)S(1)} %stack.31.refs_0_, f32[128]{0:T(128)S(1)} %copy-done.4, f32[512,1]{1,0:T(8,128)S(1)} %copy.5.refs_2_, f32[1,512]{1,0:T(1,128)S(1)} %bitcast.25, bf16[512,1280]{1,0:T(8,128)(2,1)S(1)} %bitcast.17, bf16[512,1280]{1,0:T(8,128)(2,1)S(1)} %collective-permute-done.1.refs_5_.other), custom_call_target="tpu_custom_call" | custom-call | flops 1000 | bytes 1000 | tf_op jit(solution)/shard_map/amps/pallas_call | solution.py:105
  60.8 0.0 collective-permute-done.5.arrived
  60.8 1.0 last.1
  61.9 0.0 copy-start.2
  61.9 42.9 %all_to_all.5 = bf16[128,40,128]{2,1,0:T(8,128)(2,1)S(1)} all-to-all(bf16[128,40,128]{2,1,0:T(8,128)(2,1)S(1)} %bitcast.18), channel_id=1, replica_groups=mesh['occ_0'=2,'occ_1'=4,'occ_2'=8,'occ_3'=2,'frag'=4] {'occ_0','occ_1',..., dimensions={0} | all-to-all | bytes 2621440 | tf_op jit(solution)/shard_map/all_to_all | solution.py:220
  104.8 0.0 copy-done.2
  104.8 2.7 %back.1 = bf16[10,128,1024]{2,1,0:T(8,128)(2,1)} custom-call(bf16[5120,128]{1,0:T(8,128)(2,1)S(1)} %bitcast.19, bf16[1024,512]{1,0:T(8,128)(2,1)S(1)} %copy-done.2), custom_call_target="tpu_custom_call" | custom-call | flops 1342177280 | bytes 3932160 | tf_op jit(solution)/shard_map/back/pallas_call | solution.py:177
Async XLA Ops:
  0.0 23.9 %copy-start.4 = (f32[128]{0:T(128)S(1)}, f32[128]{0:T(128)}, u32[]{:S(2)}) copy-start(f32[128]{0:T(128)} %refs_1_.9) | copy-start | bytes 1540
  0.0 30.1 %collective-permute-start = (bf16[512,1280]{1,0:T(8,128)(2,1)}, bf16[512,1280]{1,0:T(8,128)(2,1)}, u32[]{:S(2)}, u32[]{:S(2)}) collective-permute-start(bf16[512,1280]{1,0:T(8,128)(2,1)} %bitcast.12), channel_id=1, source_target_pairs={{0,504},{4,12},{8,0},{12,20},{16,8},{20,28},{24,16},{28,36},{32,24... | collective-permute-start | bytes 3932168 | tf_op jit(solution)/shard_map/ppermute | solution.py:23
  5.0 1.3 %copy-start = (bf16[1,512,1280]{2,1,0:T(8,128)(2,1)S(1)}, bf16[1,512,1280]{2,1,0:T(8,128)(2,1)}, u32[]{:S(2)}) copy-start(bf16[1,512,1280]{2,1,0:T(8,128)(2,1)} %param.4) | copy-start | bytes 3932164
  6.3 15.7 %copy-start.3 = (f32[512]{0:T(512)S(1)}, f32[512]{0:T(512)}, u32[]{:S(2)}) copy-start(f32[512]{0:T(512)} %param.6) | copy-start | bytes 6148
  6.3 17.7 %copy-start.1 = (bf16[1,512,1280]{2,1,0:T(8,128)(2,1)S(1)}, bf16[1,512,1280]{2,1,0:T(8,128)(2,1)}, u32[]{:S(2)}) copy-start(bf16[1,512,1280]{2,1,0:T(8,128)(2,1)} %param.4) | copy-start | bytes 3932164
  7.2 15.1 %collective-permute-start.2 = (bf16[256,1280]{1,0:T(8,128)(2,1)}, bf16[256,1280]{1,0:T(8,128)(2,1)S(1)}, u32[]{:S(2)}, u32[]{:S(2)}) collective-permute-start(bf16[256,1280]{1,0:T(8,128)(2,1)} %get-tuple-element.11), channel_id=1, source_target_pairs={{0,4},{4,0},{8,12},{12,8},{16,20},{20,16},{24,28},{28,24},{32,36},... | collective-permute-start | bytes 1966088 | tf_op jit(solution)/shard_map/ppermute | solution.py:23
  19.9 4.0 %collective-permute-start.3 = (bf16[256,1280]{1,0:T(8,128)(2,1)S(1)}, bf16[256,1280]{1,0:T(8,128)(2,1)S(1)}, u32[]{:S(2)}, u32[]{:S(2)}) collective-permute-start(bf16[256,1280]{1,0:T(8,128)(2,1)S(1)} %get-tuple-element.12), channel_id=1, source_target_pairs={{0,4},{4,0},{8,12},{12,8},{16,20},{20,16},{24,28},{28,24},{32,36},... | collective-permute-start | bytes 1966088 | tf_op jit(solution)/shard_map/ppermute | solution.py:23
  26.1 19.2 %collective-permute-start.4 = (bf16[512,1280]{1,0:T(8,128)(2,1)S(1)}, bf16[512,1280]{1,0:T(8,128)(2,1)S(1)}, u32[]{:S(2)}, u32[]{:S(2)}) collective-permute-start(bf16[512,1280]{1,0:T(8,128)(2,1)S(1)} %get-tuple-element.13.refs_5_.refs_4_), channel_id=1, source_target_pairs={{0,508},{4,8},{8,4},{12,16},{16,12},{20,24},{24,20},{28,32},{32,28... | collective-permute-start | bytes 3932168 | tf_op jit(solution)/shard_map/ppermute | solution.py:23
  30.1 29.3 %collective-permute-start.1 = (bf16[512,1280]{1,0:T(8,128)(2,1)}, bf16[512,1280]{1,0:T(8,128)(2,1)S(1)}, u32[]{:S(2)}, u32[]{:S(2)}) collective-permute-start(bf16[512,1280]{1,0:T(8,128)(2,1)} %collective-permute-done.refs_6_), channel_id=1, source_target_pairs={{0,508},{4,8},{8,4},{12,16},{16,12},{20,24},{24,20},{28,32},{32,28... | collective-permute-start | bytes 3932168 | tf_op jit(solution)/shard_map/ppermute | solution.py:23
  47.5 13.3 %collective-permute-start.5 = (bf16[1280,512]{1,0:T(8,128)(2,1)S(1)}, bf16[1280,512]{1,0:T(8,128)(2,1)S(1)}, u32[]{:S(2)}, u32[]{:S(2)}) collective-permute-start(bf16[1280,512]{1,0:T(8,128)(2,1)S(1)} %pairs.5), channel_id=1, source_target_pairs={{0,4},{4,0},{8,12},{12,8},{16,20},{20,16},{24,28},{28,24},{32,36},... | collective-permute-start | bytes 3932168 | tf_op jit(solution)/shard_map/ppermute | solution.py:23
  61.9 42.9 %copy-start.2 = (bf16[1024,512]{1,0:T(8,128)(2,1)S(1)}, bf16[1024,512]{1,0:T(8,128)(2,1)}, u32[]{:S(2)}) copy-start(bf16[1024,512]{1,0:T(8,128)(2,1)} %coeffs.1) | copy-start | bytes 3145732

commit v8 on v7

--- a/solution.py
+++ b/solution.py
@@ -52,15 +52,17 @@
             outs[k][part, :] = value.astype(outs[k].dtype)
 
 
-def first_kernel(steps, *refs):
+def joined_kernel(steps, carried, *refs):
     levels = refs[:4]
-    mine, upper, lower, total, other = refs[4:]
+    left, upper, lower, *totals, out, other = refs[4:]
     half = upper.shape[0]
     other[:half, :] = upper[...]
     other[half:, :] = lower[...]
-    amps = amplitudes(steps, levels, mine, other)
+    amps = amplitudes(steps, levels, left, other)
     for part, value in pair_terms(amps, other):
-        total[part, :] = value
+        if carried:
+            value = value + totals[0][part, :]
+        out[part, :] = value.astype(out.dtype)
 
 
 def split_kernel(mine, upper, lower):
@@ -99,7 +101,7 @@
     out[...] = wide[...].astype(out.dtype)
 
 
-def local_call(kernel, levels, arrays, outs, scratch=(), name=None, flops=1000):
+def local_call(kernel, levels, arrays, outs, scratch=(), name=None):
     vmem = pl.BlockSpec(memory_space=pltpu.VMEM)
     smem = pl.BlockSpec(memory_space=pltpu.SMEM)
     return pl.pallas_call(
@@ -109,7 +111,7 @@
         out_specs=[vmem] * len(outs),
         scratch_shapes=list(scratch),
         compiler_params=pltpu.CompilerParams(vmem_limit_bytes=VMEM_LIMIT),
-        cost_estimate=pl.CostEstimate(flops=flops, bytes_accessed=1000, transcendentals=0),
+        cost_estimate=pl.CostEstimate(flops=1000, bytes_accessed=1000, transcendentals=0),
         name=name,
     )(*levels, *arrays)
 
@@ -118,14 +120,13 @@
     shape = blocks[0].shape[::-1]
     kernel = functools.partial(pairs_kernel, pairs, len(blocks), len(totals))
     outs = [(shape, dtype) for dtype in dtypes]
-    flops = 10**10 if len(pairs) > 1 else 1000
-    return local_call(kernel, levels, [*blocks, *totals], outs, name="pairs", flops=flops)
-
-
-def first_pair(levels, steps, mine, upper, lower):
-    outs = [(mine.shape[::-1], jnp.float32), (mine.shape, mine.dtype)]
-    kernel = functools.partial(first_kernel, steps)
-    return local_call(kernel, levels, [mine, upper, lower], outs, name="first")
+    return local_call(kernel, levels, [*blocks, *totals], outs, name="pairs")
+
+
+def joined_pair(levels, steps, left, halves, totals, dtype, name):
+    outs = [(left.shape[::-1], dtype), (left.shape, left.dtype)]
+    kernel = functools.partial(joined_kernel, steps, len(totals))
+    return local_call(kernel, levels, [left, *halves, *totals], outs, name=name)
 
 
 def last_pair(levels, steps, mine, other, total, arrived):
@@ -205,15 +206,14 @@
     f32, bf16 = jnp.float32, jnp.bfloat16
 
     plus2 = mirrored(mine, count, -2)
-    upper, lower = split(mine)
-    upper, lower = mirrored(upper, count, 1), mirrored(lower, count, 1)
-    total, plus1 = first_pair(levels, (0, 1), mine, upper, lower)
-    minus2 = mirrored(plus1, count, -1)
+    halves = [mirrored(half, count, 1) for half in split(mine)]
+    far_halves = [mirrored(half, count, -1) for half in halves]
+    total, plus1 = joined_pair(levels, (0, 1), mine, halves, [], f32, "first")
     minus3 = mirrored(plus2, count, -1)
     total, beside = pairs_sum(
         levels, [mine, plus1, plus2], [((0, 2), 0, 2), ((1, 2), 1, 2)], [total], [f32, f32]
     )
-    (beside,) = pairs_sum(levels, [plus1, minus2], [((1, -2), 0, 1)], [beside], [bf16])
+    beside, minus2 = joined_pair(levels, (1, -2), plus1, far_halves, [beside], bf16, "beside")
     (total,) = pairs_sum(levels, [mine, minus2], [((0, -2), 0, 1)], [total], [f32])
     arrived = mirrored(beside, count, 1)
     gamma = last_pair(levels, (0, -3), mine, minus3, total, arrived)

time: 108 us -> 108 us (level)
  waiting for transfers between devices: 16.3 us -> 7.22 us
  blocking collectives: 42.9 us -> 47.5 us
  starting transfers between devices: 29.4 us -> 33.8 us
    ppermute x6 -> x7, waiting for transfers between devices: 16.3 us -> 7.22 us  [mirrored(): return lax.ppermute(block, OCC, route)]
    all_to_all x1, blocking collectives: 42.9 us -> 47.5 us  [on_device(): lax.all_to_all(gamma.reshape(count, -1, LANES), OCC, 0, 0, tiled=True)]
    ppermute x6 -> x7, starting transfers between devices: 29.4 us -> 33.8 us  [mirrored(): return lax.ppermute(block, OCC, route)]
  transfers between devices with their start and end apart: 6 -> 7, of which waited for: 4 -> 4; matrix products, arithmetic and copies ran while one was open for 0% -> 0% of each run, Pallas kernels for 12% -> 12%
where the time goes in v8:
time: 108 us; the launch traced here: 107 us
  blocking collectives  47.5 us (44%)
  starting transfers between devices  33.8 us (31%)
  Pallas kernels  16.7 us (15%)
  waiting for transfers between devices  7.22 us (7%)
  local copies, waits for them, and re-layouts  1.57 us (1%)
    all_to_all x1, blocking collectives, on_device(): lax.all_to_all(gamma.reshape(count, -1, LANES), OCC, 0, 0, tiled=True)  47.5 us
    ppermute x7, starting transfers between devices, mirrored(): return lax.ppermute(block, OCC, route)  33.8 us
    pallas_call x5, Pallas kernels, local_call(): pl.pallas_call(kernel, out_shape=[jax.ShapeDtypeStruct(shape, dtype) for...  12.9 us
    ppermute x7, waiting for transfers between devices, mirrored(): return lax.ppermute(block, OCC, route)  7.22 us
    pallas_call x1, Pallas kernels, back_transform(): pl.pallas_call(functools.partial(back_kernel, chunk), out_shape=jax.Shape...  2.66 us
  transfers between devices with their start and end apart: 7, of which 4 were waited for; matrix products, arithmetic and copies ran while one was open for 0% of the time, Pallas kernels for 12%

profile of v8, /device:TPU:1, one launch (start us, length us, event | category | flops | bytes accessed | tf_op | source)
XLA Modules:
  0.0 107.1 jit_solution(17703848182998187422)
XLA Ops:
  0.0 0.0 copy-start.4
  0.0 4.9 %collective-permute-start = (bf16[512,1280]{1,0:T(8,128)(2,1)}, bf16[512,1280]{1,0:T(8,128)(2,1)S(1)}, u32[]{:S(2)}, u32[]{:S(2)}) collective-permute-start(bf16[512,1280]{1,0:T(8,128)(2,1)} %bitcast.12), channel_id=1, source_target_pairs={{0,504},{4,12},{8,0},{12,20},{16,8},{20,28},{24,16},{28,36},{32,24... | collective-permute-start | bytes 3932168 | tf_op jit(solution)/shard_map/ppermute | solution.py:23
  5.0 0.0 copy-start
  5.0 1.3 %copy-done = bf16[1,512,1280]{2,1,0:T(8,128)(2,1)S(1)} copy-done((bf16[1,512,1280]{2,1,0:T(8,128)(2,1)S(1)}, bf16[1,512,1280]{2,1,0:T(8,128)(2,1)}, u32[]{:S(2)}) %copy-start) | copy-done | bytes 1310744
  6.3 0.0 copy-start.3
  6.3 0.0 copy-start.1
  6.3 0.1 split.1
  6.4 12.9 %collective-permute-start.2 = (bf16[256,1280]{1,0:T(8,128)(2,1)S(1)}, bf16[256,1280]{1,0:T(8,128)(2,1)S(1)}, u32[]{:S(2)}, u32[]{:S(2)}) collective-permute-start(bf16[256,1280]{1,0:T(8,128)(2,1)S(1)} %get-tuple-element.13), channel_id=1, source_target_pairs={{0,4},{4,0},{8,12},{12,8},{16,20},{20,16},{24,28},{28,24},{32,36},... | collective-permute-start | bytes 1966088 | tf_op jit(solution)/shard_map/ppermute | solution.py:23
  19.3 1.9 %collective-permute-start.3 = (bf16[256,1280]{1,0:T(8,128)(2,1)S(1)}, bf16[256,1280]{1,0:T(8,128)(2,1)}, u32[]{:S(2)}, u32[]{:S(2)}) collective-permute-start(bf16[256,1280]{1,0:T(8,128)(2,1)S(1)} %get-tuple-element.14), channel_id=1, source_target_pairs={{0,4},{4,0},{8,12},{12,8},{16,20},{20,16},{24,28},{28,24},{32,36},... | collective-permute-start | bytes 1966088 | tf_op jit(solution)/shard_map/ppermute | solution.py:23
  21.2 0.0 collective-permute-done.2.refs_5_
  21.2 1.9 %collective-permute-start.4 = (bf16[256,1280]{1,0:T(8,128)(2,1)S(1)}, bf16[256,1280]{1,0:T(8,128)(2,1)}, u32[]{:S(2)}, u32[]{:S(2)}) collective-permute-start(bf16[256,1280]{1,0:T(8,128)(2,1)S(1)} %collective-permute-done.2.refs_5_), channel_id=1, source_target_pairs={{0,508},{4,8},{8,4},{12,16},{16,12},{20,24},{24,20},{28,32},{32,28... | collective-permute-start | bytes 1966088 | tf_op jit(solution)/shard_map/ppermute | solution.py:23
  23.1 0.3 collective-permute-done.3.refs_6_
  23.4 3.4 %collective-permute-start.5 = (bf16[256,1280]{1,0:T(8,128)(2,1)}, bf16[256,1280]{1,0:T(8,128)(2,1)}, u32[]{:S(2)}, u32[]{:S(2)}) collective-permute-start(bf16[256,1280]{1,0:T(8,128)(2,1)} %collective-permute-done.3.refs_6_), channel_id=1, source_target_pairs={{0,508},{4,8},{8,4},{12,16},{16,12},{20,24},{24,20},{28,32},{32,28... | collective-permute-start | bytes 1966088 | tf_op jit(solution)/shard_map/ppermute | solution.py:23
  26.9 0.0 copy-done.3
  26.9 0.1 copy.5.refs_2_
  27.1 0.1 stack.31.refs_0_
  27.2 0.0 copy-done.4
  27.2 0.0 copy-done.1
  27.2 2.7 %first.1 = (f32[1280,512]{1,0:T(8,128)S(1)}, bf16[512,1280]{1,0:T(8,128)(2,1)S(1)}) custom-call(s32[7]{0:T(128)S(1)} %stack.31.refs_0_, f32[128]{0:T(128)S(1)} %copy-done.4, f32[512,1]{1,0:T(8,128)S(1)} %copy.5.refs_2_, f32[1,512]{1,0:T(1,128)S(1)} %bitcast.21, bf16[512,1280]{1,0:T(8,128)(2,1)S(1)} %bitcast.14, ...), custom_call_target="tpu_custom_call" | custom-call | flops 1000 | bytes 1000 | tf_op jit(solution)/shard_map/first/pallas_call | solution.py:107
  30.0 0.1 collective-permute-done.refs_6_
  30.0 2.1 %collective-permute-start.1 = (bf16[512,1280]{1,0:T(8,128)(2,1)S(1)}, bf16[512,1280]{1,0:T(8,128)(2,1)S(1)}, u32[]{:S(2)}, u32[]{:S(2)}) collective-permute-start(bf16[512,1280]{1,0:T(8,128)(2,1)S(1)} %collective-permute-done.refs_6_), channel_id=1, source_target_pairs={{0,508},{4,8},{8,4},{12,16},{16,12},{20,24},{24,20},{28,32},{32,28... | collective-permute-start | bytes 3932168 | tf_op jit(solution)/shard_map/ppermute | solution.py:23
  32.1 3.7 %pairs.2 = (f32[1280,512]{1,0:T(8,128)S(1)}, f32[1280,512]{1,0:T(8,128)S(1)}) custom-call(s32[7]{0:T(128)S(1)} %stack.31.refs_0_, f32[128]{0:T(128)S(1)} %copy-done.4, f32[512,1]{1,0:T(8,128)S(1)} %copy.5.refs_2_, f32[1,512]{1,0:T(1,128)S(1)} %bitcast.22, bf16[512,1280]{1,0:T(8,128)(2,1)S(1)} %bitcast.15, ...), custom_call_target="tpu_custom_call" | custom-call | flops 1000 | bytes 1000 | tf_op jit(solution)/shard_map/pairs/pallas_call | solution.py:107
  35.8 0.0 collective-permute-done.4.refs_5_
  35.8 4.7 %collective-permute-done.5.refs_6_ = bf16[256,1280]{1,0:T(8,128)(2,1)} collective-permute-done((bf16[256,1280]{1,0:T(8,128)(2,1)}, bf16[256,1280]{1,0:T(8,128)(2,1)}, u32[]{:S(2)}, u32[]{:S(2)}) %collective-permute-start.5) | collective-permute-done | bytes 655392 | tf_op jit(solution)/shard_map/ppermute | solution.py:23
  40.5 2.9 %beside.1 = (bf16[1280,512]{1,0:T(8,128)(2,1)S(1)}, bf16[512,1280]{1,0:T(8,128)(2,1)S(1)}) custom-call(s32[7]{0:T(128)S(1)} %stack.31.refs_0_, f32[128]{0:T(128)S(1)} %copy-done.4, f32[512,1]{1,0:T(8,128)S(1)} %copy.5.refs_2_, f32[1,512]{1,0:T(1,128)S(1)} %bitcast.23, bf16[512,1280]{1,0:T(8,128)(2,1)S(1)} %get-tuple-element.15.refs_5_.refs_4_, ...), custom_call_target="tpu_custom_call" | custom-call | flops 1000 | bytes 1000 | tf_op jit(solution)/shard_map/beside/pallas_call | solution.py:107
  43.5 6.6 %collective-permute-start.6 = (bf16[1280,512]{1,0:T(8,128)(2,1)S(1)}, bf16[1280,512]{1,0:T(8,128)(2,1)S(1)}, u32[]{:S(2)}, u32[]{:S(2)}) collective-permute-start(bf16[1280,512]{1,0:T(8,128)(2,1)S(1)} %get-tuple-element.20), channel_id=1, source_target_pairs={{0,4},{4,0},{8,12},{12,8},{16,20},{20,16},{24,28},{28,24},{32,36},... | collective-permute-start | bytes 3932168 | tf_op jit(solution)/shard_map/ppermute | solution.py:23
  50.1 2.2 %pairs.3.total = f32[1280,512]{1,0:T(8,128)S(1)} custom-call(s32[7]{0:T(128)S(1)} %stack.31.refs_0_, f32[128]{0:T(128)S(1)} %copy-done.4, f32[512,1]{1,0:T(8,128)S(1)} %copy.5.refs_2_, f32[1,512]{1,0:T(1,128)S(1)} %bitcast.24, bf16[512,1280]{1,0:T(8,128)(2,1)S(1)} %bitcast.16, bf16[512,1280]{1,0:T(8,128)(2,1)S(1)} %get-tuple-element.18.refs_5_, ...), custom_call_target="tpu_custom_call" | custom-call | flops 1000 | bytes 1000 | tf_op jit(solution)/shard_map/pairs/pallas_call | solution.py:107
  52.3 2.2 %collective-permute-done.1.refs_5_.other = bf16[512,1280]{1,0:T(8,128)(2,1)S(1)} collective-permute-done((bf16[512,1280]{1,0:T(8,128)(2,1)S(1)}, bf16[512,1280]{1,0:T(8,128)(2,1)S(1)}, u32[]{:S(2)}, u32[]{:S(2)}) %collective-permute-start.1) | collective-permute-done | bytes 1310752 | tf_op jit(solution)/shard_map/ppermute | solution.py:23
  54.5 1.4 %amps.1 = bf16[512,512]{1,0:T(8,128)(2,1)S(1)} custom-call(s32[7]{0:T(128)S(1)} %stack.31.refs_0_, f32[128]{0:T(128)S(1)} %copy-done.4, f32[512,1]{1,0:T(8,128)S(1)} %copy.5.refs_2_, f32[1,512]{1,0:T(1,128)S(1)} %bitcast.25, bf16[512,1280]{1,0:T(8,128)(2,1)S(1)} %bitcast.17, bf16[512,1280]{1,0:T(8,128)(2,1)S(1)} %collective-permute-done.1.refs_5_.other), custom_call_target="tpu_custom_call" | custom-call | flops 1000 | bytes 1000 | tf_op jit(solution)/shard_map/amps/pallas_call | solution.py:107
  55.9 0.0 collective-permute-done.6.arrived
  55.9 1.1 last.1
  57.0 0.0 copy-start.2
  57.0 47.5 %all_to_all.5 = bf16[128,40,128]{2,1,0:T(8,128)(2,1)S(1)} all-to-all(bf16[128,40,128]{2,1,0:T(8,128)(2,1)S(1)} %bitcast.18), channel_id=1, replica_groups=mesh['occ_0'=2,'occ_1'=4,'occ_2'=8,'occ_3'=2,'frag'=4] {'occ_0','occ_1',..., dimensions={0} | all-to-all | bytes 2621440 | tf_op jit(solution)/shard_map/all_to_all | solution.py:220
  104.5 0.0 copy-done.2
  104.5 2.7 %back.1 = bf16[10,128,1024]{2,1,0:T(8,128)(2,1)} custom-call(bf16[5120,128]{1,0:T(8,128)(2,1)S(1)} %bitcast.19, bf16[1024,512]{1,0:T(8,128)(2,1)S(1)} %copy-done.2), custom_call_target="tpu_custom_call" | custom-call | flops 1342177280 | bytes 3932160 | tf_op jit(solution)/shard_map/back/pallas_call | solution.py:178
Async XLA Ops:
  0.0 27.2 %copy-start.4 = (f32[128]{0:T(128)S(1)}, f32[128]{0:T(128)}, u32[]{:S(2)}) copy-start(f32[128]{0:T(128)} %refs_1_.9) | copy-start | bytes 1540
  0.0 30.0 %collective-permute-start = (bf16[512,1280]{1,0:T(8,128)(2,1)}, bf16[512,1280]{1,0:T(8,128)(2,1)S(1)}, u32[]{:S(2)}, u32[]{:S(2)}) collective-permute-start(bf16[512,1280]{1,0:T(8,128)(2,1)} %bitcast.12), channel_id=1, source_target_pairs={{0,504},{4,12},{8,0},{12,20},{16,8},{20,28},{24,16},{28,36},{32,24... | collective-permute-start | bytes 3932168 | tf_op jit(solution)/shard_map/ppermute | solution.py:23
  5.0 1.3 %copy-start = (bf16[1,512,1280]{2,1,0:T(8,128)(2,1)S(1)}, bf16[1,512,1280]{2,1,0:T(8,128)(2,1)}, u32[]{:S(2)}) copy-start(bf16[1,512,1280]{2,1,0:T(8,128)(2,1)} %param.4) | copy-start | bytes 3932164
  6.3 20.6 %copy-start.3 = (f32[512]{0:T(512)S(1)}, f32[512]{0:T(512)}, u32[]{:S(2)}) copy-start(f32[512]{0:T(512)} %param.6) | copy-start | bytes 6148
  6.3 20.9 %copy-start.1 = (bf16[1,512,1280]{2,1,0:T(8,128)(2,1)S(1)}, bf16[1,512,1280]{2,1,0:T(8,128)(2,1)}, u32[]{:S(2)}) copy-start(bf16[1,512,1280]{2,1,0:T(8,128)(2,1)} %param.4) | copy-start | bytes 3932164
  6.4 14.8 %collective-permute-start.2 = (bf16[256,1280]{1,0:T(8,128)(2,1)S(1)}, bf16[256,1280]{1,0:T(8,128)(2,1)S(1)}, u32[]{:S(2)}, u32[]{:S(2)}) collective-permute-start(bf16[256,1280]{1,0:T(8,128)(2,1)S(1)} %get-tuple-element.13), channel_id=1, source_target_pairs={{0,4},{4,0},{8,12},{12,8},{16,20},{20,16},{24,28},{28,24},{32,36},... | collective-permute-start | bytes 1966088 | tf_op jit(solution)/shard_map/ppermute | solution.py:23
  19.3 4.1 %collective-permute-start.3 = (bf16[256,1280]{1,0:T(8,128)(2,1)S(1)}, bf16[256,1280]{1,0:T(8,128)(2,1)}, u32[]{:S(2)}, u32[]{:S(2)}) collective-permute-start(bf16[256,1280]{1,0:T(8,128)(2,1)S(1)} %get-tuple-element.14), channel_id=1, source_target_pairs={{0,4},{4,0},{8,12},{12,8},{16,20},{20,16},{24,28},{28,24},{32,36},... | collective-permute-start | bytes 1966088 | tf_op jit(solution)/shard_map/ppermute | solution.py:23
  21.2 14.6 %collective-permute-start.4 = (bf16[256,1280]{1,0:T(8,128)(2,1)S(1)}, bf16[256,1280]{1,0:T(8,128)(2,1)}, u32[]{:S(2)}, u32[]{:S(2)}) collective-permute-start(bf16[256,1280]{1,0:T(8,128)(2,1)S(1)} %collective-permute-done.2.refs_5_), channel_id=1, source_target_pairs={{0,508},{4,8},{8,4},{12,16},{16,12},{20,24},{24,20},{28,32},{32,28... | collective-permute-start | bytes 1966088 | tf_op jit(solution)/shard_map/ppermute | solution.py:23
  23.4 17.1 %collective-permute-start.5 = (bf16[256,1280]{1,0:T(8,128)(2,1)}, bf16[256,1280]{1,0:T(8,128)(2,1)}, u32[]{:S(2)}, u32[]{:S(2)}) collective-permute-start(bf16[256,1280]{1,0:T(8,128)(2,1)} %collective-permute-done.3.refs_6_), channel_id=1, source_target_pairs={{0,508},{4,8},{8,4},{12,16},{16,12},{20,24},{24,20},{28,32},{32,28... | collective-permute-start | bytes 1966088 | tf_op jit(solution)/shard_map/ppermute | solution.py:23
  30.0 24.4 %collective-permute-start.1 = (bf16[512,1280]{1,0:T(8,128)(2,1)S(1)}, bf16[512,1280]{1,0:T(8,128)(2,1)S(1)}, u32[]{:S(2)}, u32[]{:S(2)}) collective-permute-start(bf16[512,1280]{1,0:T(8,128)(2,1)S(1)} %collective-permute-done.refs_6_), channel_id=1, source_target_pairs={{0,508},{4,8},{8,4},{12,16},{16,12},{20,24},{24,20},{28,32},{32,28... | collective-permute-start | bytes 3932168 | tf_op jit(solution)/shard_map/ppermute | solution.py:23
  43.5 12.4 %collective-permute-start.6 = (bf16[1280,512]{1,0:T(8,128)(2,1)S(1)}, bf16[1280,512]{1,0:T(8,128)(2,1)S(1)}, u32[]{:S(2)}, u32[]{:S(2)}) collective-permute-start(bf16[1280,512]{1,0:T(8,128)(2,1)S(1)} %get-tuple-element.20), channel_id=1, source_target_pairs={{0,4},{4,0},{8,12},{12,8},{16,20},{20,16},{24,28},{28,24},{32,36},... | collective-permute-start | bytes 3932168 | tf_op jit(solution)/shard_map/ppermute | solution.py:23
  57.0 47.5 %copy-start.2 = (bf16[1024,512]{1,0:T(8,128)(2,1)S(1)}, bf16[1024,512]{1,0:T(8,128)(2,1)}, u32[]{:S(2)}) copy-start(bf16[1024,512]{1,0:T(8,128)(2,1)} %coeffs.1) | copy-start | bytes 3145732

commit v9 on v8

--- a/solution.py
+++ b/solution.py
@@ -63,6 +63,23 @@
         if carried:
             value = value + totals[0][part, :]
         out[part, :] = value.astype(out.dtype)
+
+
+def near_kernel(*refs):
+    levels = refs[:4]
+    mine, upper, lower, plus2, total, beside, plus1 = refs[4:]
+    half = upper.shape[0]
+    plus1[:half, :] = upper[...]
+    plus1[half:, :] = lower[...]
+    amps = amplitudes((0, 1), levels, mine, plus1)
+    for part, value in pair_terms(amps, plus1):
+        total[part, :] = value
+    amps = amplitudes((0, 2), levels, mine, plus2)
+    for part, value in pair_terms(amps, plus2):
+        total[part, :] = total[part, :] + value
+    amps = amplitudes((1, 2), levels, plus1, plus2)
+    for part, value in pair_terms(amps, plus2):
+        beside[part, :] = value
 
 
 def split_kernel(mine, upper, lower):
@@ -208,10 +225,11 @@
     plus2 = mirrored(mine, count, -2)
     halves = [mirrored(half, count, 1) for half in split(mine)]
     far_halves = [mirrored(half, count, -1) for half in halves]
-    total, plus1 = joined_pair(levels, (0, 1), mine, halves, [], f32, "first")
     minus3 = mirrored(plus2, count, -1)
-    total, beside = pairs_sum(
-        levels, [mine, plus1, plus2], [((0, 2), 0, 2), ((1, 2), 1, 2)], [total], [f32, f32]
+    shape = (mine.shape[::-1], f32)
+    outs = [shape, shape, (mine.shape, mine.dtype)]
+    total, beside, plus1 = local_call(
+        near_kernel, levels, [mine, *halves, plus2], outs, name="first"
     )
     beside, minus2 = joined_pair(levels, (1, -2), plus1, far_halves, [beside], bf16, "beside")
     (total,) = pairs_sum(levels, [mine, minus2], [((0, -2), 0, 1)], [total], [f32])

time: 108 us -> 108 us (level)
    pallas_call x5 -> x4, Pallas kernels: 12.9 us -> 12.2 us  [local_call(): pl.pallas_call(kernel, out_shape=[jax.ShapeDtypeStruct(shape, dtype) for...]
  transfers between devices with their start and end apart: 7 -> 7, of which waited for: 4 -> 4; matrix products, arithmetic and copies ran while one was open for 0% -> 0% of each run, Pallas kernels for 12% -> 11%
where the time goes in v9:
time: 108 us; the launch traced here: 107 us
  blocking collectives  47.5 us (44%)
  starting transfers between devices  33.6 us (31%)
  Pallas kernels  16 us (15%)
  waiting for transfers between devices  8.11 us (8%)
  local copies, waits for them, and re-layouts  1.57 us (1%)
    all_to_all x1, blocking collectives, on_device(): lax.all_to_all(gamma.reshape(count, -1, LANES), OCC, 0, 0, tiled=True)  47.5 us
    ppermute x7, starting transfers between devices, mirrored(): return lax.ppermute(block, OCC, route)  33.6 us
    pallas_call x4, Pallas kernels, local_call(): pl.pallas_call(kernel, out_shape=[jax.ShapeDtypeStruct(shape, dtype) for...  12.2 us
    ppermute x7, waiting for transfers between devices, mirrored(): return lax.ppermute(block, OCC, route)  8.11 us
    pallas_call x1, Pallas kernels, back_transform(): pl.pallas_call(functools.partial(back_kernel, chunk), out_shape=jax.Shape...  2.66 us
  transfers between devices with their start and end apart: 7, of which 4 were waited for; matrix products, arithmetic and copies ran while one was open for 0% of the time, Pallas kernels for 11%

profile of v9, /device:TPU:1, one launch (start us, length us, event | category | flops | bytes accessed | tf_op | source)
XLA Modules:
  0.0 107.1 jit_solution(18154991993472646317)
XLA Ops:
  0.0 0.0 copy-start.4
  0.0 4.9 %collective-permute-start = (bf16[512,1280]{1,0:T(8,128)(2,1)}, bf16[512,1280]{1,0:T(8,128)(2,1)S(1)}, u32[]{:S(2)}, u32[]{:S(2)}) collective-permute-start(bf16[512,1280]{1,0:T(8,128)(2,1)} %bitcast.12), channel_id=1, source_target_pairs={{0,504},{4,12},{8,0},{12,20},{16,8},{20,28},{24,16},{28,36},{32,24... | collective-permute-start | bytes 3932168 | tf_op jit(solution)/shard_map/ppermute | solution.py:23
  5.0 0.0 copy-start
  5.0 1.3 %copy-done = bf16[1,512,1280]{2,1,0:T(8,128)(2,1)S(1)} copy-done((bf16[1,512,1280]{2,1,0:T(8,128)(2,1)S(1)}, bf16[1,512,1280]{2,1,0:T(8,128)(2,1)}, u32[]{:S(2)}) %copy-start) | copy-done | bytes 1310744
  6.3 0.0 copy-start.3
  6.3 0.0 copy-start.1
  6.3 0.1 split.1
  6.4 12.9 %collective-permute-start.2 = (bf16[256,1280]{1,0:T(8,128)(2,1)S(1)}, bf16[256,1280]{1,0:T(8,128)(2,1)S(1)}, u32[]{:S(2)}, u32[]{:S(2)}) collective-permute-start(bf16[256,1280]{1,0:T(8,128)(2,1)S(1)} %get-tuple-element.12), channel_id=1, source_target_pairs={{0,4},{4,0},{8,12},{12,8},{16,20},{20,16},{24,28},{28,24},{32,36},... | collective-permute-start | bytes 1966088 | tf_op jit(solution)/shard_map/ppermute | solution.py:23
  19.3 1.9 %collective-permute-start.3 = (bf16[256,1280]{1,0:T(8,128)(2,1)S(1)}, bf16[256,1280]{1,0:T(8,128)(2,1)}, u32[]{:S(2)}, u32[]{:S(2)}) collective-permute-start(bf16[256,1280]{1,0:T(8,128)(2,1)S(1)} %get-tuple-element.13), channel_id=1, source_target_pairs={{0,4},{4,0},{8,12},{12,8},{16,20},{20,16},{24,28},{28,24},{32,36},... | collective-permute-start | bytes 1966088 | tf_op jit(solution)/shard_map/ppermute | solution.py:23
  21.2 0.0 collective-permute-done.2.refs_5_
  21.2 1.9 %collective-permute-start.4 = (bf16[256,1280]{1,0:T(8,128)(2,1)S(1)}, bf16[256,1280]{1,0:T(8,128)(2,1)}, u32[]{:S(2)}, u32[]{:S(2)}) collective-permute-start(bf16[256,1280]{1,0:T(8,128)(2,1)S(1)} %collective-permute-done.2.refs_5_), channel_id=1, source_target_pairs={{0,508},{4,8},{8,4},{12,16},{16,12},{20,24},{24,20},{28,32},{32,28... | collective-permute-start | bytes 1966088 | tf_op jit(solution)/shard_map/ppermute | solution.py:23
  23.1 0.3 collective-permute-done.3.refs_6_
  23.4 3.4 %collective-permute-start.5 = (bf16[256,1280]{1,0:T(8,128)(2,1)}, bf16[256,1280]{1,0:T(8,128)(2,1)}, u32[]{:S(2)}, u32[]{:S(2)}) collective-permute-start(bf16[256,1280]{1,0:T(8,128)(2,1)} %collective-permute-done.3.refs_6_), channel_id=1, source_target_pairs={{0,508},{4,8},{8,4},{12,16},{16,12},{20,24},{24,20},{28,32},{32,28... | collective-permute-start | bytes 1966088 | tf_op jit(solution)/shard_map/ppermute | solution.py:23
  26.9 0.0 copy-done.3
  26.9 0.1 copy.5.refs_2_
  27.1 0.1 stack.31.refs_0_
  27.2 2.8 %collective-permute-done.refs_7_ = bf16[512,1280]{1,0:T(8,128)(2,1)S(1)} collective-permute-done((bf16[512,1280]{1,0:T(8,128)(2,1)}, bf16[512,1280]{1,0:T(8,128)(2,1)S(1)}, u32[]{:S(2)}, u32[]{:S(2)}) %collective-permute-start) | collective-permute-done | bytes 1310752 | tf_op jit(solution)/shard_map/ppermute | solution.py:23
  30.0 1.9 %collective-permute-start.1 = (bf16[512,1280]{1,0:T(8,128)(2,1)S(1)}, bf16[512,1280]{1,0:T(8,128)(2,1)S(1)}, u32[]{:S(2)}, u32[]{:S(2)}) collective-permute-start(bf16[512,1280]{1,0:T(8,128)(2,1)S(1)} %collective-permute-done.refs_7_), channel_id=1, source_target_pairs={{0,508},{4,8},{8,4},{12,16},{16,12},{20,24},{24,20},{28,32},{32,28... | collective-permute-start | bytes 3932168 | tf_op jit(solution)/shard_map/ppermute | solution.py:23
  31.9 0.0 copy-done.4
  32.0 0.0 copy-done.1
  32.0 5.7 %first.1 = (f32[1280,512]{1,0:T(8,128)S(1)}, f32[1280,512]{1,0:T(8,128)S(1)}, bf16[512,1280]{1,0:T(8,128)(2,1)S(1)}) custom-call(s32[7]{0:T(128)S(1)} %stack.31.refs_0_, f32[128]{0:T(128)S(1)} %copy-done.4, f32[512,1]{1,0:T(8,128)S(1)} %copy.5.refs_2_, f32[1,512]{1,0:T(1,128)S(1)} %bitcast.20, bf16[512,1280]{1,0:T(8,128)(2,1)S(1)} %bitcast.14, ...), custom_call_target="tpu_custom_call" | custom-call | flops 1000 | bytes 1000 | tf_op jit(solution)/shard_map/first/pallas_call | solution.py:124
  37.6 0.0 collective-permute-done.4.refs_5_
  37.6 2.9 %collective-permute-done.5.refs_6_ = bf16[256,1280]{1,0:T(8,128)(2,1)} collective-permute-done((bf16[256,1280]{1,0:T(8,128)(2,1)}, bf16[256,1280]{1,0:T(8,128)(2,1)}, u32[]{:S(2)}, u32[]{:S(2)}) %collective-permute-start.5) | collective-permute-done | bytes 655392 | tf_op jit(solution)/shard_map/ppermute | solution.py:23
  40.5 2.9 %beside.1 = (bf16[1280,512]{1,0:T(8,128)(2,1)S(1)}, bf16[512,1280]{1,0:T(8,128)(2,1)S(1)}) custom-call(s32[7]{0:T(128)S(1)} %stack.31.refs_0_, f32[128]{0:T(128)S(1)} %copy-done.4, f32[512,1]{1,0:T(8,128)S(1)} %copy.5.refs_2_, f32[1,512]{1,0:T(1,128)S(1)} %bitcast.21, bf16[512,1280]{1,0:T(8,128)(2,1)S(1)} %get-tuple-element.14.refs_4_, ...), custom_call_target="tpu_custom_call" | custom-call | flops 1000 | bytes 1000 | tf_op jit(solution)/shard_map/beside/pallas_call | solution.py:124
  43.5 6.6 %collective-permute-start.6 = (bf16[1280,512]{1,0:T(8,128)(2,1)S(1)}, bf16[1280,512]{1,0:T(8,128)(2,1)S(1)}, u32[]{:S(2)}, u32[]{:S(2)}) collective-permute-start(bf16[1280,512]{1,0:T(8,128)(2,1)S(1)} %get-tuple-element.18), channel_id=1, source_target_pairs={{0,4},{4,0},{8,12},{12,8},{16,20},{20,16},{24,28},{28,24},{32,36},... | collective-permute-start | bytes 3932168 | tf_op jit(solution)/shard_map/ppermute | solution.py:23
  50.1 2.2 %pairs.1.total = f32[1280,512]{1,0:T(8,128)S(1)} custom-call(s32[7]{0:T(128)S(1)} %stack.31.refs_0_, f32[128]{0:T(128)S(1)} %copy-done.4, f32[512,1]{1,0:T(8,128)S(1)} %copy.5.refs_2_, f32[1,512]{1,0:T(1,128)S(1)} %bitcast.22, bf16[512,1280]{1,0:T(8,128)(2,1)S(1)} %bitcast.15, bf16[512,1280]{1,0:T(8,128)(2,1)S(1)} %get-tuple-element.16.refs_5_, ...), custom_call_target="tpu_custom_call" | custom-call | flops 1000 | bytes 1000 | tf_op jit(solution)/shard_map/pairs/pallas_call | solution.py:124
  52.3 2.2 %collective-permute-done.1.refs_5_.other = bf16[512,1280]{1,0:T(8,128)(2,1)S(1)} collective-permute-done((bf16[512,1280]{1,0:T(8,128)(2,1)S(1)}, bf16[512,1280]{1,0:T(8,128)(2,1)S(1)}, u32[]{:S(2)}, u32[]{:S(2)}) %collective-permute-start.1) | collective-permute-done | bytes 1310752 | tf_op jit(solution)/shard_map/ppermute | solution.py:23
  54.5 1.4 %amps.1 = bf16[512,512]{1,0:T(8,128)(2,1)S(1)} custom-call(s32[7]{0:T(128)S(1)} %stack.31.refs_0_, f32[128]{0:T(128)S(1)} %copy-done.4, f32[512,1]{1,0:T(8,128)S(1)} %copy.5.refs_2_, f32[1,512]{1,0:T(1,128)S(1)} %bitcast.23, bf16[512,1280]{1,0:T(8,128)(2,1)S(1)} %bitcast.16, bf16[512,1280]{1,0:T(8,128)(2,1)S(1)} %collective-permute-done.1.refs_5_.other), custom_call_target="tpu_custom_call" | custom-call | flops 1000 | bytes 1000 | tf_op jit(solution)/shard_map/amps/pallas_call | solution.py:124
  55.9 0.0 collective-permute-done.6.arrived
  55.9 1.0 last.1
  57.0 0.0 copy-start.2
  57.0 47.5 %all_to_all.5 = bf16[128,40,128]{2,1,0:T(8,128)(2,1)S(1)} all-to-all(bf16[128,40,128]{2,1,0:T(8,128)(2,1)S(1)} %bitcast.17), channel_id=1, replica_groups=mesh['occ_0'=2,'occ_1'=4,'occ_2'=8,'occ_3'=2,'frag'=4] {'occ_0','occ_1',..., dimensions={0} | all-to-all | bytes 2621440 | tf_op jit(solution)/shard_map/all_to_all | solution.py:238
  104.5 0.0 copy-done.2
  104.5 2.7 %back.1 = bf16[10,128,1024]{2,1,0:T(8,128)(2,1)} custom-call(bf16[5120,128]{1,0:T(8,128)(2,1)S(1)} %bitcast.18, bf16[1024,512]{1,0:T(8,128)(2,1)S(1)} %copy-done.2), custom_call_target="tpu_custom_call" | custom-call | flops 1342177280 | bytes 3932160 | tf_op jit(solution)/shard_map/back/pallas_call | solution.py:195
Async XLA Ops:
  0.0 31.9 %copy-start.4 = (f32[128]{0:T(128)S(1)}, f32[128]{0:T(128)}, u32[]{:S(2)}) copy-start(f32[128]{0:T(128)} %refs_1_.7) | copy-start | bytes 1540
  0.0 30.0 %collective-permute-start = (bf16[512,1280]{1,0:T(8,128)(2,1)}, bf16[512,1280]{1,0:T(8,128)(2,1)S(1)}, u32[]{:S(2)}, u32[]{:S(2)}) collective-permute-start(bf16[512,1280]{1,0:T(8,128)(2,1)} %bitcast.12), channel_id=1, source_target_pairs={{0,504},{4,12},{8,0},{12,20},{16,8},{20,28},{24,16},{28,36},{32,24... | collective-permute-start | bytes 3932168 | tf_op jit(solution)/shard_map/ppermute | solution.py:23
  5.0 1.3 %copy-start = (bf16[1,512,1280]{2,1,0:T(8,128)(2,1)S(1)}, bf16[1,512,1280]{2,1,0:T(8,128)(2,1)}, u32[]{:S(2)}) copy-start(bf16[1,512,1280]{2,1,0:T(8,128)(2,1)} %param.4) | copy-start | bytes 3932164
  6.3 20.6 %copy-start.3 = (f32[512]{0:T(512)S(1)}, f32[512]{0:T(512)}, u32[]{:S(2)}) copy-start(f32[512]{0:T(512)} %param.6) | copy-start | bytes 6148
  6.3 25.7 %copy-start.1 = (bf16[1,512,1280]{2,1,0:T(8,128)(2,1)S(1)}, bf16[1,512,1280]{2,1,0:T(8,128)(2,1)}, u32[]{:S(2)}) copy-start(bf16[1,512,1280]{2,1,0:T(8,128)(2,1)} %param.4) | copy-start | bytes 3932164
  6.4 14.8 %collective-permute-start.2 = (bf16[256,1280]{1,0:T(8,128)(2,1)S(1)}, bf16[256,1280]{1,0:T(8,128)(2,1)S(1)}, u32[]{:S(2)}, u32[]{:S(2)}) collective-permute-start(bf16[256,1280]{1,0:T(8,128)(2,1)S(1)} %get-tuple-element.12), channel_id=1, source_target_pairs={{0,4},{4,0},{8,12},{12,8},{16,20},{20,16},{24,28},{28,24},{32,36},... | collective-permute-start | bytes 1966088 | tf_op jit(solution)/shard_map/ppermute | solution.py:23
  19.3 4.1 %collective-permute-start.3 = (bf16[256,1280]{1,0:T(8,128)(2,1)S(1)}, bf16[256,1280]{1,0:T(8,128)(2,1)}, u32[]{:S(2)}, u32[]{:S(2)}) collective-permute-start(bf16[256,1280]{1,0:T(8,128)(2,1)S(1)} %get-tuple-element.13), channel_id=1, source_target_pairs={{0,4},{4,0},{8,12},{12,8},{16,20},{20,16},{24,28},{28,24},{32,36},... | collective-permute-start | bytes 1966088 | tf_op jit(solution)/shard_map/ppermute | solution.py:23
  21.2 16.4 %collective-permute-start.4 = (bf16[256,1280]{1,0:T(8,128)(2,1)S(1)}, bf16[256,1280]{1,0:T(8,128)(2,1)}, u32[]{:S(2)}, u32[]{:S(2)}) collective-permute-start(bf16[256,1280]{1,0:T(8,128)(2,1)S(1)} %collective-permute-done.2.refs_5_), channel_id=1, source_target_pairs={{0,508},{4,8},{8,4},{12,16},{16,12},{20,24},{24,20},{28,32},{32,28... | collective-permute-start | bytes 1966088 | tf_op jit(solution)/shard_map/ppermute | solution.py:23
  23.4 17.1 %collective-permute-start.5 = (bf16[256,1280]{1,0:T(8,128)(2,1)}, bf16[256,1280]{1,0:T(8,128)(2,1)}, u32[]{:S(2)}, u32[]{:S(2)}) collective-permute-start(bf16[256,1280]{1,0:T(8,128)(2,1)} %collective-permute-done.3.refs_6_), channel_id=1, source_target_pairs={{0,508},{4,8},{8,4},{12,16},{16,12},{20,24},{24,20},{28,32},{32,28... | collective-permute-start | bytes 1966088 | tf_op jit(solution)/shard_map/ppermute | solution.py:23
  30.0 24.4 %collective-permute-start.1 = (bf16[512,1280]{1,0:T(8,128)(2,1)S(1)}, bf16[512,1280]{1,0:T(8,128)(2,1)S(1)}, u32[]{:S(2)}, u32[]{:S(2)}) collective-permute-start(bf16[512,1280]{1,0:T(8,128)(2,1)S(1)} %collective-permute-done.refs_7_), channel_id=1, source_target_pairs={{0,508},{4,8},{8,4},{12,16},{16,12},{20,24},{24,20},{28,32},{32,28... | collective-permute-start | bytes 3932168 | tf_op jit(solution)/shard_map/ppermute | solution.py:23
  43.5 12.4 %collective-permute-start.6 = (bf16[1280,512]{1,0:T(8,128)(2,1)S(1)}, bf16[1280,512]{1,0:T(8,128)(2,1)S(1)}, u32[]{:S(2)}, u32[]{:S(2)}) collective-permute-start(bf16[1280,512]{1,0:T(8,128)(2,1)S(1)} %get-tuple-element.18), channel_id=1, source_target_pairs={{0,4},{4,0},{8,12},{12,8},{16,20},{20,16},{24,28},{28,24},{32,36},... | collective-permute-start | bytes 3932168 | tf_op jit(solution)/shard_map/ppermute | solution.py:23
  57.0 47.5 %copy-start.2 = (bf16[1024,512]{1,0:T(8,128)(2,1)S(1)}, bf16[1024,512]{1,0:T(8,128)(2,1)}, u32[]{:S(2)}) copy-start(bf16[1024,512]{1,0:T(8,128)(2,1)} %coeffs.1) | copy-start | bytes 3145732
